TPU v7x, 32 devices: a whole 2x2x4 slice. The times are simulated.
32 devices in a mesh: fsdp: 2 (over y), ctx: 16 (over z, x, core).
Axes of the slice: x: 2, y: 2, z: 4, core: 2. Of those that a mesh axis runs over, the one named last changes fastest.
Arguments:
- tokens: bfloat16 [3, 2, 2048, 768], P(None, 'fsdp', 'ctx'), may hold values from -6 to 6
- cotangent: bfloat16 [3, 2, 2048, 768], P(None, 'fsdp', 'ctx'), may hold values from -6 to 6
- segment_ids: int32 [3, 2, 2048], P(None, 'fsdp', 'ctx'), may hold values from 0 to 15, never falling along the last dimension, each value on 1 to 1024 neighbouring positions
- q_weight: bfloat16 [192, 768], P('fsdp'), may hold values from -0.4375 to 0.4375
- key_weight: bfloat16 [192, 768], P('fsdp'), may hold values from -0.4375 to 0.4375
- value_weight: bfloat16 [192, 768], P('fsdp'), may hold values from -0.4375 to 0.4375
- q_bias: bfloat16 [768], P('fsdp'), may hold values from -4 to 4
- value_bias: bfloat16 [768], P('fsdp'), may hold values from -1.5 to 1.5
- out_weight: bfloat16 [768, 768], P('fsdp'), may hold values from -1.25 to 1.25
- out_bias: bfloat16 [768], P('fsdp'), may hold values from -1.5 to 1.5
- norm1_gain: bfloat16 [768], P('fsdp'), may hold values from 0.5 to 1.5
- norm1_bias: bfloat16 [768], P('fsdp'), may hold values from -1.5 to 1.5
- inter_weight: bfloat16 [192, 3072], P('fsdp'), may hold values from -0.4375 to 0.4375
- inter_bias: bfloat16 [3072], P('fsdp'), may hold values from -1.5 to 1.5
- ffo_weight: bfloat16 [768, 768], P('fsdp'), may hold values from -0.21875 to 0.21875
- ffo_bias: bfloat16 [768], P('fsdp'), may hold values from -1.5 to 1.5
- norm2_gain: bfloat16 [768], P('fsdp'), may hold values from 0.5 to 1.5
- norm2_bias: bfloat16 [768], P('fsdp'), may hold values from -1.5 to 1.5
Outputs:
- out: bfloat16 [3, 2, 2048, 768], P(None, 'fsdp', 'ctx')
- tokens_grad: bfloat16 [3, 2, 2048, 768], P(None, 'fsdp', 'ctx')
- q_weight_grad: float32 [192, 768], P('fsdp')
- key_weight_grad: float32 [192, 768], P('fsdp')
- value_weight_grad: float32 [192, 768], P('fsdp')
- q_bias_grad: float32 [768], P('fsdp')
- value_bias_grad: float32 [768], P('fsdp')
- out_weight_grad: float32 [768, 768], P('fsdp')
- out_bias_grad: float32 [768], P('fsdp')
- norm1_gain_grad: float32 [768], P('fsdp')
- norm1_bias_grad: float32 [768], P('fsdp')
- inter_weight_grad: float32 [192, 3072], P('fsdp')
- inter_bias_grad: float32 [3072], P('fsdp')
- ffo_weight_grad: float32 [768, 768], P('fsdp')
- ffo_bias_grad: float32 [768], P('fsdp')
- norm2_gain_grad: float32 [768], P('fsdp')
- norm2_bias_grad: float32 [768], P('fsdp')
Inputs may be any that keep to these rules, and one draw needn't show every extreme that they name: `segment_ids`: within each sequence the segment numbers never fall; each of the 16 numbers is used, every document has 1 to 1024 tokens, and one has exactly 1024.
All inputs are finite; a program needn't handle non-finite values.
Results may differ from a plain program's by a relative error of at most 0.024.
Values may be sent and summed in bfloat16 or wider, within the bound.
A program may use at most 192 MiB of HBM per device.

v0:
```python
import math

import jax
import jax.numpy as jnp
from jax import lax
from jax.sharding import PartitionSpec as P

HEADS = 12
HEAD = 64
GROUPS = 4


NORM_EPS = 1e-12
MASKED = -1000000000.0


def group_proj(inputs, weight, groups):
    row_count = inputs.shape[0]
    width_in = inputs.shape[1] // groups
    width_out = weight.shape[1] // groups
    shaped = inputs.reshape(row_count, groups, width_in)
    kernel = weight.reshape(width_in, groups, width_out)
    result = jnp.einsum("rgi,igo->rgo", shaped, kernel, preferred_element_type=jnp.float32)
    return result.reshape(row_count, groups * width_out)


def group_back(gradient, weight, groups):
    row_count = gradient.shape[0]
    width_in = weight.shape[0]
    width_out = weight.shape[1] // groups
    shaped = gradient.reshape(row_count, groups, width_out)
    kernel = weight.reshape(width_in, groups, width_out)
    result = jnp.einsum("rgo,igo->rgi", shaped, kernel, preferred_element_type=jnp.float32)
    return result.reshape(row_count, groups * width_in)


def group_grad(inputs, gradient, groups):
    row_count = inputs.shape[0]
    width_in = inputs.shape[1] // groups
    width_out = gradient.shape[1] // groups
    result = jnp.einsum(
        "rgi,rgo->igo",
        inputs.reshape(row_count, groups, width_in),
        gradient.reshape(row_count, groups, width_out),
        preferred_element_type=jnp.float32,
    )
    return result.reshape(width_in, groups * width_out)


def column_sum(gradient):
    return jnp.sum(gradient.astype(jnp.float32), axis=0)


def layer_norm(residual, norm_gain, norm_shift):
    average = jnp.mean(residual, axis=-1, keepdims=True)
    centred = residual - average
    inverse_root = lax.rsqrt(jnp.mean(centred * centred, axis=-1, keepdims=True) + NORM_EPS)
    return centred * inverse_root * norm_gain + norm_shift


def gelu_exact(values):
    return 0.5 * values * (1.0 + lax.erf(values * math.sqrt(0.5)))


def split_heads(tensor):
    return tensor.reshape(tensor.shape[0], tensor.shape[1], HEADS, HEAD)


def score_block(query_block, key_block, query_anchor, query_segs, key_segs):
    scores = jnp.einsum(
        "sqhd,skhd->shqk", query_block, key_block, preferred_element_type=jnp.float32
    ) * HEAD ** (-0.5)
    anchor_rows = jnp.swapaxes(query_anchor.astype(jnp.float32), 1, 2)[..., None]
    same_doc = query_segs[:, None, :, None] == key_segs[:, None, None, :]
    return jnp.exp(jnp.where(same_doc, scores - anchor_rows, MASKED))


def fold_blocks(step_rule, running, sources, seg_piece):
    piece_len = seg_piece.shape[1]
    block_len = math.gcd(piece_len, 512)
    block_count = piece_len // block_len

    def to_blocks(tensor):
        shaped = tensor.reshape((tensor.shape[0], block_count, block_len) + tensor.shape[2:])
        return jnp.moveaxis(shaped, 1, 0)

    def scan_step(carried, block_in):
        return (step_rule(carried, block_in[0], block_in[1]), None)

    result, ignored = lax.scan(
        scan_step, running, (tuple((to_blocks(tensor) for tensor in sources)), to_blocks(seg_piece))
    )
    return result


def local(
    tokens,
    cotangent,
    segment_ids,
    q_weight,
    key_weight,
    value_weight,
    q_bias,
    value_bias,
    out_weight,
    out_bias,
    norm1_gain,
    norm1_bias,
    inter_weight,
    inter_bias,
    ffo_weight,
    ffo_bias,
    norm2_gain,
    norm2_bias,
):
    micro_count, seq_count, tok_count, model_width = tokens.shape
    row_count = seq_count * tok_count
    score_scale = HEAD ** (-0.5)
    fsdp_count = lax.axis_size("fsdp")
    shard_list = (
        q_weight,
        key_weight,
        value_weight,
        q_bias,
        value_bias,
        out_weight,
        out_bias,
        norm1_gain,
        norm1_bias,
        inter_weight,
        inter_bias,
        ffo_weight,
        ffo_bias,
        norm2_gain,
        norm2_bias,
    )

    def fetch_each():
        return (
            lax.all_gather(q_weight, "fsdp", axis=0, tiled=True),
            lax.all_gather(key_weight, "fsdp", axis=0, tiled=True),
            lax.all_gather(value_weight, "fsdp", axis=0, tiled=True),
            lax.all_gather(q_bias, "fsdp", axis=0, tiled=True),
            lax.all_gather(value_bias, "fsdp", axis=0, tiled=True),
            lax.all_gather(out_weight, "fsdp", axis=0, tiled=True),
            lax.all_gather(out_bias, "fsdp", axis=0, tiled=True),
            lax.all_gather(norm1_gain, "fsdp", axis=0, tiled=True),
            lax.all_gather(norm1_bias, "fsdp", axis=0, tiled=True),
            lax.all_gather(inter_weight, "fsdp", axis=0, tiled=True),
            lax.all_gather(inter_bias, "fsdp", axis=0, tiled=True),
            lax.all_gather(ffo_weight, "fsdp", axis=0, tiled=True),
            lax.all_gather(ffo_bias, "fsdp", axis=0, tiled=True),
            lax.all_gather(norm2_gain, "fsdp", axis=0, tiled=True),
            lax.all_gather(norm2_bias, "fsdp", axis=0, tiled=True),
        )

    grad_sums = [
        jnp.zeros((w_shard.shape[0] * fsdp_count,) + w_shard.shape[1:], jnp.float32)
        for w_shard in shard_list
    ]
    out_blocks = []
    grad_blocks = []
    for micro_index in range(micro_count):
        params = fetch_each()
        (
            w_query,
            w_key,
            w_value,
            b_query,
            b_value,
            w_out,
            b_out,
            gain_one,
            shift_one,
            w_inter,
            b_inter,
            w_second,
            b_second,
            gain_two,
            shift_two,
        ) = params
        token_seq = tokens[micro_index]
        token_rows = token_seq.reshape(row_count, model_width)
        doc_ids = segment_ids[micro_index]
        queries = (group_proj(token_rows, w_query, GROUPS) + b_query.astype(jnp.float32)).astype(
            jnp.bfloat16
        )
        key_rows = group_proj(token_rows, w_key, GROUPS).astype(jnp.bfloat16)
        value_rows = (group_proj(token_rows, w_value, GROUPS) + b_value.astype(jnp.float32)).astype(
            jnp.bfloat16
        )
        query_seq = queries.reshape(seq_count, tok_count, model_width)
        key_seq = key_rows.reshape(seq_count, tok_count, model_width)
        value_seq = value_rows.reshape(seq_count, tok_count, model_width)
        query_heads = split_heads(query_seq)
        key_heads = split_heads(key_seq)
        value_heads = split_heads(value_seq)
        anchors = (
            jnp.sum(query_heads.astype(jnp.float32) * key_heads.astype(jnp.float32), axis=-1)
            * score_scale
        ).astype(jnp.bfloat16)

        def source_heads(sources):
            return (split_heads(sources[0]), split_heads(sources[1]))

        def forward_step(running, sources, seg_block):
            weighted, totals = running
            key_block, value_block = source_heads(sources)
            exp_weights = score_block(query_heads, key_block, anchors, doc_ids, seg_block)
            totals = totals + jnp.sum(exp_weights, axis=-1)
            weighted = weighted + jnp.einsum(
                "shqk,skhd->sqhd",
                exp_weights.astype(jnp.bfloat16),
                value_block,
                preferred_element_type=jnp.float32,
            )
            return (weighted, totals)

        start_forward = (
            jnp.zeros((seq_count, tok_count, HEADS, HEAD), jnp.float32),
            jnp.zeros((seq_count, HEADS, tok_count), jnp.float32),
        )
        pieces = (
            lax.all_gather(key_seq, "ctx", axis=1, tiled=True),
            lax.all_gather(value_seq, "ctx", axis=1, tiled=True),
            lax.all_gather(doc_ids, "ctx", axis=1, tiled=True),
        )
        weighted, totals = fold_blocks(forward_step, start_forward, pieces[:-1], pieces[-1])
        total_rows = jnp.swapaxes(totals, 1, 2)[..., None]
        context = weighted / total_rows
        context_low = context.reshape(row_count, model_width).astype(jnp.bfloat16)
        attn_out = group_proj(context_low, w_out, 1) + b_out.astype(jnp.float32)
        normed_one, norm_one_back = jax.vjp(
            layer_norm,
            attn_out + token_rows.astype(jnp.float32),
            gain_one.astype(jnp.float32),
            shift_one.astype(jnp.float32),
        )
        normed_low = normed_one.astype(jnp.bfloat16)
        hidden_pre = group_proj(normed_low, w_inter, GROUPS) + b_inter.astype(jnp.float32)
        hidden, gelu_back = jax.vjp(gelu_exact, hidden_pre)
        hidden_low = hidden.astype(jnp.bfloat16)
        branch = group_proj(hidden_low, w_second, GROUPS) + b_second.astype(jnp.float32)
        normed_two, norm_two_back = jax.vjp(
            layer_norm,
            branch + normed_one,
            gain_two.astype(jnp.float32),
            shift_two.astype(jnp.float32),
        )
        out_blocks.append(
            normed_two.astype(jnp.bfloat16).reshape(seq_count, tok_count, model_width)
        )
        params = fetch_each()
        (
            w_query,
            w_key,
            w_value,
            b_query,
            b_value,
            w_out,
            b_out,
            gain_one,
            shift_one,
            w_inter,
            b_inter,
            w_second,
            b_second,
            gain_two,
            shift_two,
        ) = params
        upstream = cotangent[micro_index].reshape(row_count, model_width).astype(jnp.float32)
        d_resid_two, d_gain_two, d_shift_two = norm_two_back(upstream)
        d_branch = d_resid_two.astype(jnp.bfloat16)
        (d_pre,) = gelu_back(group_back(d_branch, w_second, GROUPS))
        d_pre_low = d_pre.astype(jnp.bfloat16)
        d_normed = group_back(d_pre_low, w_inter, GROUPS) + d_resid_two
        d_resid_one, d_gain_one, d_shift_one = norm_one_back(d_normed)
        d_attn = d_resid_one.astype(jnp.bfloat16)
        d_context = group_back(d_attn, w_out, 1).reshape(seq_count, tok_count, HEADS, HEAD)
        d_numer = (d_context / total_rows).astype(jnp.bfloat16)
        row_delta = (jnp.sum(d_context * context, axis=-1) / total_rows[..., 0]).astype(
            jnp.bfloat16
        )
        delta_cols = jnp.swapaxes(row_delta.astype(jnp.float32), 1, 2)[..., None]
        d_numer_seq = d_numer.reshape(seq_count, tok_count, model_width)

        def query_grad_step(running, sources, seg_block):
            key_block, value_block = source_heads(sources)
            exp_weights = score_block(query_heads, key_block, anchors, doc_ids, seg_block)
            d_probs = jnp.einsum(
                "sqhd,skhd->shqk", d_numer, value_block, preferred_element_type=jnp.float32
            )
            d_scores = (exp_weights * (d_probs - delta_cols)).astype(jnp.bfloat16)
            return (
                running
                + jnp.einsum(
                    "shqk,skhd->sqhd", d_scores, key_block, preferred_element_type=jnp.float32
                )
                * score_scale
            )

        start_query = jnp.zeros((seq_count, tok_count, HEADS, HEAD), jnp.float32)
        query_pieces = (
            lax.all_gather(key_seq, "ctx", axis=1, tiled=True),
            lax.all_gather(value_seq, "ctx", axis=1, tiled=True),
            lax.all_gather(doc_ids, "ctx", axis=1, tiled=True),
        )
        d_query = fold_blocks(query_grad_step, start_query, query_pieces[:-1], query_pieces[-1])

        def key_grad_step(running, sources, seg_block):
            d_keys, d_values = running
            query_part, numer_part, anchor_part, delta_part = sources
            query_block = split_heads(query_part)
            numer_block = split_heads(numer_part)
            exp_weights = score_block(query_block, key_heads, anchor_part, seg_block, doc_ids)
            d_probs = jnp.einsum(
                "sqhd,skhd->shqk", numer_block, value_heads, preferred_element_type=jnp.float32
            )
            delta_block = jnp.swapaxes(delta_part.astype(jnp.float32), 1, 2)[..., None]
            d_scores = (exp_weights * (d_probs - delta_block)).astype(jnp.bfloat16)
            d_values = d_values + jnp.einsum(
                "shqk,sqhd->skhd",
                exp_weights.astype(jnp.bfloat16),
                numer_block,
                preferred_element_type=jnp.float32,
            )
            d_keys = (
                d_keys
                + jnp.einsum(
                    "shqk,sqhd->skhd", d_scores, query_block, preferred_element_type=jnp.float32
                )
                * score_scale
            )
            return (d_keys, d_values)

        key_pieces = (
            lax.all_gather(query_seq, "ctx", axis=1, tiled=True),
            lax.all_gather(d_numer_seq, "ctx", axis=1, tiled=True),
            lax.all_gather(anchors, "ctx", axis=1, tiled=True),
            lax.all_gather(row_delta, "ctx", axis=1, tiled=True),
            lax.all_gather(doc_ids, "ctx", axis=1, tiled=True),
        )
        d_keys, d_values = fold_blocks(
            key_grad_step, (start_query, start_query), key_pieces[:-1], key_pieces[-1]
        )
        d_query_low = d_query.reshape(row_count, model_width).astype(jnp.bfloat16)
        d_key_low = d_keys.reshape(row_count, model_width).astype(jnp.bfloat16)
        d_value_low = d_values.reshape(row_count, model_width).astype(jnp.bfloat16)
        d_tokens = (
            group_back(d_query_low, w_query, GROUPS)
            + group_back(d_key_low, w_key, GROUPS)
            + group_back(d_value_low, w_value, GROUPS)
            + d_resid_one
        )
        grad_blocks.append(d_tokens.astype(jnp.bfloat16).reshape(seq_count, tok_count, model_width))
        new_terms = (
            group_grad(token_rows, d_query_low, GROUPS),
            group_grad(token_rows, d_key_low, GROUPS),
            group_grad(token_rows, d_value_low, GROUPS),
            column_sum(d_query_low),
            column_sum(d_value_low),
            group_grad(context_low, d_attn, 1),
            column_sum(d_attn),
            d_gain_one,
            d_shift_one,
            group_grad(normed_low, d_pre_low, GROUPS),
            column_sum(d_pre_low),
            group_grad(hidden_low, d_branch, GROUPS),
            column_sum(d_branch),
            d_gain_two,
            d_shift_two,
        )
        grad_sums = [running_sum + new_term for running_sum, new_term in zip(grad_sums, new_terms)]
    reduced = (
        lax.psum_scatter(
            grad_sums[0].astype(jnp.bfloat16), "fsdp", scatter_dimension=0, tiled=True
        ).astype(jnp.float32),
        lax.psum_scatter(
            grad_sums[1].astype(jnp.bfloat16), "fsdp", scatter_dimension=0, tiled=True
        ).astype(jnp.float32),
        lax.psum_scatter(
            grad_sums[2].astype(jnp.bfloat16), "fsdp", scatter_dimension=0, tiled=True
        ).astype(jnp.float32),
        lax.psum_scatter(
            grad_sums[3].astype(jnp.bfloat16), "fsdp", scatter_dimension=0, tiled=True
        ).astype(jnp.float32),
        lax.psum_scatter(
            grad_sums[4].astype(jnp.bfloat16), "fsdp", scatter_dimension=0, tiled=True
        ).astype(jnp.float32),
        lax.psum_scatter(
            grad_sums[5].astype(jnp.bfloat16), "fsdp", scatter_dimension=0, tiled=True
        ).astype(jnp.float32),
        lax.psum_scatter(
            grad_sums[6].astype(jnp.bfloat16), "fsdp", scatter_dimension=0, tiled=True
        ).astype(jnp.float32),
        lax.psum_scatter(
            grad_sums[7].astype(jnp.bfloat16), "fsdp", scatter_dimension=0, tiled=True
        ).astype(jnp.float32),
        lax.psum_scatter(
            grad_sums[8].astype(jnp.bfloat16), "fsdp", scatter_dimension=0, tiled=True
        ).astype(jnp.float32),
        lax.psum_scatter(
            grad_sums[9].astype(jnp.bfloat16), "fsdp", scatter_dimension=0, tiled=True
        ).astype(jnp.float32),
        lax.psum_scatter(
            grad_sums[10].astype(jnp.bfloat16), "fsdp", scatter_dimension=0, tiled=True
        ).astype(jnp.float32),
        lax.psum_scatter(
            grad_sums[11].astype(jnp.bfloat16), "fsdp", scatter_dimension=0, tiled=True
        ).astype(jnp.float32),
        lax.psum_scatter(
            grad_sums[12].astype(jnp.bfloat16), "fsdp", scatter_dimension=0, tiled=True
        ).astype(jnp.float32),
        lax.psum_scatter(
            grad_sums[13].astype(jnp.bfloat16), "fsdp", scatter_dimension=0, tiled=True
        ).astype(jnp.float32),
        lax.psum_scatter(
            grad_sums[14].astype(jnp.bfloat16), "fsdp", scatter_dimension=0, tiled=True
        ).astype(jnp.float32),
    )
    summed = (
        lax.psum(reduced[0].astype(jnp.bfloat16), "ctx").astype(jnp.float32),
        lax.psum(reduced[1].astype(jnp.bfloat16), "ctx").astype(jnp.float32),
        lax.psum(reduced[2].astype(jnp.bfloat16), "ctx").astype(jnp.float32),
        lax.psum(reduced[3].astype(jnp.bfloat16), "ctx").astype(jnp.float32),
        lax.psum(reduced[4].astype(jnp.bfloat16), "ctx").astype(jnp.float32),
        lax.psum(reduced[5].astype(jnp.bfloat16), "ctx").astype(jnp.float32),
        lax.psum(reduced[6].astype(jnp.bfloat16), "ctx").astype(jnp.float32),
        lax.psum(reduced[7].astype(jnp.bfloat16), "ctx").astype(jnp.float32),
        lax.psum(reduced[8].astype(jnp.bfloat16), "ctx").astype(jnp.float32),
        lax.psum(reduced[9].astype(jnp.bfloat16), "ctx").astype(jnp.float32),
        lax.psum(reduced[10].astype(jnp.bfloat16), "ctx").astype(jnp.float32),
        lax.psum(reduced[11].astype(jnp.bfloat16), "ctx").astype(jnp.float32),
        lax.psum(reduced[12].astype(jnp.bfloat16), "ctx").astype(jnp.float32),
        lax.psum(reduced[13].astype(jnp.bfloat16), "ctx").astype(jnp.float32),
        lax.psum(reduced[14].astype(jnp.bfloat16), "ctx").astype(jnp.float32),
    )
    return (
        jnp.stack(out_blocks),
        jnp.stack(grad_blocks),
        summed[0],
        summed[1],
        summed[2],
        summed[3],
        summed[4],
        summed[5],
        summed[6],
        summed[7],
        summed[8],
        summed[9],
        summed[10],
        summed[11],
        summed[12],
        summed[13],
        summed[14],
    )


def solution(mesh):
    placed = (
        P(None, "fsdp", "ctx", None),
        P(None, "fsdp", "ctx", None),
        P(None, "fsdp", "ctx"),
        P("fsdp", None),
        P("fsdp", None),
        P("fsdp", None),
        P("fsdp"),
        P("fsdp"),
        P("fsdp", None),
        P("fsdp"),
        P("fsdp"),
        P("fsdp"),
        P("fsdp", None),
        P("fsdp"),
        P("fsdp", None),
        P("fsdp"),
        P("fsdp"),
        P("fsdp"),
    )
    return jax.shard_map(
        local,
        mesh=mesh,
        in_specs=placed,
        out_specs=(
            P(None, "fsdp", "ctx", None),
            P(None, "fsdp", "ctx", None),
            P("fsdp", None),
            P("fsdp", None),
            P("fsdp", None),
            P("fsdp"),
            P("fsdp"),
            P("fsdp", None),
            P("fsdp"),
            P("fsdp"),
            P("fsdp"),
            P("fsdp", None),
            P("fsdp"),
            P("fsdp", None),
            P("fsdp"),
            P("fsdp"),
            P("fsdp"),
        ),
        check_vma=False,
    )
```

profile of v0, /device:TPU:0, one launch (start us, length us, event | category | flops | bytes accessed | tf_op | source)
XLA Modules:
  0.0 1148.6 jit_solution(10292609332974605698)
XLA Ops:
  9.1 7.7 all_gather.72
  17.7 4.3 all-gather.6
  24.9 9.6 all_gather.76
  40.9 5.8 all_gather.78
  48.5 4.3 all-gather.8
  54.1 4.3 all-gather.10
  59.2 4.3 all-gather.9
  64.2 4.3 all-gather.12
  69.8 4.3 all-gather.13
  75.5 21.6 %all-gather.1 = s32[1,1,2048]{2,1,0:T(1,128)S(1)} all-gather(s32[1,1,128]{2,1,0:T(1,128)S(1)} %get-tuple-element.2414), channel_id=3, replica_groups=mesh['fsdp'=2,'ctx'=16] {'ctx'}, dimensions={2}, use_global_device_ids=true | all-gather | bytes 8704 | tf_op jit(solution)/shard_map/all_gather | solution.py:226
  97.1 4.3 all-gather.7
  104.1 17.0 %all-gather.2 = s32[1,1,2048]{2,1,0:T(1,128)S(1)} all-gather(s32[1,1,128]{2,1,0:T(1,128)S(1)} %get-tuple-element.2339), channel_id=4, replica_groups=mesh['fsdp'=2,'ctx'=16] {'ctx'}, dimensions={2}, use_global_device_ids=true | all-gather | bytes 8704 | tf_op jit(solution)/shard_map/all_gather | solution.py:226
  121.1 20.1 %all-gather = s32[1,1,2048]{2,1,0:T(1,128)} all-gather(s32[1,1,128]{2,1,0:T(1,128)S(1)} %get-tuple-element.2489), channel_id=2, replica_groups=mesh['fsdp'=2,'ctx'=16] {'ctx'}, dimensions={2}, use_global_device_ids=true | all-gather | bytes 8704 | tf_op jit(solution)/shard_map/all_gather | solution.py:226
  141.9 4.8 all-gather.11
  154.4 4.7 copy.330
  159.1 4.7 copy.331
  163.8 29.0 %while.112 = (s32[]{:T(128)}, f32[1,128,12,64]{1,3,2,0:T(8,128)S(1)}, f32[1,12,128]{2,1,0:T(8,128)S(1)}, bf16[4,1,512,768]{2,3,1,0:T(8,128)(2,1)}, s32[1,1,128]{...) while((s32[]{:T(128)}, ...), condition=%wide.region_11.12_spmd.clone, body=%wide.region_9.11_spmd.clone.sunk | while | flops 207883264 | bytes 12242568 | solution.py:90
  193.0 4.9 copy.338
  197.9 28.8 %all-gather.47.cloned.1.call-done = bf16[1,2048,768]{2,1,0:T(8,128)(2,1)} async-done(((bf16[1,128,768]{2,1,0:T(8,128)(2,1)}), bf16[1,2048,768]{2,1,0:T(8,128)(2,1)}) %all-gather.47.cloned.1.call-update) | async-done | bytes 3145744 | tf_op jit(solution)/shard_map/all_gather | solution.py:224
  226.7 4.7 copy.339
  231.5 28.9 %while.113 = (s32[]{:T(128)}, f32[1,128,12,64]{1,3,2,0:T(8,128)S(1)}, f32[1,12,128]{2,1,0:T(8,128)S(1)}, bf16[4,1,512,768]{2,3,1,0:T(8,128)(2,1)}, s32[1,1,128]{...) while((s32[]{:T(128)}, ...), condition=%wide.region_19.20_spmd.clone, body=%wide.region_17.19_spmd.clone.sunk | while | flops 207883264 | bytes 12242568 | solution.py:90
  260.4 13.3 %all-gather.31.cloned.1.call-done = bf16[1,2048,768]{2,1,0:T(8,128)(2,1)} async-done(((bf16[1,128,768]{2,1,0:T(8,128)(2,1)}), bf16[1,2048,768]{2,1,0:T(8,128)(2,1)}) %all-gather.31.cloned.1.call-update) | async-done | bytes 3145744 | tf_op jit(solution)/shard_map/all_gather | solution.py:225
  276.9 43.1 %all-gather.33.cloned.1.call-done = bf16[1,2048,768]{2,1,0:T(8,128)(2,1)} async-done(((bf16[1,128,768]{2,1,0:T(8,128)(2,1)}), bf16[1,2048,768]{2,1,0:T(8,128)(2,1)}) %all-gather.33.cloned.1.call-update) | async-done | bytes 3145744 | tf_op jit(solution)/shard_map/all_gather | solution.py:224
  320.0 4.7 copy.322
  324.7 41.5 %while.111 = (s32[]{:T(128)}, f32[1,128,12,64]{1,3,2,0:T(8,128)}, f32[1,12,128]{2,1,0:T(8,128)S(1)}, bf16[4,1,512,768]{2,3,1,0:T(8,128)(2,1)S(1)}, s32[1,1,128]{...) while((s32[]{:T(128)}, f32[1,128,12,64]{1,3,2,0:T(8,128)}, ...), condition=%wide.region_3.4_spmd.clone, body=%wide.region_1.3_spmd.clone.sunk | while | flops 207883264 | bytes 13354800 | solution.py:90
  341.2 3.9 fusion.536
  351.5 4.2 fusion.536
  362.1 3.9 fusion.536
  468.9 4.3 all-gather.14
  473.8 19.4 %all-gather.5 = bf16[2048,12]{0,1:T(8,128)(2,1)S(1)} all-gather(bf16[128,12]{0,1:T(8,128)(2,1)S(1)} %multiply_convert_fusion.6), channel_id=7, replica_groups=mesh['fsdp'=2,'ctx'=16] {'ctx'}, dimensions={0}, use_global_device_ids=true | all-gather | bytes 52224 | tf_op jit(solution)/shard_map/all_gather | solution.py:339
  493.9 17.7 %all-gather.4 = bf16[2048,12]{0,1:T(8,128)(2,1)S(1)} all-gather(bf16[128,12]{0,1:T(8,128)(2,1)S(1)} %multiply_convert_fusion.7), channel_id=6, replica_groups=mesh['fsdp'=2,'ctx'=16] {'ctx'}, dimensions={0}, use_global_device_ids=true | all-gather | bytes 52224 | tf_op jit(solution)/shard_map/all_gather | solution.py:339
  512.3 19.0 %all-gather.3 = bf16[2048,12]{0,1:T(8,128)(2,1)S(1)} all-gather(bf16[128,12]{0,1:T(8,128)(2,1)S(1)} %multiply_convert_fusion.8), channel_id=5, replica_groups=mesh['fsdp'=2,'ctx'=16] {'ctx'}, dimensions={0}, use_global_device_ids=true | all-gather | bytes 52224 | tf_op jit(solution)/shard_map/all_gather | solution.py:339
  537.0 39.8 %while.118 = (s32[]{:T(128)}, f32[1,128,12,64]{1,3,2,0:T(8,128)}, bf16[4,1,512,768]{2,3,1,0:T(8,128)(2,1)}, s32[1,1,128]{2,1,0:T(1,128)}, s32[4,1,512]{2,1,0:T(1...) while((s32[]{:T(128)}, f32[1,128,12,64]{1,3,2,0:T(8,128)}, ...), condition=%wide.region_48.49_spmd.clone, body=%wide.region_47.48_spmd.clone.sunk | while | flops 307070464 | bytes 17082112 | solution.py:90
  553.1 4.0 fusion.587
  563.1 3.8 fusion.587
  584.2 39.9 %while.116 = (s32[]{:T(128)}, f32[1,128,12,64]{1,3,2,0:T(8,128)}, bf16[4,1,512,768]{2,3,1,0:T(8,128)(2,1)}, s32[1,1,128]{2,1,0:T(1,128)}, s32[4,1,512]{2,1,0:T(1...) while((s32[]{:T(128)}, f32[1,128,12,64]{1,3,2,0:T(8,128)}, ...), condition=%wide.region_39.40_spmd.clone, body=%wide.region_38.39_spmd.clone.sunk | while | flops 307070464 | bytes 17082112 | solution.py:90
  600.0 4.2 fusion.570
  610.3 3.8 fusion.570
  624.1 39.1 %while.114 = (s32[]{:T(128)}, f32[1,128,12,64]{1,3,2,0:T(8,128)}, bf16[4,1,512,768]{2,3,1,0:T(8,128)(2,1)}, s32[1,1,128]{2,1,0:T(1,128)}, s32[4,1,512]{2,1,0:T(1...) while((s32[]{:T(128)}, f32[1,128,12,64]{1,3,2,0:T(8,128)}, ...), condition=%wide.region_30.31_spmd.clone, body=%wide.region_29.30_spmd.clone.sunk | while | flops 307070464 | bytes 17082112 | solution.py:90
  639.8 3.8 fusion.553
  649.6 3.8 fusion.553
  659.4 3.8 fusion.553
  667.9 17.9 %all_gather.203 = bf16[1,2048,12]{1,2,0:T(8,128)(2,1)S(1)} all-gather(bf16[1,128,12]{1,2,0:T(8,128)(2,1)S(1)} %fusion.308), channel_id=1, replica_groups=mesh['fsdp'=2,'ctx'=16] {'ctx'}, dimensions={1}, use_global_device_ids=true | all-gather | bytes 52224 | tf_op jit(solution)/shard_map/all_gather | solution.py:340
  687.4 19.1 %all_gather.199 = bf16[1,2048,12]{1,2,0:T(8,128)(2,1)S(1)} all-gather(bf16[1,128,12]{1,2,0:T(8,128)(2,1)S(1)} %fusion.309), channel_id=1, replica_groups=mesh['fsdp'=2,'ctx'=16] {'ctx'}, dimensions={1}, use_global_device_ids=true | all-gather | bytes 52224 | tf_op jit(solution)/shard_map/all_gather | solution.py:340
  708.1 18.0 %all_gather.195 = bf16[1,2048,12]{1,2,0:T(8,128)(2,1)S(1)} all-gather(bf16[1,128,12]{1,2,0:T(8,128)(2,1)S(1)} %fusion.310), channel_id=1, replica_groups=mesh['fsdp'=2,'ctx'=16] {'ctx'}, dimensions={1}, use_global_device_ids=true | all-gather | bytes 52224 | tf_op jit(solution)/shard_map/all_gather | solution.py:340
  766.5 75.4 %while.119 = (s32[]{:T(128)}, f32[1,128,12,64]{1,3,2,0:T(8,128)}, f32[1,128,12,64]{1,3,2,0:T(8,128)}, bf16[4,1,512,768]{3,2,0,1:T(8,128)(2,1)}, s32[4,1,512]{2,1...) while((s32[]{:T(128)}, f32[1,128,12,64]{1,3,2,0:T(8,128)}, ...), condition=%wide.region_50.51_spmd.clone, body=%wide.region_49.50_spmd.clone.sunk | while | flops 411086848 | bytes 21191324 | solution.py:90
  777.5 4.5 fusion.596
  796.1 4.7 fusion.596
  815.1 4.7 fusion.596
  834.0 4.7 fusion.596
  841.9 75.4 %while.117 = (s32[]{:T(128)}, f32[1,128,12,64]{1,3,2,0:T(8,128)}, f32[1,128,12,64]{1,3,2,0:T(8,128)}, bf16[4,1,512,768]{3,2,0,1:T(8,128)(2,1)}, s32[4,1,512]{2,1...) while((s32[]{:T(128)}, f32[1,128,12,64]{1,3,2,0:T(8,128)}, ...), condition=%wide.region_41.42_spmd.clone, body=%wide.region_40.41_spmd.clone.sunk | while | flops 411086848 | bytes 21191324 | solution.py:90
  852.9 4.5 fusion.579
  871.6 4.7 fusion.579
  890.5 4.7 fusion.579
  909.4 4.7 fusion.579
  917.2 75.6 %while.115 = (s32[]{:T(128)}, f32[1,128,12,64]{1,3,2,0:T(8,128)}, f32[1,128,12,64]{1,3,2,0:T(8,128)}, bf16[4,1,512,768]{3,2,0,1:T(8,128)(2,1)}, s32[4,1,512]{2,1...) while((s32[]{:T(128)}, f32[1,128,12,64]{1,3,2,0:T(8,128)}, ...), condition=%wide.region_32.33_spmd.clone, body=%wide.region_31.32_spmd.clone.sunk | while | flops 411086848 | bytes 21191324 | solution.py:90
  928.5 4.5 fusion.562
  947.1 4.7 fusion.562
  966.1 4.7 fusion.562
  985.0 4.7 fusion.562
  1012.3 15.0 %reduce-scatter.13.cloned.1.call-done = bf16[96,768]{1,0:T(8,128)(2,1)} async-done(((bf16[192,768]{1,0:T(8,128)(2,1)}), bf16[96,768]{1,0:T(8,128)(2,1)}) %reduce-scatter.13.cloned.1.call-update) | async-done | bytes 147472 | tf_op jit(solution)/shard_map/reduce_scatter | solution.py:381
  1030.1 8.4 all-reduce.11
  1050.3 59.9 %all-reduce.9 = (bf16[384]{0:T(512)(128)(2,1)}, bf16[384]{0:T(512)(128)(2,1)}, bf16[384]{0:T(512)(128)(2,1)}, bf16[384]{0:T(512)(128)(2,1)}, bf16[384]{0:T(512)(...) all-reduce(bf16[384]{0:T(512)(128)(2,1)} %dynamic-slice.1, ...), channel_id=1, replica_groups=mesh['fsdp'=2,'ctx'=16] {'ctx'}, use_global_device_ids=true, to_apply=%region_61.62 | all-reduce | flops 4608 | bytes 18432 | tf_op jit(solution)/shard_map/psum | solution.py:425
  1125.9 6.0 all-reduce.14.cloned.1.call-done
  (1357 shorter events, 601.3 us)
Async XLA Ops:
  7.2 144.8 %all-gather.39.cloned.1.call-start = ((), (), s32[]{:S(2)}) async-start(), calls=%async_computation.10 | async-start | bytes 1769472 | tf_op jit(solution)/shard_map/all_gather | solution.py:151
  7.9 146.5 %all-gather.41.cloned.1.call-start = ((), (), s32[]{:S(2)}) async-start(), calls=%async_computation.11 | async-start | bytes 3342336 | tf_op jit(solution)/shard_map/all_gather | solution.py:225
  22.8 25.1 %copy-start.4 = (bf16[1,1,128,768]{2,3,1,0:T(8,128)(2,1)}, bf16[1,1,128,768]{2,3,1,0:T(8,128)(2,1)S(1)}, u32[]{:S(2)}) copy-start(bf16[1,1,128,768]{2,3,1,0:T(8,128)(2,1)S(1)} %copy.327) | copy-start | bytes 589828
  24.8 134.3 %all-gather.43.cloned.1.call-start = ((), (), s32[]{:S(2)}) async-start(), calls=%async_computation.12 | async-start | bytes 3342336 | tf_op jit(solution)/shard_map/all_gather | solution.py:224
  34.9 67.1 %copy-start.28 = (bf16[4,192,128]{2,1,0:T(8,128)(2,1)}, bf16[4,192,128]{2,1,0:T(8,128)(2,1)S(1)}, u32[]{:S(2)}) copy-start(bf16[4,192,128]{2,1,0:T(8,128)(2,1)S(1)} %convolution_convert_fusion.1) | copy-start | bytes 589828
  35.8 157.2 %all-gather.45.cloned.1.call-start = ((), (), s32[]{:S(2)}) async-start(), calls=%async_computation.13 | async-start | bytes 3342336 | tf_op jit(solution)/shard_map/all_gather | solution.py:225
  36.3 190.4 %all-gather.47.cloned.1.call-start = ((), (), s32[]{:S(2)}) async-start(), calls=%async_computation.14 | async-start | bytes 3342336 | tf_op jit(solution)/shard_map/all_gather | solution.py:224
  36.6 65.4 %copy-start.27 = (bf16[4,192,128]{2,1,0:T(8,128)(2,1)}, bf16[4,192,128]{2,1,0:T(8,128)(2,1)S(1)}, u32[]{:S(2)}) copy-start(bf16[4,192,128]{2,1,0:T(8,128)(2,1)S(1)} %convolution_convert_fusion) | copy-start | bytes 589828
  37.5 236.2 %all-gather.31.cloned.1.call-start = ((), (), s32[]{:S(2)}) async-start(), calls=%async_computation.6 | async-start | bytes 3342336 | tf_op jit(solution)/shard_map/all_gather | solution.py:225
  38.1 281.9 %all-gather.33.cloned.1.call-start = ((), (), s32[]{:S(2)}) async-start(), calls=%async_computation.7 | async-start | bytes 3342336 | tf_op jit(solution)/shard_map/all_gather | solution.py:224
  38.4 63.6 %copy-start.26 = (bf16[4,192,128]{2,1,0:T(8,128)(2,1)}, bf16[4,192,128]{2,1,0:T(8,128)(2,1)S(1)}, u32[]{:S(2)}) copy-start(bf16[4,192,128]{2,1,0:T(8,128)(2,1)S(1)} %convolution_convert_fusion.2) | copy-start | bytes 589828
  39.2 332.4 %all-gather.35.cloned.1.call-start = ((), (), s32[]{:S(2)}) async-start(), calls=%async_computation.8 | async-start | bytes 1769472 | tf_op jit(solution)/shard_map/all_gather | solution.py:145
  40.0 24.2 %copy-start.305 = (bf16[384]{0:T(512)(128)(2,1)S(1)}, bf16[384]{0:T(512)(128)(2,1)}, u32[]{:S(2)}) copy-start(bf16[384]{0:T(512)(128)(2,1)} %param.51) | copy-start | bytes 2308
  40.1 29.8 %copy-start.306 = (bf16[384]{0:T(512)(128)(2,1)S(1)}, bf16[384]{0:T(512)(128)(2,1)}, u32[]{:S(2)}) copy-start(bf16[384]{0:T(512)(128)(2,1)} %param.52) | copy-start | bytes 2308
  40.1 35.4 %copy-start.300 = (s32[3,1,128]{2,1,0:T(1,128)S(1)}, s32[3,1,128]{2,1,0:T(1,128)}, u32[]{:S(2)}) copy-start(s32[3,1,128]{2,1,0:T(1,128)} %param.38) | copy-start | bytes 4612
  40.1 57.0 %copy-start.307 = (bf16[384]{0:T(512)(128)(2,1)S(1)}, bf16[384]{0:T(512)(128)(2,1)}, u32[]{:S(2)}) copy-start(bf16[384]{0:T(512)(128)(2,1)} %param.42) | copy-start | bytes 2308
  40.1 341.3 %all-gather.37.cloned.1.call-start = ((), (), s32[]{:S(2)}) async-start(), calls=%async_computation.9 | async-start | bytes 1769472 | tf_op jit(solution)/shard_map/all_gather | solution.py:149
  40.8 723.5 %reduce-scatter.19.cloned.1.call-start = ((), (), s32[]{:S(2)}) async-start(), calls=%async_computation.26 | async-start | bytes 1769472
  46.9 57.2 %copy-start.12 = (bf16[192,768]{0,1:T(8,128)(2,1)}, bf16[192,768]{0,1:T(8,128)(2,1)S(1)}, u32[]{:S(2)}) copy-start(bf16[192,768]{0,1:T(8,128)(2,1)S(1)} %copy.320) | copy-start | bytes 884740
  47.9 93.9 %copy-start.299 = (bf16[1536]{0:T(1024)(128)(2,1)S(1)}, bf16[1536]{0:T(1024)(128)(2,1)}, u32[]{:S(2)}) copy-start(bf16[1536]{0:T(1024)(128)(2,1)} %param.49) | copy-start | bytes 9220
  47.9 99.5 %copy-start.15 = (bf16[3,1,128,768]{3,2,1,0:T(8,128)(2,1)S(1)}, bf16[3,1,128,768]{3,2,1,0:T(8,128)(2,1)}, u32[]{:S(2)}) copy-start(bf16[3,1,128,768]{3,2,1,0:T(8,128)(2,1)} %param.37) | copy-start | bytes 1769476
  48.2 100.0 %copy-start.93 = (f32[4,192,128]{2,1,0:T(8,128)}, f32[4,192,128]{2,1,0:T(8,128)S(1)}, u32[]{:S(2)}) copy-start(f32[4,192,128]{2,1,0:T(8,128)S(1)} %fusion.340) | copy-start | bytes 1179652
  48.4 101.7 %copy-start.91 = (f32[4,192,128]{2,1,0:T(8,128)}, f32[4,192,128]{2,1,0:T(8,128)S(1)}, u32[]{:S(2)}) copy-start(f32[4,192,128]{2,1,0:T(8,128)S(1)} %fusion.344) | copy-start | bytes 1179652
  75.5 74.7 %copy-start.183 = (s32[1,1,128]{2,1,0:T(1,128)}, s32[1,1,128]{2,1,0:T(1,128)S(1)}, u32[]{:S(2)}) copy-start(s32[1,1,128]{2,1,0:T(1,128)S(1)} %get-tuple-element.2489) | copy-start | bytes 1540
  104.1 50.3 %copy-start.208 = (f32[128,12]{0,1:T(8,128)}, f32[128,12]{0,1:T(8,128)S(1)}, u32[]{:S(2)}) copy-start(f32[128,12]{0,1:T(8,128)S(1)} %get-tuple-element.1481) | copy-start | bytes 18436
  104.1 50.3 %copy-start.210 = (f32[128,12]{0,1:T(8,128)}, f32[128,12]{0,1:T(8,128)S(1)}, u32[]{:S(2)}) copy-start(f32[128,12]{0,1:T(8,128)S(1)} %get-tuple-element.1557) | copy-start | bytes 18436
  104.1 50.3 %copy-start.212 = (f32[128,12]{0,1:T(8,128)}, f32[128,12]{0,1:T(8,128)S(1)}, u32[]{:S(2)}) copy-start(f32[128,12]{0,1:T(8,128)S(1)} %get-tuple-element.1559) | copy-start | bytes 18436
  377.8 73.0 %copy-start.39 = (f32[128,768]{1,0:T(8,128)}, f32[128,768]{1,0:T(8,128)S(1)}, u32[]{:S(2)}) copy-start(f32[128,768]{1,0:T(8,128)S(1)} %get-tuple-element.1573) | copy-start | bytes 1179652
  389.5 56.3 %copy-start.38 = (f32[4,128,192]{1,2,0:T(8,128)}, f32[4,128,192]{1,2,0:T(8,128)S(1)}, u32[]{:S(2)}) copy-start(f32[4,128,192]{1,2,0:T(8,128)S(1)} %fusion.342) | copy-start | bytes 1179652
  457.7 308.7 %all-gather.57.cloned.1.call-start = ((), (), s32[]{:S(2)}) async-start(), calls=%async_computation.19 | async-start | bytes 3342336 | tf_op jit(solution)/shard_map/all_gather | solution.py:337
  461.0 305.5 %all-gather.59.cloned.1.call-start = ((), (), s32[]{:S(2)}) async-start(), calls=%async_computation.20 | async-start | bytes 3342336 | tf_op jit(solution)/shard_map/all_gather | solution.py:338
  463.5 378.3 %all-gather.53.cloned.1.call-start = ((), (), s32[]{:S(2)}) async-start(), calls=%async_computation.17 | async-start | bytes 3342336 | tf_op jit(solution)/shard_map/all_gather | solution.py:337
  464.3 377.5 %all-gather.55.cloned.1.call-start = ((), (), s32[]{:S(2)}) async-start(), calls=%async_computation.18 | async-start | bytes 3342336 | tf_op jit(solution)/shard_map/all_gather | solution.py:338
  465.3 66.6 %copy-start.318 = (u32[32]{0:T(128)S(1)}, u32[32]{0:T(128)}, u32[]{:S(2)}) copy-start(u32[32]{0:T(128)} %constant.180) | copy-start | bytes 388
  465.3 69.1 %copy-start.86 = (f32[4,192,128]{2,1,0:T(8,128)S(1)}, f32[4,192,128]{2,1,0:T(8,128)}, u32[]{:S(2)}) copy-start(f32[4,192,128]{2,1,0:T(8,128)} %copy-done.85) | copy-start | bytes 1179652
  465.3 69.1 %copy-start.88 = (f32[4,192,128]{2,1,0:T(8,128)S(1)}, f32[4,192,128]{2,1,0:T(8,128)}, u32[]{:S(2)}) copy-start(f32[4,192,128]{2,1,0:T(8,128)} %copy-done.87) | copy-start | bytes 1179652
  465.3 69.1 %copy-start.90 = (f32[4,192,128]{2,1,0:T(8,128)S(1)}, f32[4,192,128]{2,1,0:T(8,128)}, u32[]{:S(2)}) copy-start(f32[4,192,128]{2,1,0:T(8,128)} %copy-done.89) | copy-start | bytes 1179652
  467.9 67.6 %copy-start.178 = (f32[128,768]{1,0:T(8,128)S(1)}, f32[128,768]{1,0:T(8,128)}, u32[]{:S(2)}) copy-start(f32[128,768]{1,0:T(8,128)} %get-tuple-element.1577) | copy-start | bytes 1179652
  467.9 67.8 %copy-start.131 = (f32[1,128,12,64]{1,3,2,0:T(8,128)S(1)}, f32[1,128,12,64]{1,3,2,0:T(8,128)}, u32[]{:S(2)}) copy-start(f32[1,128,12,64]{1,3,2,0:T(8,128)} %copy-done.130) | copy-start | bytes 1179652
  467.9 449.3 %all-gather.49.cloned.1.call-start = ((), (), s32[]{:S(2)}) async-start(), calls=%async_computation.15 | async-start | bytes 3342336 | tf_op jit(solution)/shard_map/all_gather | solution.py:337
  468.5 448.8 %all-gather.51.cloned.1.call-start = ((), (), s32[]{:S(2)}) async-start(), calls=%async_computation.16 | async-start | bytes 3342336 | tf_op jit(solution)/shard_map/all_gather | solution.py:338
  624.1 387.2 %reduce-scatter.9.cloned.1.call-start = ((), (), s32[]{:S(2)}) async-start(), calls=%async_computation.21 | async-start | bytes 442368 | tf_op jit(solution)/shard_map/reduce_scatter | solution.py:375
  663.3 24.2 %copy-start.146 = (f32[1,12,128]{2,1,0:T(8,128)S(1)}, f32[1,12,128]{2,1,0:T(8,128)}, u32[]{:S(2)}) copy-start(f32[1,12,128]{2,1,0:T(8,128)} %copy-done.144) | copy-start | bytes 18436
  663.3 24.2 %copy-start.205 = (f32[128,12]{0,1:T(8,128)S(1)}, f32[128,12]{0,1:T(8,128)}, u32[]{:S(2)}) copy-start(f32[128,12]{0,1:T(8,128)} %copy-done.204) | copy-start | bytes 18436
  663.3 43.9 %copy-start.63 = (f32[4,128,192]{1,2,0:T(8,128)S(1)}, f32[4,128,192]{1,2,0:T(8,128)}, u32[]{:S(2)}) copy-start(f32[4,128,192]{1,2,0:T(8,128)} %fusion.175) | copy-start | bytes 1179652
  663.3 44.8 %copy-start.207 = (f32[128,12]{0,1:T(8,128)S(1)}, f32[128,12]{0,1:T(8,128)}, u32[]{:S(2)}) copy-start(f32[128,12]{0,1:T(8,128)} %copy-done.206) | copy-start | bytes 18436
  663.3 63.5 %copy-start.74 = (f32[4,128,192]{1,2,0:T(8,128)S(1)}, f32[4,128,192]{1,2,0:T(8,128)}, u32[]{:S(2)}) copy-start(f32[4,128,192]{1,2,0:T(8,128)} %fusion.177) | copy-start | bytes 1179652
  666.5 94.1 %copy-start.105 = (f32[1,1,128,768]{3,2,1,0:T(8,128)}, f32[1,1,128,768]{3,2,1,0:T(8,128)S(1)}, u32[]{:S(2)}) copy-start(f32[1,1,128,768]{3,2,1,0:T(8,128)S(1)} %copy.334) | copy-start | bytes 1179652
  667.8 93.8 %copy-start.103 = (f32[1,1,128,768]{3,2,1,0:T(8,128)}, f32[1,1,128,768]{3,2,1,0:T(8,128)S(1)}, u32[]{:S(2)}) copy-start(f32[1,1,128,768]{3,2,1,0:T(8,128)S(1)} %copy.326) | copy-start | bytes 1179652
  667.9 62.7 %copy-start.177 = (f32[1,128,12,64]{1,3,2,0:T(8,128)S(1)}, f32[1,128,12,64]{1,3,2,0:T(8,128)}, u32[]{:S(2)}) copy-start(f32[1,128,12,64]{1,3,2,0:T(8,128)} %get-tuple-element.497) | copy-start | bytes 1179652
  707.2 25.2 %copy-start.6 = (bf16[1,1,128,768]{2,3,1,0:T(8,128)(2,1)S(1)}, bf16[1,1,128,768]{2,3,1,0:T(8,128)(2,1)}, u32[]{:S(2)}) copy-start(bf16[1,1,128,768]{2,3,1,0:T(8,128)(2,1)} %copy-done.4) | copy-start | bytes 589828
  743.3 268.0 %reduce-scatter.15.cloned.1.call-start = ((), (), s32[]{:S(2)}) async-start(), calls=%async_computation.24 | async-start | bytes 1769472 | tf_op jit(solution)/shard_map/reduce_scatter | solution.py:402
  749.4 261.9 %reduce-scatter.17.cloned.1.call-start = ((), (), s32[]{:S(2)}) async-start(), calls=%async_computation.25 | async-start | bytes 1769472 | tf_op jit(solution)/shard_map/reduce_scatter | solution.py:408
  762.0 250.3 %reduce-scatter.11.cloned.1.call-start = ((), (), s32[]{:S(2)}) async-start(), calls=%async_computation.22 | async-start | bytes 442368 | tf_op jit(solution)/shard_map/reduce_scatter | solution.py:378
  1002.6 24.7 %reduce-scatter.13.cloned.1.call-start = ((), (), s32[]{:S(2)}) async-start(), calls=%async_computation.23 | async-start | bytes 442368 | tf_op jit(solution)/shard_map/reduce_scatter | solution.py:381
  1007.3 124.7 %all-reduce.14.cloned.1.call-start = ((), (), s32[]{:S(2)}) async-start(), calls=%async_computation.27 | async-start | bytes 4423680 | tf_op jit(solution)/shard_map/psum | solution.py:427
  1009.9 111.9 %copy-start.17 = (bf16[3,1,128,768]{3,2,1,0:T(8,128)(2,1)S(1)}, bf16[3,1,128,768]{3,2,1,0:T(8,128)(2,1)}, u32[]{:S(2)}) copy-start(bf16[3,1,128,768]{3,2,1,0:T(8,128)(2,1)} %param.37) | copy-start | bytes 1769476
  1009.9 111.9 %copy-start.25 = (f32[128,768]{1,0:T(8,128)S(1)}, f32[128,768]{1,0:T(8,128)}, u32[]{:S(2)}) copy-start(f32[128,768]{1,0:T(8,128)} %copy-done.22) | copy-start | bytes 1179652
  1010.0 111.9 %copy-start.31 = (bf16[3,1,128,768]{3,2,1,0:T(8,128)(2,1)S(1)}, bf16[3,1,128,768]{3,2,1,0:T(8,128)(2,1)}, u32[]{:S(2)}) copy-start(bf16[3,1,128,768]{3,2,1,0:T(8,128)(2,1)} %param.36) | copy-start | bytes 1769476
  1010.0 111.9 %copy-start.107 = (f32[1,1,128,768]{3,2,1,0:T(8,128)S(1)}, f32[1,1,128,768]{3,2,1,0:T(8,128)}, u32[]{:S(2)}) copy-start(f32[1,1,128,768]{3,2,1,0:T(8,128)} %copy.342) | copy-start | bytes 1179652
  1011.3 112.1 %copy-start.21 = (f32[128,768]{1,0:T(8,128)S(1)}, f32[128,768]{1,0:T(8,128)}, u32[]{:S(2)}) copy-start(f32[128,768]{1,0:T(8,128)} %copy-done.18) | copy-start | bytes 1179652
  1011.3 112.1 %copy-start.106 = (f32[1,1,128,768]{3,2,1,0:T(8,128)S(1)}, f32[1,1,128,768]{3,2,1,0:T(8,128)}, u32[]{:S(2)}) copy-start(f32[1,1,128,768]{3,2,1,0:T(8,128)} %copy-done.105) | copy-start | bytes 1179652
  1027.3 97.2 %copy-start.41 = (f32[128,768]{1,0:T(8,128)S(1)}, f32[128,768]{1,0:T(8,128)}, u32[]{:S(2)}) copy-start(f32[128,768]{1,0:T(8,128)} %copy-done.39) | copy-start | bytes 1179652
  1027.3 97.2 %copy-start.104 = (f32[1,1,128,768]{3,2,1,0:T(8,128)S(1)}, f32[1,1,128,768]{3,2,1,0:T(8,128)}, u32[]{:S(2)}) copy-start(f32[1,1,128,768]{3,2,1,0:T(8,128)} %copy-done.103) | copy-start | bytes 1179652
  (331 other events, 1331.3 us)
Sparse Core Ops, SparseCore 0:
  9.6 28.6 all-gather.38
  41.1 45.2 all-gather.40
  89.3 44.0 all-gather.42
  136.1 44.2 all-gather.44
  182.5 44.2 all-gather.46
  229.4 44.2 all-gather.30
  276.0 43.9 all-gather.32
  321.6 21.5 all-gather.34
  344.7 22.7 all-gather.36
  457.8 20.6 reduce-scatter.18
  481.1 45.3 all-gather.56
  529.5 44.1 all-gather.58
  576.3 43.9 all-gather.52
  622.7 43.9 all-gather.54
  669.7 44.4 all-gather.48
  716.6 44.1 all-gather.50
  763.5 10.9 reduce-scatter.8
  777.3 21.7 reduce-scatter.14
  801.9 21.7 reduce-scatter.16
  1002.7 9.5 reduce-scatter.10
  1015.2 12.0 reduce-scatter.12
  1032.2 99.6 all-reduce.13
where the time goes:
time: 1160 us; the launch traced here: 1150 us
  blocking collectives  301 us (26%)
  matrix products  291 us (25%)
  local copies, waits for them, and re-layouts  271 us (23%)
  other arithmetic  151 us (13%)
  waiting for transfers between devices  112 us (10%)
  between operations  19.8 us (2%)
    dynamic_slice x96, local copies, waits for them, and re-layouts, fold_blocks(): lax.scan(scan_step, running, (tuple((to_blocks(tensor) for tensor in sour...  138 us
    all_gather x3, waiting for transfers between devices, local(): lax.all_gather(key_seq, 'ctx', axis=1, tiled=True)  71.9 us
    dot_general x36, matrix products, score_block(): jnp.einsum('sqhd,skhd->shqk', query_block, key_block, preferred_element_t...  63.8 us
    unnamed x636, local copies, waits for them, and re-layouts  62.3 us
    psum x1, blocking collectives, local(): lax.psum(reduced[3].astype(jnp.bfloat16), 'ctx').astype(jnp.float32)  59.9 us
    all_gather x3, blocking collectives, local(): lax.all_gather(doc_ids, 'ctx', axis=1, tiled=True)  58.8 us
    all_gather x3, blocking collectives, local(): lax.all_gather(anchors, 'ctx', axis=1, tiled=True)  56.1 us
    dot_general x12, matrix products, key_grad_step(): jnp.einsum('shqk,sqhd->skhd', d_scores, query_block, preferred_element_ty...  55.6 us
  transfers between devices with their start and end apart: 22, of which 6 were waited for; matrix products, arithmetic and copies ran while one was open for 53% of the time, Pallas kernels for 0%

commit v1 on v0

v1 whole, which is shorter than its diff:
```python
import math

import jax
import jax.numpy as jnp
from jax import lax
from jax.experimental import pallas as pl
from jax.experimental.pallas import tpu as pltpu
from jax.sharding import PartitionSpec as P

MESH = pl.DeviceIdType.MESH
MICRO = 3


def place(n, g, m):
    return g * (n // 4) + m + (g % 2)


def owners(n):
    return [place(n, g, m) for m in range(MICRO) for g in range(4)]


def unit_of(c, n):
    g = c // (n // 4)
    m = c - g * (n // 4) - lax.rem(g, 2)
    return g, m, (m >= 0) & (m < MICRO)


def greet(f, c, n):
    bar = pltpu.get_barrier_semaphore()
    for d in range(1, n):
        pl.semaphore_signal(bar, inc=1, device_id=(f, lax.rem(c + d, n)), device_id_type=MESH)
    pl.semaphore_wait(bar, n - 1)


def to_units(n, src, dst, ssem, rsem, lsem):
    f, c = lax.axis_index("fsdp"), lax.axis_index("ctx")
    own = owners(n)
    mine = unit_of(c, n)[2]
    def copy(u):
        return pltpu.make_async_remote_copy(src_ref=src.at[u], dst_ref=dst.at[c], send_sem=ssem.at[u], recv_sem=rsem.at[c],
                                            device_id=(f, own[u]), device_id_type=MESH)
    for u in range(12):
        @pl.when(c != own[u])
        def _():
            copy(u).start()
        @pl.when(c == own[u])
        def _():
            pltpu.make_async_copy(src.at[u], dst.at[c], lsem).start()
    @pl.when(mine)
    def _():
        pltpu.make_async_copy(src.at[0], dst.at[c], lsem).wait()
        for s in range(n):
            @pl.when(c != s)
            def _():
                pltpu.make_async_remote_copy(src_ref=src.at[0], dst_ref=dst.at[s], send_sem=ssem.at[0], recv_sem=rsem.at[s], device_id=(f, s), device_id_type=MESH).wait_recv()
    for u in range(12):
        @pl.when(c != own[u])
        def _():
            copy(u).wait_send()


def to_rows(n, src, dst, ssem, rsem, lsem):
    f, c = lax.axis_index("fsdp"), lax.axis_index("ctx")
    own = owners(n)
    g, m, mine = unit_of(c, n)
    u = m * 4 + g
    def copy(d):
        t = lax.rem(c + d, n)
        return pltpu.make_async_remote_copy(src_ref=src.at[t], dst_ref=dst.at[u], send_sem=ssem.at[d], recv_sem=rsem.at[u],
                                            device_id=(f, t), device_id_type=MESH)
    @pl.when(mine)
    def _():
        for d in range(1, n):
            copy(d).start()
        pltpu.make_async_copy(src.at[c], dst.at[u], lsem).start()
    for k in range(12):
        @pl.when(c != own[k])
        def _():
            pltpu.make_async_remote_copy(src_ref=src.at[0], dst_ref=dst.at[k], send_sem=ssem.at[0], recv_sem=rsem.at[k], device_id=(f, own[k]), device_id_type=MESH).wait_recv()
    @pl.when(mine)
    def _():
        pltpu.make_async_copy(src.at[c], dst.at[u], lsem).wait()
        for d in range(1, n):
            copy(d).wait_send()

BF, F32 = jnp.bfloat16, jnp.float32
HEAD, GW = 64, 192
CH = 208
XA = 240
BIG = 1e9
NN = (((1,), (0,)), ((), ()))
NT = (((1,), (1,)), ((), ()))
TN = (((0,), (0,)), ((), ()))

def mm(a, b, dims=NN):
    return lax.dot_general(a, b, dims, preferred_element_type=F32)

def iota(shape, axis):
    return lax.broadcasted_iota(jnp.int32, shape, axis)

def select_group(n, wf_ref, bf_ref, w_ref, b_ref):
    g = lax.axis_index("ctx") // (n // 4)
    for k in range(4):
        @pl.when(g == k)
        def _():
            w_ref[...] = wf_ref[:, :, k * GW:k * GW + GW]
            b_ref[...] = bf_ref[:, k * GW:k * GW + GW]


def build_weights(w_ref, b_ref, wa_ref, wat_ref):
    for s in range(3):
        for h in range(3):
            w = w_ref[s, :, h * 64:h * 64 + 64].astype(F32)
            top = jnp.concatenate([w * (0.125 if s == 0 else 1.0), jnp.zeros((GW, 64), F32)], axis=1)
            r, c = iota((48, 128), 0), iota((48, 128), 1)
            same = (c - 64 == r)
            lanes = (c >= 64) & (c < 96) & (r < 32)
            one = (r == 32)
            zero = jnp.zeros((48, 128), F32)
            if s == 0:
                bias = jnp.concatenate([b_ref[0:1, h * 64:h * 64 + 64].astype(F32) * 0.125, jnp.zeros((1, 64), F32)], axis=1)
                low = jnp.where(lanes & same, 1.0, zero) + jnp.where(one, bias, zero)
            elif s == 1:
                low = jnp.where(lanes & ~same, -BIG, zero) + jnp.where(one & (c == 96), 1.0, zero)
            else:
                bias = jnp.concatenate([b_ref[1:2, h * 64:h * 64 + 64].astype(F32), jnp.zeros((1, 64), F32)], axis=1)
                low = jnp.where(one, bias, zero) + jnp.where(one & (c == 64), 1.0, zero)
            full = jnp.concatenate([top, low], axis=0)
            wa_ref[s, :, h * 128:h * 128 + 128] = full.astype(BF)
            wat_ref[s, h * 128:h * 128 + 128, :] = jnp.transpose(full).astype(BF)

def bounds(xt_ref, nb, seg_ref, lohi_ref):
    for b in range(nb):
        seg_ref[b:b + 1, :] = xt_ref[b, GW:GW + 16, :].astype(F32)[0:1, :]
    seg = seg_ref[0:nb, :]
    full = jnp.concatenate([seg, jnp.full((128 - nb, 128), 1e6, F32)], axis=0)
    t = jnp.transpose(full)
    minrow, maxrow = t[0:1, :], t[127:128, :]
    mincol, maxcol = seg[:, 0:1], seg[:, 127:128]
    lo = jnp.sum((maxcol < minrow).astype(F32), axis=0, keepdims=True)
    hi = (nb - 1) - jnp.sum((mincol > maxrow).astype(F32), axis=0, keepdims=True)
    r = iota((8, 128), 0)
    lohi_ref[...] = jnp.where(r == 0, lo, hi).astype(jnp.int32)

def prep(xt_ref, nb, wa_ref, wat_ref, qt_ref, ka_ref, vt_ref, xn_ref=None, qn_ref=None, kt_ref=None, va_ref=None):
    def block(i, carry):
        x = jnp.concatenate([xt_ref[2 * i], xt_ref[2 * i + 1]], axis=1)
        seg = x[GW:GW + 16].astype(F32)[0:1].astype(jnp.int32)
        r = iota((48, 256), 0)
        aug = jnp.where((r == seg) & (r < 32) | (r == 32), 1.0, 0.0).astype(BF)
        xa = jnp.concatenate([x[0:GW], aug], axis=0)
        xn = jnp.transpose(xa)
        qt = mm(wat_ref[0], xa).astype(BF)
        kt = mm(wat_ref[1], xa).astype(BF)
        kn = mm(xn, wa_ref[1]).astype(BF)
        if vt_ref is not None:
            vt = mm(wat_ref[2], xa).astype(BF)
        if qn_ref is not None:
            qn = mm(xn, wa_ref[0]).astype(BF)
            vn = mm(xn, wa_ref[2]).astype(BF)
        for h in range(3):
            o = h * 128
            qt_ref[h, i] = qt[o:o + 128]
            anchor = jnp.sum(qt[o:o + 64].astype(F32) * kt[o:o + 64].astype(F32), axis=0, keepdims=True)
            qt_ref[h, i, 96:112] = jnp.where(iota((16, 256), 0) == 0, -anchor, 0.0).astype(BF)
            ka_ref[h, i] = kn[:, o:o + 128]
            if vt_ref is not None:
                vt_ref[h, i] = vt[o:o + 80]
            if qn_ref is not None:
                qn_ref[h, i] = qn[:, o:o + 128]
                kt_ref[h, i] = kt[o:o + 64]
                va_ref[h, i] = vn[:, o:o + 128]
        return carry
    lax.fori_loop(0, nb // 2, block, 0)

def fwd_kernel(nb, xt_ref, wf_ref, bf_ref, ctx_ref, cf_ref, l_ref, lohi_ref, w_ref, b_ref, wa_ref, wat_ref, qt_ref, ka_ref, vt_ref, seg_ref, acc_ref, lohi_v, lohi_s, sem):
    @pl.when(unit_of(lax.axis_index("ctx"), nb)[2])
    def _():
        select_group(nb, wf_ref, bf_ref, w_ref, b_ref)
        sb = nb // 2
        bounds(xt_ref, nb, seg_ref, lohi_v)
        cp = pltpu.make_async_copy(lohi_v, lohi_s, sem)
        cp.start()
        lohi_ref[...] = lohi_v[...]
        build_weights(w_ref, b_ref, wa_ref, wat_ref)
        prep(xt_ref, nb, wa_ref, wat_ref, qt_ref, ka_ref, vt_ref)
        cp.wait()
        def qblock(i, carry):
            lo, hi = lohi_s[0, 2 * i] // 2, lohi_s[1, 2 * i + 1] // 2
            acc_ref[...] = jnp.zeros_like(acc_ref)
            def kblock(j, c):
                s = [mm(ka_ref[h, j], qt_ref[h, i]) for h in range(3)]
                e = [jnp.exp(x).astype(BF) for x in s]
                o = [mm(vt_ref[h, j], e[h]) for h in range(3)]
                for h in range(3):
                    acc_ref[h] += o[h]
                return c
            lax.fori_loop(lo, hi + 1, kblock, 0)
            for h in range(3):
                a = acc_ref[h]
                l = a[64:65]
                c = a[0:64] / l
                cf_ref[i, h * 64:h * 64 + 64, :] = c
                l_ref[i, h:h + 1, :] = l
                cb = c.astype(BF)
                ctx_ref[2 * i, h * 64:h * 64 + 64, :] = cb[:, 0:128]
                ctx_ref[2 * i + 1, h * 64:h * 64 + 64, :] = cb[:, 128:256]
            return carry
        lax.fori_loop(0, sb, qblock, 0)


def attn_fwd(xt, w, b):
    nb = xt.shape[0]
    sb = nb // 2
    return pl.pallas_call(
        lambda *a: fwd_kernel(nb, *a),
        out_shape=(jax.ShapeDtypeStruct((nb, GW, 128), BF), jax.ShapeDtypeStruct((sb, GW, 256), F32),
                   jax.ShapeDtypeStruct((sb, 8, 256), F32), jax.ShapeDtypeStruct((8, 128), jnp.int32)),
        scratch_shapes=[pltpu.VMEM((3, GW, GW), BF), pltpu.VMEM((8, GW), BF), pltpu.VMEM((3, XA, 384), BF), pltpu.VMEM((3, 384, XA), BF), pltpu.VMEM((3, sb, 128, 256), BF), pltpu.VMEM((3, sb, 256, 128), BF),
                        pltpu.VMEM((3, sb, 80, 256), BF), pltpu.VMEM((max(nb, 8), 128), F32), pltpu.VMEM((3, 80, 256), F32),
                        pltpu.VMEM((8, 128), jnp.int32), pltpu.SMEM((8, 128), jnp.int32), pltpu.SemaphoreType.DMA],
        compiler_params=pltpu.CompilerParams(vmem_limit_bytes=60 * 2**20))(xt, w, b)

def bwd_kernel(nb, xt_ref, wf_ref, bf_ref, dc_ref, cf_ref, l_ref, lohi_s, dx_ref, gw_ref, gb_ref,
               w_ref, b_ref, wa_ref, wat_ref, qt_ref, ka_ref, qn_ref, kt_ref, va_ref, dnt_ref, dnn_ref, dq_ref, dqt_ref, dkv_ref, gacc_ref, gbacc_ref):
    gw_ref[...] = jnp.zeros_like(gw_ref)
    gb_ref[...] = jnp.zeros_like(gb_ref)
    @pl.when(unit_of(lax.axis_index("ctx"), nb)[2])
    def _():
        select_group(nb, wf_ref, bf_ref, w_ref, b_ref)
        sb = nb // 2
        build_weights(w_ref, b_ref, wa_ref, wat_ref)
        prep(xt_ref, nb, wa_ref, wat_ref, qt_ref, ka_ref, None, True, qn_ref, kt_ref, va_ref)
        dkv_ref[...] = jnp.zeros_like(dkv_ref)
        def pre(i, carry):
            d = jnp.concatenate([dc_ref[2 * i], dc_ref[2 * i + 1]], axis=1).astype(F32)
            for h in range(3):
                dh = d[h * 64:h * 64 + 64]
                inv = 1.0 / l_ref[i, h:h + 1, :]
                delta = jnp.sum(dh * cf_ref[i, h * 64:h * 64 + 64, :], axis=0, keepdims=True) * inv
                dn = dh * inv
                full = jnp.concatenate([dn, jnp.where(iota((64, 256), 0) == 0, -delta, 0.0)], axis=0)
                dnt_ref[h, i] = full.astype(BF)
                dnn_ref[h, i] = jnp.transpose(full).astype(BF)
            return carry
        lax.fori_loop(0, sb, pre, 0)
        def qblock(i, carry):
            lo, hi = lohi_s[0, 2 * i] // 2, lohi_s[1, 2 * i + 1] // 2
            dq_ref[...] = jnp.zeros_like(dq_ref)
            def kblock(j, c):
                s = [mm(ka_ref[h, j], qt_ref[h, i]) for h in range(3)]
                dp = [mm(va_ref[h, j], dnt_ref[h, i]) for h in range(3)]
                e = [jnp.exp(x) for x in s]
                eb = [x.astype(BF) for x in e]
                ds = [(e[h] * dp[h]).astype(BF) for h in range(3)]
                q = [mm(kt_ref[h, j], ds[h]) for h in range(3)]
                k = [mm(ds[h], qn_ref[h, i])[:, 0:64] for h in range(3)]
                v = [mm(eb[h], dnn_ref[h, i])[:, 0:64] for h in range(3)]
                for h in range(3):
                    dq_ref[h] += q[h]
                    dkv_ref[h, j, :, 0:64] += k[h]
                    dkv_ref[h, j, :, 64:128] += v[h]
                return c
            lax.fori_loop(lo, hi + 1, kblock, 0)
            dqt_ref[i] = (dq_ref[...].reshape(GW, 256) * 0.125).astype(BF)
            return carry
        lax.fori_loop(0, sb, qblock, 0)
        def post(i, carry):
            xt = jnp.concatenate([xt_ref[2 * i], xt_ref[2 * i + 1]], axis=1)[0:GW]
            dqt = dqt_ref[i]
            dk = jnp.concatenate([dkv_ref[h, i, :, 0:64] for h in range(3)], axis=1).astype(BF)
            dv = jnp.concatenate([dkv_ref[h, i, :, 64:128] for h in range(3)], axis=1).astype(BF)
            dx = mm(w_ref[0], dqt) + mm(w_ref[1], dk, NT) + mm(w_ref[2], dv, NT)
            dxb = dx.astype(BF)
            dx_ref[2 * i] = dxb[:, 0:128]
            dx_ref[2 * i + 1] = dxb[:, 128:256]
            gacc_ref[0] += mm(xt, dqt, NT)
            gacc_ref[1] += mm(xt, dk)
            gacc_ref[2] += mm(xt, dv)
            dqn = jnp.transpose(dqt.astype(F32))
            gbacc_ref[0:1] += jnp.sum(dqn, axis=0, keepdims=True)
            gbacc_ref[1:2] += jnp.sum(dv.astype(F32), axis=0, keepdims=True)
            return carry
        gacc_ref[...] = jnp.zeros_like(gacc_ref)
        gbacc_ref[...] = jnp.zeros_like(gbacc_ref)
        lax.fori_loop(0, sb, post, 0)
        g = lax.axis_index("ctx") // (nb // 4)
        for k in range(4):
            @pl.when(g == k)
            def _():
                gw_ref[:, :, k * GW:k * GW + GW] = gacc_ref[...].astype(BF)
                gb_ref[:, k * GW:k * GW + GW] = gbacc_ref[...]


def attn_bwd(xt, w, b, dc, cf, l, lohi):
    nb = xt.shape[0]
    sb = nb // 2
    return pl.pallas_call(
        lambda *a: bwd_kernel(nb, *a),
        out_shape=(jax.ShapeDtypeStruct((nb, GW, 128), BF), jax.ShapeDtypeStruct((3, GW, 768), BF), jax.ShapeDtypeStruct((8, 768), F32)),
        in_specs=[pl.BlockSpec(memory_space=pltpu.VMEM)] * 6 + [pl.BlockSpec(memory_space=pltpu.SMEM)],
        scratch_shapes=[pltpu.VMEM((3, GW, GW), BF), pltpu.VMEM((8, GW), BF), pltpu.VMEM((3, XA, 384), BF), pltpu.VMEM((3, 384, XA), BF), pltpu.VMEM((3, sb, 128, 256), BF), pltpu.VMEM((3, sb, 256, 128), BF),
                        pltpu.VMEM((3, sb, 256, 128), BF), pltpu.VMEM((3, sb, 64, 256), BF), pltpu.VMEM((3, sb, 256, 128), BF),
                        pltpu.VMEM((3, sb, 128, 256), BF), pltpu.VMEM((3, sb, 256, 128), BF), pltpu.VMEM((3, 64, 256), F32),
                        pltpu.VMEM((sb, GW, 256), BF), pltpu.VMEM((3, sb, 256, 128), F32), pltpu.VMEM((3, GW, GW), F32), pltpu.VMEM((8, GW), F32)],
        compiler_params=pltpu.CompilerParams(vmem_limit_bytes=60 * 2**20))(xt, w, b, dc, cf, l, lohi)


D, FF = 768, 3072
EPS = 1e-12
WIN = (0, 128, 384, 512)
OFF = (0, 64, 0, 64)
RS2 = math.sqrt(0.5)
IPI = 1.0 / math.sqrt(2.0 * math.pi)
CK = 32

def rowmean(x):
    return jnp.sum(x, axis=-1, keepdims=True) * (1.0 / D)

def dense_body(rows, tok, cot, ctxt, wout, wint, wffo, vec, out, d1, dct, ga, gi, gf, gv,
               ctx, attn, n1, n1b, wip, wfp, gp, hid, br, d2, db, dpre, dn, da, st):
    nm = rows // 128
    v = lambda i: vec[i:i + 1, :]
    for j in range(4):
        o = OFF[j]
        wip[j] = jnp.zeros((256, D), BF)
        wip[j, o:o + 192, :] = wint[:, j * D:(j + 1) * D]
        lane = iota((D, 256), 1)
        w = wffo[:, WIN[j]:WIN[j] + 256]
        wfp[j] = jnp.where((lane >= o) & (lane < o + 192), w.astype(F32), 0.0).astype(BF)
    for m in range(nm):
        ctx[m * 128:(m + 1) * 128, :] = jnp.transpose(ctxt[m])
    attn[...] = mm(ctx[...], wout[...])
    def ln1(t, c):
        s = pl.ds(pl.multiple_of(t * CK, CK), CK)
        r = attn[s, :] + v(0) + tok[s, :].astype(F32)
        cen = r - rowmean(r)
        rstd = lax.rsqrt(rowmean(cen * cen) + EPS)
        xh = cen * rstd
        attn[s, :] = xh
        st[s, :] = jnp.broadcast_to(rstd, (CK, 128))
        n = xh * v(1) + v(2)
        n1[s, :] = n
        n1b[s, :] = n.astype(BF)
        br[s, :] = n + v(3)
        return c
    lax.fori_loop(0, rows // CK, ln1, 0)
    for j in range(4):
        for m in range(nm):
            s = slice(m * 128, (m + 1) * 128)
            u = mm(n1b[s, WIN[j]:WIN[j] + 256], wip[j]) + v(8 + j)
            half = 0.5 + 0.5 * lax.erf(u * RS2)
            hid[j, s, :] = (u * half).astype(BF)
            gp[j, s, :] = half + u * (jnp.exp(u * u * -0.5) * IPI)
        br[:, WIN[j]:WIN[j] + 256] += mm(hid[j], wfp[j])
    gv[...] = jnp.zeros_like(gv)
    def ln2(t, c):
        s = pl.ds(pl.multiple_of(t * CK, CK), CK)
        r = br[s, :]
        cen = r - rowmean(r)
        rstd = lax.rsqrt(rowmean(cen * cen) + EPS)
        xh = cen * rstd
        out[s, :] = (xh * v(4) + v(5)).astype(BF)
        ct = cot[s, :].astype(F32)
        u = ct * v(4)
        dd = rstd * (u - rowmean(u) - xh * rowmean(u * xh))
        d2[s, :] = dd
        ddb = dd.astype(BF)
        db[s, :] = ddb
        gv[4:5, :] += jnp.sum(ct * xh, axis=0, keepdims=True)
        gv[5:6, :] += jnp.sum(ct, axis=0, keepdims=True)
        gv[3:4, :] += jnp.sum(ddb.astype(F32), axis=0, keepdims=True)
        return c
    lax.fori_loop(0, rows // CK, ln2, 0)
    dn[...] = d2[...]
    for j in range(4):
        for m in range(nm):
            s = slice(m * 128, (m + 1) * 128)
            dh = mm(db[s, WIN[j]:WIN[j] + 256], wfp[j], NT)
            dp = (dh * gp[j, s, :]).astype(BF)
            dpre[j, s, :] = dp
            gv[8 + j:9 + j, :] += jnp.sum(dp.astype(F32), axis=0, keepdims=True)
        dn[:, WIN[j]:WIN[j] + 256] += mm(dpre[j], wip[j], NT)
    def lnb(t, c):
        s = pl.ds(pl.multiple_of(t * CK, CK), CK)
        g = dn[s, :]
        xh = attn[s, :]
        u = g * v(1)
        dd = st[s, 0:1] * (u - rowmean(u) - xh * rowmean(u * xh))
        d1[s, :] = dd
        ddb = dd.astype(BF)
        da[s, :] = ddb
        gv[1:2, :] += jnp.sum(g * xh, axis=0, keepdims=True)
        gv[2:3, :] += jnp.sum(g, axis=0, keepdims=True)
        gv[0:1, :] += jnp.sum(ddb.astype(F32), axis=0, keepdims=True)
        return c
    lax.fori_loop(0, rows // CK, lnb, 0)
    dc = mm(wout[...], da[...], NT).astype(BF)
    for m in range(nm):
        dct[m] = dc[:, m * 128:(m + 1) * 128]
    ct = jnp.concatenate([ctxt[m] for m in range(nm)], axis=1)
    ga[...] = mm(ct, da[...]).astype(BF)
    nt = jnp.transpose(n1b[...])
    dbt = jnp.transpose(db[...])
    for j in range(4):
        o = WIN[j] + OFF[j]
        gi[:, j * D:(j + 1) * D] = mm(nt[o:o + 192, :], dpre[j]).astype(BF)
        gf[j * 192:(j + 1) * 192, :] = mm(dbt[o:o + 192, :], hid[j]).astype(BF)

def scratch(rows):
    return [pltpu.VMEM((rows, D), BF), pltpu.VMEM((rows, D), F32), pltpu.VMEM((rows, D), F32), pltpu.VMEM((rows, D), BF),
            pltpu.VMEM((4, 256, D), BF), pltpu.VMEM((4, D, 256), BF), pltpu.VMEM((4, rows, D), F32), pltpu.VMEM((4, rows, D), BF),
            pltpu.VMEM((rows, D), F32), pltpu.VMEM((rows, D), F32), pltpu.VMEM((rows, D), BF), pltpu.VMEM((4, rows, D), BF),
            pltpu.VMEM((rows, D), F32), pltpu.VMEM((rows, D), BF), pltpu.VMEM((rows, 128), F32)]

def dense(tok, cot, ctxt, wout, wint, wffo, vec):
    rows = tok.shape[0]
    nm = rows // 128
    S = jax.ShapeDtypeStruct
    return pl.pallas_call(
        lambda *a: dense_body(rows, *a),
        out_shape=(S((rows, D), BF), S((rows, D), F32), S((nm, D, 128), BF), S((D, D), BF), S((192, FF), BF), S((D, D), BF), S((16, D), F32)),
        scratch_shapes=scratch(rows),
        compiler_params=pltpu.CompilerParams(vmem_limit_bytes=60 * 2**20))(tok, cot, ctxt, wout, wint, wffo, vec)


def tokens_kernel(n, tok, seg, xt, buf, ssem, rsem, lsem):
    f, c = lax.axis_index("fsdp"), lax.axis_index("ctx")
    for m in range(MICRO):
        t = jnp.transpose(tok[m])
        sg = jnp.broadcast_to(seg[m:m + 1, :].astype(F32), (16, 128)).astype(BF)
        for g in range(4):
            buf[m * 4 + g, 0:GW, :] = t[g * GW:g * GW + GW]
            buf[m * 4 + g, GW:CH, :] = sg
    greet(f, c, n)
    to_units(n, buf, xt, ssem, rsem, lsem)


def rows_kernel(n, src, dst, ssem, rsem, lsem):
    greet(lax.axis_index("fsdp"), lax.axis_index("ctx"), n)
    to_rows(n, src, dst, ssem, rsem, lsem)


def units_kernel(n, src, dst, ssem, rsem, lsem):
    greet(lax.axis_index("fsdp"), lax.axis_index("ctx"), n)
    to_units(n, src, dst, ssem, rsem, lsem)


def final_kernel(n, src, d1, grad, buf, ssem, rsem, lsem):
    greet(lax.axis_index("fsdp"), lax.axis_index("ctx"), n)
    to_rows(n, src, buf, ssem, rsem, lsem)
    for m in range(MICRO):
        x = jnp.concatenate([buf[m * 4 + g] for g in range(4)], axis=0).astype(F32)
        grad[m] = (jnp.transpose(x) + d1[m]).astype(BF)


DMA = pltpu.SemaphoreType.DMA


def remote(kernel, n, cid, outs, args, scratch=()):
    vm = pl.BlockSpec(memory_space=pltpu.VMEM)
    return pl.pallas_call(
        lambda *a: kernel(n, *a), out_shape=outs, in_specs=[vm] * len(args),
        out_specs=jax.tree.map(lambda _: vm, outs),
        scratch_shapes=list(scratch) + [DMA((n,)), DMA((n,)), DMA],
        compiler_params=pltpu.CompilerParams(collective_id=cid, has_side_effects=True, vmem_limit_bytes=60 * 2**20))(*args)


def local(tokens, cotangent, segment_ids, q_weight, key_weight, value_weight, q_bias, value_bias, out_weight, out_bias,
          norm1_gain, norm1_bias, inter_weight, inter_bias, ffo_weight, ffo_bias, norm2_gain, norm2_bias):
    n, nf = lax.axis_size("ctx"), lax.axis_size("fsdp")
    S = jax.ShapeDtypeStruct
    rows = MICRO * 128
    tok = tokens.reshape(MICRO, 128, D)
    gather = lambda a, ax: lax.all_gather(a, "fsdp", axis=ax, tiled=True)
    wqkv = gather(jnp.stack([q_weight, key_weight, value_weight]), 1)
    wout, wint, wffo = gather(out_weight, 0), gather(inter_weight, 0), gather(ffo_weight, 0)
    dl = q_bias.shape[0]
    pack = jnp.concatenate([jnp.stack([out_bias, norm1_gain, norm1_bias, ffo_bias, norm2_gain, norm2_bias, q_bias, value_bias]),
                            inter_bias.reshape(4, dl)], axis=0)
    allv = lax.all_gather(pack, "fsdp", axis=0)
    top = jnp.swapaxes(allv[:, 0:8], 0, 1).reshape(8, D)
    low = allv[:, 8:12].reshape(4, D)
    vec = jnp.concatenate([top, low, jnp.zeros((4, D), BF)], axis=0).astype(F32)
    bqv = jnp.concatenate([top[6:8], jnp.zeros((6, D), BF)], axis=0)
    xt = remote(tokens_kernel, n, 0, S((n, CH, 128), BF), (tok, segment_ids.reshape(MICRO, 128)), [pltpu.VMEM((12, CH, 128), BF)])
    ctx, cf, l, lohi = attn_fwd(xt, wqkv, bqv)
    ctxt = remote(rows_kernel, n, 1, S((12, GW, 128), BF), (ctx,))
    out, d1, dct, ga, gi, gf, gv = dense(tok.reshape(rows, D), cotangent.reshape(rows, D), ctxt.reshape(MICRO, D, 128), wout, wint, wffo, vec)
    dc = remote(units_kernel, n, 2, S((n, GW, 128), BF), (dct.reshape(12, GW, 128),))
    dx, gw, gb = attn_bwd(xt, wqkv, bqv, dc, cf, l, lohi)
    grad = remote(final_kernel, n, 3, S((MICRO, 128, D), BF), (dx, d1.reshape(MICRO, 128, D)), [pltpu.VMEM((12, GW, 128), BF)])
    scatter = lambda a: lax.psum(lax.psum_scatter(a, "fsdp", scatter_dimension=0, tiled=True), "ctx").astype(F32)
    gvec = lax.psum(jnp.concatenate([gv, gb], axis=0), ("fsdp", "ctx"))
    me = lax.axis_index("fsdp")
    part = lambda i: lax.dynamic_slice(gvec[i], (me * dl,), (dl,))
    gib = lax.dynamic_slice(gvec[8:12].reshape(4 * D), (me * 4 * dl,), (4 * dl,))
    return (out.reshape(tokens.shape), grad.reshape(tokens.shape), scatter(gw[0]), scatter(gw[1]), scatter(gw[2]), part(16), part(17),
            scatter(ga), part(0), part(1), part(2), scatter(gi), gib, scatter(gf.T), part(3), part(4), part(5))


def solution(mesh):
    act, seg, mat, vec = P(None, "fsdp", "ctx", None), P(None, "fsdp", "ctx"), P("fsdp", None), P("fsdp")
    return jax.shard_map(
        local, mesh=mesh,
        in_specs=(act, act, seg, mat, mat, mat, vec, vec, mat, vec, vec, vec, mat, vec, mat, vec, vec, vec),
        out_specs=(act, act, mat, mat, mat, vec, vec, mat, vec, vec, vec, mat, vec, mat, vec, vec, vec),
        check_vma=False)
```

time: 1160 us -> 521 us (0.45)
  matrix products: 291 us -> 0 us
  blocking collectives: 301 us -> 20.9 us
  local copies, waits for them, and re-layouts: 271 us -> 15.1 us
  waiting for transfers between devices: 112 us -> 301 us
  Pallas kernels: 0 us -> 161 us
  other arithmetic: 151 us -> 6.92 us
    dot_general x138 -> x0, matrix products: 291 us -> none  [the longest x36 63.8 us: score_block(): jnp.einsum('sqhd,skhd->shqk', query_block, key_block, preferred_element_t...]
    all_gather x21 -> x2, blocking collectives: 232 us -> 20.9 us  [the longest x1 15.6 us: local(): gather = lambda a, ax: lax.all_gather(a, 'fsdp', axis=ax, tiled=True)]
    psum x1 -> x2, waiting for transfers between devices: 6.04 us -> 206 us  [the longest x1 104 us: local(): gvec = lax.psum(jnp.concatenate([gv, gb], axis=0), ('fsdp', 'ctx'))]
    pallas_call x0 -> x7, Pallas kernels: none -> 161 us  [the longest x4 80 us: remote(): pl.pallas_call(lambda *a: kernel(n, *a), out_shape=outs, in_specs=[vm] *...]
    dynamic_slice x96 -> x5, local copies, waits for them, and re-layouts: 138 us -> 3.09 us  [the longest x4 2.41 us: local(): part = lambda i: lax.dynamic_slice(gvec[i], (me * dl,), (dl,))]
    all_gather x15 -> x3, waiting for transfers between devices: 85.2 us -> 0.01 us  [local(): gather = lambda a, ax: lax.all_gather(a, 'fsdp', axis=ax, tiled=True)]
    reduce_scatter x5, waiting for transfers between devices: 15.9 us -> 90.4 us  [local(): lax.psum_scatter(a, 'fsdp', scatter_dimension=0, tiled=True)]
    psum x1 -> x0, blocking collectives: 59.9 us -> none  [local(): lax.psum(reduced[3].astype(jnp.bfloat16), 'ctx').astype(jnp.float32)]
  transfers between devices with their start and end apart: 22 -> 11, of which waited for: 6 -> 7; matrix products, arithmetic and copies ran while one was open for 53% -> 2% of each run, Pallas kernels for 0% -> 27%
where the time goes in v1:
time: 521 us; the launch traced here: 520 us
  waiting for transfers between devices  301 us (58%)
  Pallas kernels  161 us (31%)
  blocking collectives  20.9 us (4%)
  local copies, waits for them, and re-layouts  15.1 us (3%)
  between operations  14.3 us (3%)
  other arithmetic  6.92 us (1%)
    psum x1, waiting for transfers between devices, local(): gvec = lax.psum(jnp.concatenate([gv, gb], axis=0), ('fsdp', 'ctx'))  104 us
    psum x1, waiting for transfers between devices, local(): lax.psum(lax.psum_scatter(a, 'fsdp', scatter_dimension=0, tiled=True), 'c...  102 us
    reduce_scatter x5, waiting for transfers between devices, local(): lax.psum_scatter(a, 'fsdp', scatter_dimension=0, tiled=True)  90.4 us
    pallas_call x4, Pallas kernels, remote(): pl.pallas_call(lambda *a: kernel(n, *a), out_shape=outs, in_specs=[vm] *...  80 us
    pallas_call x1, Pallas kernels, attn_bwd(): pl.pallas_call(lambda *a: bwd_kernel(nb, *a), out_shape=(jax.ShapeDtypeSt...  39.7 us
    pallas_call x1, Pallas kernels, attn_fwd(): pl.pallas_call(lambda *a: fwd_kernel(nb, *a), out_shape=(jax.ShapeDtypeSt...  20.8 us
    pallas_call x1, Pallas kernels, dense(): pl.pallas_call(lambda *a: dense_body(rows, *a), out_shape=(S((rows, D), B...  20.5 us
    all_gather x1, blocking collectives, local(): gather = lambda a, ax: lax.all_gather(a, 'fsdp', axis=ax, tiled=True)  15.6 us
  transfers between devices with their start and end apart: 11, of which 7 were waited for; matrix products, arithmetic and copies ran while one was open for 2% of the time, Pallas kernels for 27%

profile of v1, /device:TPU:0, one launch (start us, length us, event | category | flops | bytes accessed | tf_op | source)
XLA Modules:
  0.0 520.2 jit_solution(777386890518465962)
XLA Ops:
  7.3 0.0 all-gather.10.cloned.1.call-start
  7.3 0.7 all-gather.10.cloned.1.call-update
  8.0 0.0 all-gather.6.cloned.1.call-start
  8.1 0.7 all-gather.6.cloned.1.call-update
  8.8 0.0 all-gather.8.cloned.1.call-start
  8.9 0.7 all-gather.8.cloned.1.call-update
  9.5 0.0 reduce-scatter.19.cloned.1.call-start
  9.8 0.1 concatenate.12
  9.8 5.3 %all-gather.1 = bf16[2,12,384]{2,1,0:T(8,128)(2,1)S(1)} all-gather(bf16[1,12,384]{2,1,0:T(8,128)(2,1)S(1)} %bitcast.43), channel_id=2, replica_groups=mesh['fsdp'=2,'ctx'=16] {'fsdp'}, dimensions={0}, use_global_device_ids=true | all-gather | bytes 27648 | tf_op jit(solution)/shard_map/all_gather | solution.py:481
  15.2 0.6 copy.49
  15.8 0.6 concatenate.13.a_2_
  16.4 18.4 %shard_map.305.a_0_ = bf16[16,208,128]{2,1,0:T(8,128)(2,1)} custom-call(bf16[3,128,768]{2,1,0:T(8,128)(2,1)} %bitcast.33, s32[3,128]{1,0:T(4,128)} %bitcast.46), custom_call_target="tpu_custom_call" | custom-call | tf_op jit(solution)/shard_map/pallas_call | solution.py:462
  34.8 0.1 pad_maximum_fusion
  34.9 15.6 %all_gather.18.a_1_ = bf16[3,192,768]{2,1,0:T(8,128)(2,1)} all-gather(bf16[3,96,768]{2,1,0:T(8,128)(2,1)S(1)} %pad_maximum_fusion), channel_id=1, replica_groups=mesh['fsdp'=2,'ctx'=16] {'fsdp'}, dimensions={1}, use_global_device_ids=true | all-gather | bytes 1327104 | tf_op jit(solution)/shard_map/all_gather | solution.py:475
  50.5 20.8 %shard_map.306 = (bf16[16,192,128]{2,1,0:T(8,128)(2,1)}, f32[8,192,256]{2,1,0:T(8,128)}, f32[8,8,256]{2,1,0:T(8,128)}, s32[8,128]{1,0:T(8,128)}) custom-call(bf16[16,208,128]{2,1,0:T(8,128)(2,1)} %shard_map.305.a_0_, bf16[3,192,768]{2,1,0:T(8,128)(2,1)} %all_gather.18.a_1_, bf16[8,768]{1,0:T(8,128)(2,1)} %concatenate.13.a_2_), custom_call_target="tpu_custom_call" | custom-call | tf_op jit(solution)/shard_map/pallas_call | solution.py:215
  71.3 23.8 %shard_map.307 = bf16[12,192,128]{2,1,0:T(8,128)(2,1)} custom-call(bf16[16,192,128]{2,1,0:T(8,128)(2,1)} %get-tuple-element.31.a_0_), custom_call_target="tpu_custom_call" | custom-call | tf_op jit(solution)/shard_map/pallas_call | solution.py:462
  95.2 0.1 pad.5.clone
  95.3 0.7 maximum_convert_fusion.a_6_
  96.0 20.5 %shard_map.308 = (bf16[384,768]{1,0:T(8,128)(2,1)}, f32[384,768]{1,0:T(8,128)}, bf16[3,768,128]{2,1,0:T(8,128)(2,1)}, bf16[768,768]{1,0:T(8,128)(2,1)}, bf16[192...) custom-call(bf16[384,768]{1,0:T(8,128)(2,1)} %bitcast.34, bf16[384,768]{1,0:T(8,128)(2,1)} %bitcast.38, ...), custom_call_target="tpu_custom_call" | custom-call | tf_op jit(solution)/shard_map/pallas_call | solution.py:420
  116.5 2.4 copy.45
  118.9 0.0 reduce-scatter.19.cloned.1.call-update
  118.9 0.0 reduce-scatter.11.cloned.1.call-start
  119.0 17.0 %shard_map.309.a_3_ = bf16[16,192,128]{2,1,0:T(8,128)(2,1)} custom-call(bf16[12,192,128]{2,1,0:T(8,128)(2,1)} %bitcast.39), custom_call_target="tpu_custom_call" | custom-call | tf_op jit(solution)/shard_map/pallas_call | solution.py:462
  135.9 39.7 %shard_map.310 = (bf16[16,192,128]{2,1,0:T(8,128)(2,1)}, bf16[3,192,768]{2,1,0:T(8,128)(2,1)}, f32[8,768]{1,0:T(8,128)}) custom-call(bf16[16,208,128]{2,1,0:T(8,128)(2,1)} %shard_map.305.a_0_, bf16[3,192,768]{2,1,0:T(8,128)(2,1)} %all_gather.18.a_1_, bf16[8,768]{1,0:T(8,128)(2,1)} %concatenate.13.a_2_, bf16[16,192,128]{2,1,0:T(8,128)(2,1)} %shard_map.309.a_3_, ...), custom_call_target="tpu_custom_call" | custom-call | tf_op jit(solution)/shard_map/pallas_call | solution.py:298
  175.7 2.1 slice_bitcast_fusion
  177.7 0.0 reduce-scatter.11.cloned.1.call-update
  177.8 0.0 reduce-scatter.13.cloned.1.call-start
  177.8 0.5 reduce-scatter.13.cloned.1.call-update
  178.3 0.0 reduce-scatter.9.cloned.1.call-start
  178.4 0.7 reduce-scatter.9.cloned.1.call-update
  179.1 0.0 reduce-scatter.15.cloned.1.call-start
  179.2 0.7 reduce-scatter.15.cloned.1.call-update
  179.8 0.0 reduce-scatter.17.cloned.1.call-start
  179.9 0.7 reduce-scatter.17.cloned.1.call-update
  180.6 0.0 all-reduce.5.cloned.1.call-start
  180.6 0.6 pad_maximum_fusion.1
  181.3 0.0 all-reduce.5.cloned.1.call-update
  181.3 0.0 all-reduce.7.cloned.1.call-start
  181.4 0.0 reduce-scatter.19.cloned.1.call-done
  181.4 2.1 copy.46
  183.5 11.3 %reduce-scatter.11.cloned.1.call-done = bf16[96,768]{1,0:T(8,128)(2,1)} async-done(((bf16[192,768]{1,0:T(8,128)(2,1)}), bf16[96,768]{1,0:T(8,128)(2,1)}) %reduce-scatter.11.cloned.1.call-update) | async-done | bytes 147472 | tf_op jit(solution)/shard_map/reduce_scatter | solution.py:493
  194.8 14.8 %reduce-scatter.13.cloned.1.call-done = bf16[96,768]{1,0:T(8,128)(2,1)} async-done(((bf16[192,768]{1,0:T(8,128)(2,1)}), bf16[96,768]{1,0:T(8,128)(2,1)}) %reduce-scatter.13.cloned.1.call-update) | async-done | bytes 147472 | tf_op jit(solution)/shard_map/reduce_scatter | solution.py:493
  209.7 15.0 %reduce-scatter.9.cloned.1.call-done = bf16[96,768]{1,0:T(8,128)(2,1)} async-done(((bf16[192,768]{1,0:T(8,128)(2,1)}), bf16[96,768]{1,0:T(8,128)(2,1)}) %reduce-scatter.9.cloned.1.call-update) | async-done | bytes 147472 | tf_op jit(solution)/shard_map/reduce_scatter | solution.py:493
  224.6 24.7 %reduce-scatter.15.cloned.1.call-done = bf16[384,768]{1,0:T(8,128)(2,1)} async-done(((bf16[768,768]{1,0:T(8,128)(2,1)}), bf16[384,768]{1,0:T(8,128)(2,1)}) %reduce-scatter.15.cloned.1.call-update) | async-done | bytes 589840 | tf_op jit(solution)/shard_map/reduce_scatter | solution.py:493
  249.3 24.6 %reduce-scatter.17.cloned.1.call-done = bf16[96,3072]{1,0:T(8,128)(2,1)} async-done(((bf16[192,3072]{1,0:T(8,128)(2,1)}), bf16[96,3072]{1,0:T(8,128)(2,1)}) %reduce-scatter.17.cloned.1.call-update) | async-done | bytes 589840 | tf_op jit(solution)/shard_map/reduce_scatter | solution.py:493
  273.9 0.0 all-reduce.7.cloned.1.call-update
  273.9 20.8 %shard_map.311 = bf16[3,128,768]{2,1,0:T(8,128)(2,1)} custom-call(bf16[16,192,128]{2,1,0:T(8,128)(2,1)} %get-tuple-element.37.a_0_, f32[3,128,768]{2,1,0:T(8,128)} %bitcast.36), custom_call_target="tpu_custom_call" | custom-call | tf_op jit(solution)/shard_map/pallas_call | solution.py:462
  294.7 104.1 %all-reduce.5.cloned.1.call-done = f32[24,768]{1,0:T(8,128)} async-done(((f32[24,768]{1,0:T(8,128)}), f32[24,768]{1,0:T(8,128)}) %all-reduce.5.cloned.1.call-update) | async-done | bytes 73744 | tf_op jit(solution)/shard_map/psum | solution.py:494
  398.8 0.7 slice.72
  399.5 0.7 dynamic_slice.53
  400.2 1.1 fusion.8
  401.3 0.6 fusion.6
  401.9 0.6 fusion.4
  402.5 0.6 fusion.2
  403.1 0.6 fusion
  403.7 102.2 %all-reduce.7.cloned.1.call-done = (bf16[384,768]{0,1:T(8,128)(2,1)}, bf16[96,768]{1,0:T(8,128)(2,1)}, bf16[96,768]{1,0:T(8,128)(2,1)}, bf16[96,768]{1,0:T(8,128...) async-done(((bf16[384,768]{0,1:T(8,128)(2,1)}, bf16[96,768]{1,0:T(8,128)(2,1)}, bf16[96,768]{1,0:T(8,128)(2,1)}, bf16[96,768]{1,0:T(8,128)(2,1)}, ...) | async-done | bytes 2211856 | tf_op jit(solution)/shard_map/psum | solution.py:493
  505.9 2.2 convert_element_type.25
  508.1 1.1 convert_element_type.26
  509.2 0.1 copy-done.1
  509.3 1.3 copy.44
  510.6 0.7 convert_element_type.22
  511.3 0.7 convert_element_type.23
  512.1 0.7 convert_element_type.24
  512.8 0.8 copy.58
  (59 shorter events, 0.2 us)
Async XLA Ops:
  7.2 2.4 copy-start.11
  7.2 2.4 copy-start.13
  7.2 2.4 copy-start.14
  7.2 2.4 copy-start.15
  7.2 2.4 copy-start.16
  7.2 2.5 copy-start.17
  7.3 2.5 copy-start.18
  7.3 2.5 copy-start.19
  7.3 2.5 copy-start.20
  7.3 7.9 %copy-start.12 = (s32[3,1,128]{2,1,0:T(1,128)S(1)}, s32[3,1,128]{2,1,0:T(1,128)}, u32[]{:S(2)}) copy-start(s32[3,1,128]{2,1,0:T(1,128)} %param.20) | copy-start | bytes 4612
  7.3 88.7 %all-gather.10.cloned.1.call-start = ((), (), s32[]{:S(2)}) async-start(), calls=%async_computation.8 | async-start | bytes 1769472 | tf_op jit(solution)/shard_map/all_gather | solution.py:475
  8.0 88.0 %all-gather.6.cloned.1.call-start = ((), (), s32[]{:S(2)}) async-start(), calls=%async_computation.6 | async-start | bytes 1769472 | tf_op jit(solution)/shard_map/all_gather | solution.py:475
  8.8 26.0 %copy-start.3 = (bf16[96,768]{1,0:T(8,128)(2,1)S(1)}, bf16[96,768]{1,0:T(8,128)(2,1)}, u32[]{:S(2)}) copy-start(bf16[96,768]{1,0:T(8,128)(2,1)} %param.23) | copy-start | bytes 442372
  8.8 26.0 %copy-start.4 = (bf16[96,768]{1,0:T(8,128)(2,1)S(1)}, bf16[96,768]{1,0:T(8,128)(2,1)}, u32[]{:S(2)}) copy-start(bf16[96,768]{1,0:T(8,128)(2,1)} %param.22) | copy-start | bytes 442372
  8.8 26.0 %copy-start.5 = (bf16[96,768]{1,0:T(8,128)(2,1)S(1)}, bf16[96,768]{1,0:T(8,128)(2,1)}, u32[]{:S(2)}) copy-start(bf16[96,768]{1,0:T(8,128)(2,1)} %param.21) | copy-start | bytes 442372
  8.8 87.2 %all-gather.8.cloned.1.call-start = ((), (), s32[]{:S(2)}) async-start(), calls=%async_computation.7 | async-start | bytes 1769472 | tf_op jit(solution)/shard_map/all_gather | solution.py:475
  9.5 171.8 %reduce-scatter.19.cloned.1.call-start = ((), (), s32[]{:S(2)}) async-start(), calls=%async_computation.15 | async-start | bytes 1769472
  118.9 75.9 %reduce-scatter.11.cloned.1.call-start = ((), (), s32[]{:S(2)}) async-start(), calls=%async_computation.10 | async-start | bytes 442368 | tf_op jit(solution)/shard_map/reduce_scatter | solution.py:493
  177.8 31.9 %reduce-scatter.13.cloned.1.call-start = ((), (), s32[]{:S(2)}) async-start(), calls=%async_computation.11 | async-start | bytes 442368 | tf_op jit(solution)/shard_map/reduce_scatter | solution.py:493
  178.3 46.3 %reduce-scatter.9.cloned.1.call-start = ((), (), s32[]{:S(2)}) async-start(), calls=%async_computation.9 | async-start | bytes 442368 | tf_op jit(solution)/shard_map/reduce_scatter | solution.py:493
  179.1 70.2 %reduce-scatter.15.cloned.1.call-start = ((), (), s32[]{:S(2)}) async-start(), calls=%async_computation.13 | async-start | bytes 1769472 | tf_op jit(solution)/shard_map/reduce_scatter | solution.py:493
  179.1 1.5 copy-start.9
  179.1 1.5 copy-start.10
  179.8 94.1 %reduce-scatter.17.cloned.1.call-start = ((), (), s32[]{:S(2)}) async-start(), calls=%async_computation.14 | async-start | bytes 1769472 | tf_op jit(solution)/shard_map/reduce_scatter | solution.py:493
  180.6 218.2 %all-reduce.5.cloned.1.call-start = ((), (), s32[]{:S(2)}) async-start(), calls=%async_computation.12 | async-start | bytes 147456 | tf_op jit(solution)/shard_map/psum | solution.py:494
  181.3 324.6 %all-reduce.7.cloned.1.call-start = ((), (), s32[]{:S(2)}) async-start(), calls=%async_computation.16 | async-start | bytes 4423680 | tf_op jit(solution)/shard_map/psum | solution.py:493
  505.9 2.2 copy-start.2
  508.1 1.2 copy-start.1
  509.2 1.4 copy-start.8
  509.2 2.1 copy-start.7
  509.3 2.8 copy-start.6
  509.3 3.5 copy-start
Sparse Core Ops, SparseCore 0:
  9.7 25.4 all-gather.9
  36.7 24.7 all-gather.5
  63.0 25.4 all-gather.7
  119.0 24.1 reduce-scatter.18
  177.9 16.8 reduce-scatter.10
  197.6 12.0 reduce-scatter.12
  212.5 12.0 reduce-scatter.8
  227.5 21.7 reduce-scatter.14
  252.1 21.7 reduce-scatter.16
  280.3 118.4 all-reduce.4
  404.3 101.5 all-reduce.6

commit v2 on v1

v2 whole, which is shorter than its diff:
```python
import math

import jax
import jax.numpy as jnp
from jax import lax
from jax.experimental import pallas as pl
from jax.experimental.pallas import tpu as pltpu
from jax.sharding import PartitionSpec as P

MESH = pl.DeviceIdType.MESH
MICRO = 3


def place(n, g, m):
    return g * (n // 4) + m + (g % 2)


def owners(n):
    return [place(n, g, m) for m in range(MICRO) for g in range(4)]


def unit_of(c, n):
    g = c // (n // 4)
    m = c - g * (n // 4) - lax.rem(g, 2)
    return g, m, (m >= 0) & (m < MICRO)


def greet(f, c, n):
    bar = pltpu.get_barrier_semaphore()
    for d in range(1, n):
        pl.semaphore_signal(bar, inc=1, device_id=(f, lax.rem(c + d, n)), device_id_type=MESH)
    pl.semaphore_wait(bar, n - 1)


BF, F32 = jnp.bfloat16, jnp.float32
HEAD, GW = 64, 192
CH = 208
XA = 240
BIG = 1e9
NN = (((1,), (0,)), ((), ()))
NT = (((1,), (1,)), ((), ()))
TN = (((0,), (0,)), ((), ()))

def mm(a, b, dims=NN):
    return lax.dot_general(a, b, dims, preferred_element_type=F32)

def iota(shape, axis):
    return lax.broadcasted_iota(jnp.int32, shape, axis)

def build_weights(w_ref, b_ref, wa_ref, wat_ref):
    for s in range(3):
        for h in range(3):
            w = w_ref[s, :, h * 64:h * 64 + 64].astype(F32)
            top = jnp.concatenate([w * (0.125 if s == 0 else 1.0), jnp.zeros((GW, 64), F32)], axis=1)
            r, c = iota((48, 128), 0), iota((48, 128), 1)
            same = (c - 64 == r)
            lanes = (c >= 64) & (c < 96) & (r < 32)
            one = (r == 32)
            zero = jnp.zeros((48, 128), F32)
            if s == 0:
                bias = jnp.concatenate([b_ref[0:1, h * 64:h * 64 + 64].astype(F32) * 0.125, jnp.zeros((1, 64), F32)], axis=1)
                low = jnp.where(lanes & same, 1.0, zero) + jnp.where(one, bias, zero)
            elif s == 1:
                low = jnp.where(lanes & ~same, -BIG, zero) + jnp.where(one & (c == 96), 1.0, zero)
            else:
                bias = jnp.concatenate([b_ref[1:2, h * 64:h * 64 + 64].astype(F32), jnp.zeros((1, 64), F32)], axis=1)
                low = jnp.where(one, bias, zero) + jnp.where(one & (c == 64), 1.0, zero)
            full = jnp.concatenate([top, low], axis=0)
            wa_ref[s, :, h * 128:h * 128 + 128] = full.astype(BF)
            wat_ref[s, h * 128:h * 128 + 128, :] = jnp.transpose(full).astype(BF)

D, FF = 768, 3072
EPS = 1e-12
WIN = (0, 128, 384, 512)
OFF = (0, 64, 0, 64)
RS2 = math.sqrt(0.5)
IPI = 1.0 / math.sqrt(2.0 * math.pi)
CK = 32

def rowmean(x):
    return jnp.sum(x, axis=-1, keepdims=True) * (1.0 / D)

def tall(ref, m):
    return jnp.concatenate([ref[m * 4 + g] for g in range(4)], axis=0)


def dense_body(rows, tok, cot, ctxt, wout, wint, wffo, vec, out, d1, dct, ga, gi, gf, gv,
               ctx, attn, n1b, wip, wfp, dpre, hid, br, dn, db, st, send):
    da = ctx
    nm = rows // 128
    v = lambda i: vec[i:i + 1, :]
    for j in range(4):
        o = OFF[j]
        wip[j] = jnp.zeros((256, D), BF)
        wip[j, o:o + 192, :] = wint[:, j * D:(j + 1) * D]
        lane = iota((D, 256), 1)
        w = wffo[:, WIN[j]:WIN[j] + 256]
        wfp[j] = jnp.where((lane >= o) & (lane < o + 192), w.astype(F32), 0.0).astype(BF)
    for m in range(nm):
        ctx[m * 128:(m + 1) * 128, :] = jnp.transpose(tall(ctxt, m))
    attn[...] = mm(ctx[...], wout[...])
    def ln1(t, c):
        s = pl.ds(pl.multiple_of(t * CK, CK), CK)
        r = attn[s, :] + v(0) + tok[s, :].astype(F32)
        cen = r - rowmean(r)
        rstd = lax.rsqrt(rowmean(cen * cen) + EPS)
        xh = cen * rstd
        attn[s, :] = xh
        st[s, :] = jnp.broadcast_to(rstd, (CK, 128))
        n = xh * v(1) + v(2)
        n1b[s, :] = n.astype(BF)
        br[s, :] = n + v(3)
        return c
    lax.fori_loop(0, rows // CK, ln1, 0)
    for j in range(4):
        for m in range(nm):
            s = slice(m * 128, (m + 1) * 128)
            u = mm(n1b[s, WIN[j]:WIN[j] + 256], wip[j]) + v(8 + j)
            half = 0.5 + 0.5 * lax.erf(u * RS2)
            hid[j, s, :] = (u * half).astype(BF)
            dpre[j, s, :] = (half + u * (jnp.exp(u * u * -0.5) * IPI)).astype(BF)
        br[:, WIN[j]:WIN[j] + 256] += mm(hid[j], wfp[j])
    gv[...] = jnp.zeros_like(gv)
    def ln2(t, c):
        s = pl.ds(pl.multiple_of(t * CK, CK), CK)
        r = br[s, :]
        cen = r - rowmean(r)
        rstd = lax.rsqrt(rowmean(cen * cen) + EPS)
        xh = cen * rstd
        out[s, :] = (xh * v(4) + v(5)).astype(BF)
        ct = cot[s, :].astype(F32)
        u = ct * v(4)
        dd = rstd * (u - rowmean(u) - xh * rowmean(u * xh))
        dn[s, :] = dd
        ddb = dd.astype(BF)
        db[s, :] = ddb
        gv[4:5, :] += jnp.sum(ct * xh, axis=0, keepdims=True)
        gv[5:6, :] += jnp.sum(ct, axis=0, keepdims=True)
        gv[3:4, :] += jnp.sum(ddb.astype(F32), axis=0, keepdims=True)
        return c
    lax.fori_loop(0, rows // CK, ln2, 0)
    for j in range(4):
        for m in range(nm):
            s = slice(m * 128, (m + 1) * 128)
            dh = mm(db[s, WIN[j]:WIN[j] + 256], wfp[j], NT)
            dp = (dh * dpre[j, s, :].astype(F32)).astype(BF)
            dpre[j, s, :] = dp
            gv[8 + j:9 + j, :] += jnp.sum(dp.astype(F32), axis=0, keepdims=True)
        dn[:, WIN[j]:WIN[j] + 256] += mm(dpre[j], wip[j], NT)
    def lnb(t, c):
        s = pl.ds(pl.multiple_of(t * CK, CK), CK)
        g = dn[s, :]
        xh = attn[s, :]
        u = g * v(1)
        dd = st[s, 0:1] * (u - rowmean(u) - xh * rowmean(u * xh))
        d1[s, :] = dd
        ddb = dd.astype(BF)
        da[s, :] = ddb
        gv[1:2, :] += jnp.sum(g * xh, axis=0, keepdims=True)
        gv[2:3, :] += jnp.sum(g, axis=0, keepdims=True)
        gv[0:1, :] += jnp.sum(ddb.astype(F32), axis=0, keepdims=True)
        return c
    lax.fori_loop(0, rows // CK, lnb, 0)
    dc = mm(wout[...], da[...], NT).astype(BF)
    for m in range(nm):
        for g in range(4):
            dct[m * 4 + g] = dc[g * GW:g * GW + GW, m * 128:(m + 1) * 128]
    send()
    ct = jnp.concatenate([tall(ctxt, m) for m in range(nm)], axis=1)
    ga[...] = mm(ct, da[...]).astype(BF)
    nt = jnp.transpose(n1b[...])
    dbt = jnp.transpose(db[...])
    for j in range(4):
        o = WIN[j] + OFF[j]
        gi[:, j * D:(j + 1) * D] = mm(nt[o:o + 192, :], dpre[j]).astype(BF)
        gf[j * 192:(j + 1) * 192, :] = mm(dbt[o:o + 192, :], hid[j]).astype(BF)

def remote_copy(src, dst, ssem, rsem, f, c):
    return pltpu.make_async_remote_copy(src_ref=src, dst_ref=dst, send_sem=ssem, recv_sem=rsem, device_id=(f, c), device_id_type=MESH)


def tile_at(q, t, half):
    p, mir = lax.rem(q, half // 2), lax.div(q, half // 2)
    b = lax.div(t + half - 1 - p, 2 * half)
    i = p + b * (half - 1 - 2 * p)
    j = t - b * (half + 1 + p)
    last = 2 * half - 1
    return b, i + mir * (last - 2 * i), j + mir * (last - 2 * j)


def rows_at(q, half):
    p, mir = lax.rem(q, half // 2), lax.div(q, half // 2)
    last = 2 * half - 1
    return [i + mir * (last - 2 * i) for i in (p, half - 1 - p)]


def forward_tiles(q, half, qt, ka, vt, acc):
    acc[...] = jnp.zeros_like(acc)
    items = [(h,) + tile_at(q, t, half) for t in range(3 * half + 1) for h in range(3)]
    def front(it):
        h, _, i, j = it
        return mm(ka[h, j], qt[h, i])
    ready = [front(it) for it in items[:3]]
    for t, (h, b, i, j) in enumerate(items):
        if t + 3 < len(items):
            ready.append(front(items[t + 3]))
        e = jnp.exp(ready[t]).astype(BF)
        ready[t] = None
        acc[h, b] += mm(vt[h, j], e)


def backward_tiles(q, half, qt, ka, kt, va, dnt, dq, dk, dv):
    dq[...] = jnp.zeros_like(dq)
    items = [(h,) + tile_at(q, t, half) for t in range(3 * half + 1) for h in range(3)]
    def front(it):
        h, _, i, j = it
        return mm(ka[h, j], qt[h, i]), mm(va[h, j, :, 0:80], dnt[h, i])
    ready = [front(it) for it in items[:2]]
    for t, (h, b, i, j) in enumerate(items):
        if t + 2 < len(items):
            ready.append(front(items[t + 2]))
        s, dp = ready[t]
        ready[t] = None
        e = jnp.exp(s)
        eb = e.astype(BF)
        ds = (e * dp).astype(BF)
        dq[h, b] += mm(kt[h, j], ds)
        dk[h, j] += mm(qt[h, i, 0:64], ds, NT)
        dv[h, j] += mm(dnt[h, i, 0:64], eb, NT)


def prep_block(i, xt, wa, wat, qt, ka, vt, kt, va):
    x = jnp.concatenate([xt[2 * i], xt[2 * i + 1]], axis=1)
    seg = x[GW:GW + 16].astype(F32)[0:1].astype(jnp.int32)
    r = iota((48, 256), 0)
    aug = jnp.where((r == seg) & (r < 32) | (r == 32), 1.0, 0.0).astype(BF)
    xa = jnp.concatenate([x[0:GW], aug], axis=0)
    xn = jnp.transpose(xa)
    q = mm(wat[0], xa).astype(BF)
    k = mm(wat[1], xa).astype(BF)
    v = mm(wat[2], xa).astype(BF)
    kn = mm(xn, wa[1]).astype(BF)
    vn = mm(xn, wa[2]).astype(BF)
    for h in range(3):
        o = h * 128
        qt[h, i] = q[o:o + 128]
        anchor = jnp.sum(q[o:o + 64].astype(F32) * k[o:o + 64].astype(F32), axis=0, keepdims=True)
        qt[h, i, 96:112] = jnp.where(iota((16, 256), 0) == 0, -anchor, 0.0).astype(BF)
        ka[h, i] = kn[:, o:o + 128]
        vt[h, i] = v[o:o + 80]
        kt[h, i] = k[o:o + 64]
        va[h, i] = vn[:, o:o + 128]


def mega(n, tok, seg, cot, wqkv, bqv, wout, wint, wffo, vec,
         out, grad, gw, gb, ga, gi, gf, gv,
         tsend, xt, csend, crecv, dsend, dc, xrecv,
         w, bias, wa, wat, qt, ka, vt, kt, va, cf, lsum, acc, dq, dk, dv, dqt, gacc, gbacc,
         d1, dense_refs, tss, trs, css, crs, dss, drs, xss, xrs, ls):
    f, c = lax.axis_index("fsdp"), lax.axis_index("ctx")
    g, m, mine = unit_of(c, n)
    u = m * 4 + g
    own = owners(n)
    sb, half = n // 2, n // 4
    dnt = vt
    bar = pltpu.get_barrier_semaphore()
    for d in range(1, n):
        pl.semaphore_signal(bar, inc=1, device_id=(f, lax.rem(c + d, n)), device_id_type=MESH)
    for k in range(MICRO):
        t = jnp.transpose(tok[k * 128:k * 128 + 128, :])
        sg = jnp.broadcast_to(seg[k:k + 1, :].astype(F32), (16, 128)).astype(BF)
        for j in range(4):
            tsend[k * 4 + j, 0:GW, :] = t[j * GW:j * GW + GW]
            tsend[k * 4 + j, GW:CH, :] = sg
    pl.semaphore_wait(bar, n - 1)

    def spread(src, dst, ss, rs, start):
        for k in range(12):
            @pl.when(c != own[k])
            def _():
                cp = remote_copy(src.at[k], dst.at[c], ss.at[k], rs.at[c], f, own[k])
                cp.start() if start else cp.wait_send()
            if start:
                @pl.when(c == own[k])
                def _():
                    pltpu.make_async_copy(src.at[k], dst.at[c], rs.at[c]).start()
    def arrived(src, dst, rs, s):
        @pl.when(c != s)
        def _():
            remote_copy(src.at[0], dst.at[s], ls, rs.at[s], f, s).wait_recv()
        @pl.when(c == s)
        def _():
            pltpu.make_async_copy(src.at[0], dst.at[s], rs.at[s]).wait()
    def give(src, dst, ss, rs, t, start):
        @pl.when(c != t)
        def _():
            cp = remote_copy(src.at[t], dst.at[u], ss.at[t], rs.at[u], f, t)
            cp.start() if start else cp.wait_send()
        if start:
            @pl.when(c == t)
            def _():
                pltpu.make_async_copy(src.at[t], dst.at[u], rs.at[u]).start()
    def taken(src, dst, rs):
        for k in range(12):
            @pl.when(c != own[k])
            def _():
                remote_copy(src.at[0], dst.at[k], ls, rs.at[k], f, own[k]).wait_recv()
            @pl.when(c == own[k])
            def _():
                pltpu.make_async_copy(src.at[0], dst.at[k], rs.at[k]).wait()

    spread(tsend, xt, tss, trs, True)

    @pl.when(mine)
    def _():
        for k in range(4):
            @pl.when(g == k)
            def _():
                w[...] = wqkv[:, :, k * GW:k * GW + GW]
                bias[...] = bqv[:, k * GW:k * GW + GW]
        build_weights(w, bias, wa, wat)
        def first(i, carry):
            arrived(tsend, xt, trs, 2 * i)
            arrived(tsend, xt, trs, 2 * i + 1)
            prep_block(i, xt, wa, wat, qt, ka, vt, kt, va)
            return carry
        lax.fori_loop(0, sb, first, 0)
        def step(q, carry):
            forward_tiles(q, half, qt, ka, vt, acc)
            for b, i in enumerate(rows_at(q, half)):
                for h in range(3):
                    a = acc[h, b]
                    x = a[0:64] / a[64:65]
                    cf[i, h * 64:h * 64 + 64, :] = x
                    lsum[i, h:h + 1, :] = a[64:65]
                    xb = x.astype(BF)
                    csend[2 * i, h * 64:h * 64 + 64, :] = xb[:, 0:128]
                    csend[2 * i + 1, h * 64:h * 64 + 64, :] = xb[:, 128:256]
                give(csend, crecv, css, crs, 2 * i, True)
                give(csend, crecv, css, crs, 2 * i + 1, True)
            return carry
        lax.fori_loop(0, half, step, 0)
        dk[...] = jnp.zeros_like(dk)
        dv[...] = jnp.zeros_like(dv)

    taken(csend, crecv, crs)
    def send_dct():
        spread(dsend, dc, dss, drs, True)
    dense_body(MICRO * 128, tok, cot, crecv, wout, wint, wffo, vec, out, d1, dsend, ga, gi, gf, gv, *dense_refs, send=send_dct)

    gw[...] = jnp.zeros_like(gw)
    gb[...] = jnp.zeros_like(gb)

    @pl.when(mine)
    def _():
        def step(q, carry):
            for b, i in enumerate(rows_at(q, half)):
                arrived(dsend, dc, drs, 2 * i)
                arrived(dsend, dc, drs, 2 * i + 1)
                d = jnp.concatenate([dc[2 * i], dc[2 * i + 1]], axis=1).astype(F32)
                for h in range(3):
                    dh = d[h * 64:h * 64 + 64]
                    inv = 1.0 / lsum[i, h:h + 1, :]
                    delta = jnp.sum(dh * cf[i, h * 64:h * 64 + 64, :], axis=0, keepdims=True) * inv
                    dnt[h, i] = jnp.concatenate([dh * inv, jnp.where(iota((16, 256), 0) == 0, -delta, 0.0)], axis=0).astype(BF)
            backward_tiles(q, half, qt, ka, kt, va, dnt, dq, dk, dv)
            for b, i in enumerate(rows_at(q, half)):
                for h in range(3):
                    dqt[i, h * 64:h * 64 + 64, :] = (dq[h, b] * 0.125).astype(BF)
            return carry
        lax.fori_loop(0, half, step, 0)
        for t in range(n):
            give(csend, crecv, css, crs, t, False)
        xsend = csend
        gacc[...] = jnp.zeros_like(gacc)
        gbacc[...] = jnp.zeros_like(gbacc)
        ones = jnp.ones((8, 256), BF)
        def post(i, carry):
            x = jnp.concatenate([xt[2 * i, 0:GW, :], xt[2 * i + 1, 0:GW, :]], axis=1)
            q = dqt[i]
            k = jnp.concatenate([dk[h, i] for h in range(3)], axis=0).astype(BF)
            v = jnp.concatenate([dv[h, i] for h in range(3)], axis=0).astype(BF)
            x2 = (mm(w[0], q) + mm(w[1], k) + mm(w[2], v)).astype(BF)
            xsend[2 * i] = x2[:, 0:128]
            xsend[2 * i + 1] = x2[:, 128:256]
            give(xsend, xrecv, xss, xrs, 2 * i, True)
            give(xsend, xrecv, xss, xrs, 2 * i + 1, True)
            gacc[0] += mm(x, q, NT)
            gacc[1] += mm(x, k, NT)
            gacc[2] += mm(x, v, NT)
            gbacc[0] += mm(ones, q, NT)
            gbacc[1] += mm(ones, v, NT)
            return carry
        lax.fori_loop(0, sb, post, 0)
        for k in range(4):
            @pl.when(g == k)
            def _():
                gw[:, :, k * GW:k * GW + GW] = gacc[...].astype(BF)
                gb[0:1, k * GW:k * GW + GW] = gbacc[0, 0:1]
                gb[1:2, k * GW:k * GW + GW] = gbacc[1, 0:1]

    taken(csend, xrecv, xrs)
    for k in range(MICRO):
        x = jnp.concatenate([xrecv[k * 4 + j] for j in range(4)], axis=0).astype(F32)
        s = slice(k * 128, k * 128 + 128)
        grad[s, :] = (jnp.transpose(x) + d1[s, :]).astype(BF)
    spread(tsend, xt, tss, trs, False)
    spread(dsend, dc, dss, drs, False)
    @pl.when(mine)
    def _():
        for t in range(n):
            give(csend, xrecv, xss, xrs, t, False)

DMA = pltpu.SemaphoreType.DMA


def run_mega(n, tok, seg, cot, wqkv, bqv, wout, wint, wffo, vec):
    S, V = jax.ShapeDtypeStruct, pltpu.VMEM
    rows, sb = MICRO * 128, n // 2
    vm = pl.BlockSpec(memory_space=pltpu.VMEM)
    outs = (S((rows, D), BF), S((rows, D), BF), S((3, GW, D), BF), S((8, D), F32), S((D, D), BF), S((192, FF), BF), S((D, D), BF), S((16, D), F32))
    dense_refs = [V((rows, D), BF), V((rows, D), F32), V((rows, D), BF), V((4, 256, D), BF), V((4, D, 256), BF), V((4, rows, D), BF),
                  V((4, rows, D), BF), V((rows, D), F32), V((rows, D), F32), V((rows, D), BF), V((rows, 128), F32)]
    scratch = [V((12, CH, 128), BF), V((n, CH, 128), BF), V((n, GW, 128), BF), V((12, GW, 128), BF), V((12, GW, 128), BF), V((n, GW, 128), BF),
               V((12, GW, 128), BF),
               V((3, GW, GW), BF), V((8, GW), BF), V((3, XA, 384), BF), V((3, 384, XA), BF), V((3, sb, 128, 256), BF), V((3, sb, 256, 128), BF),
               V((3, sb, 80, 256), BF), V((3, sb, 64, 256), BF), V((3, sb, 256, 128), BF), V((sb, GW, 256), F32), V((sb, 8, 256), F32),
               V((3, 2, 80, 256), F32), V((3, 2, 64, 256), F32), V((3, sb, 64, 256), F32), V((3, sb, 64, 256), F32), V((sb, GW, 256), BF), V((3, GW, GW), F32), V((2, 8, GW), F32),
               V((rows, D), F32), dense_refs] + [DMA((12,)), DMA((n,)), DMA((n,)), DMA((12,)), DMA((12,)), DMA((n,)), DMA((n,)), DMA((12,)), DMA]
    return pl.pallas_call(
        lambda *a: mega(n, *a), out_shape=outs, in_specs=[vm] * 9, out_specs=(vm,) * 8, scratch_shapes=scratch,
        compiler_params=pltpu.CompilerParams(collective_id=0, has_side_effects=True, vmem_limit_bytes=60 * 2**20))(
            tok, seg, cot, wqkv, bqv, wout, wint, wffo, vec)


def local(tokens, cotangent, segment_ids, q_weight, key_weight, value_weight, q_bias, value_bias, out_weight, out_bias,
          norm1_gain, norm1_bias, inter_weight, inter_bias, ffo_weight, ffo_bias, norm2_gain, norm2_bias):
    n, nf = lax.axis_size("ctx"), lax.axis_size("fsdp")
    S = jax.ShapeDtypeStruct
    rows = MICRO * 128
    tok = tokens.reshape(MICRO, 128, D)
    gather = lambda a, ax: lax.all_gather(a, "fsdp", axis=ax, tiled=True)
    wqkv = gather(jnp.stack([q_weight, key_weight, value_weight]), 1)
    wout, wint, wffo = gather(out_weight, 0), gather(inter_weight, 0), gather(ffo_weight, 0)
    dl = q_bias.shape[0]
    pack = jnp.concatenate([jnp.stack([out_bias, norm1_gain, norm1_bias, ffo_bias, norm2_gain, norm2_bias, q_bias, value_bias]),
                            inter_bias.reshape(4, dl)], axis=0)
    allv = lax.all_gather(pack, "fsdp", axis=0)
    top = jnp.swapaxes(allv[:, 0:8], 0, 1).reshape(8, D)
    low = allv[:, 8:12].reshape(4, D)
    vec = jnp.concatenate([top, low, jnp.zeros((4, D), BF)], axis=0).astype(F32)
    bqv = jnp.concatenate([top[6:8], jnp.zeros((6, D), BF)], axis=0)
    out, grad, gw, gb, ga, gi, gf, gv = run_mega(n, tok.reshape(rows, D), segment_ids.reshape(MICRO, 128), cotangent.reshape(rows, D),
                                                 wqkv, bqv, wout, wint, wffo, vec)
    scatter = lambda a: lax.psum(lax.psum_scatter(a, "fsdp", scatter_dimension=0, tiled=True), "ctx").astype(F32)
    gvec = lax.psum(jnp.concatenate([gv, gb], axis=0), ("fsdp", "ctx"))
    me = lax.axis_index("fsdp")
    part = lambda i: lax.dynamic_slice(gvec[i], (me * dl,), (dl,))
    gib = lax.dynamic_slice(gvec[8:12].reshape(4 * D), (me * 4 * dl,), (4 * dl,))
    return (out.reshape(tokens.shape), grad.reshape(tokens.shape), scatter(gw[0]), scatter(gw[1]), scatter(gw[2]), part(16), part(17),
            scatter(ga), part(0), part(1), part(2), scatter(gi), gib, scatter(gf.T), part(3), part(4), part(5))


def solution(mesh):
    act, seg, mat, vec = P(None, "fsdp", "ctx", None), P(None, "fsdp", "ctx"), P("fsdp", None), P("fsdp")
    return jax.shard_map(
        local, mesh=mesh,
        in_specs=(act, act, seg, mat, mat, mat, vec, vec, mat, vec, vec, vec, mat, vec, mat, vec, vec, vec),
        out_specs=(act, act, mat, mat, mat, vec, vec, mat, vec, vec, vec, mat, vec, mat, vec, vec, vec),
        check_vma=False)
```

time: 521 us -> 559 us (1.073)
  waiting for transfers between devices: 301 us -> 395 us
  Pallas kernels: 161 us -> 101 us
    pallas_call x7 -> x1, Pallas kernels: 161 us -> 101 us  [run_mega(): pl.pallas_call(lambda *a: mega(n, *a), out_shape=outs, in_specs=[vm] * 9,...]
    all_gather x3, waiting for transfers between devices: 0.01 us -> 53.7 us  [local(): gather = lambda a, ax: lax.all_gather(a, 'fsdp', axis=ax, tiled=True)]
    psum x1, waiting for transfers between devices: 104 us -> 125 us  [local(): gvec = lax.psum(jnp.concatenate([gv, gb], axis=0), ('fsdp', 'ctx'))]
    unnamed x12, waiting for transfers between devices: 4.72 us -> 23.1 us
  transfers between devices with their start and end apart: 11 -> 11, of which waited for: 7 -> 11; matrix products, arithmetic and copies ran while one was open for 2% -> 2% of each run, Pallas kernels for 27% -> 0%
where the time goes in v2:
time: 559 us
  waiting for transfers between devices  395 us (71%)
  Pallas kernels  101 us (18%)
  blocking collectives  25.8 us (5%)
  local copies, waits for them, and re-layouts  15.8 us (3%)
  between operations  14.2 us (3%)
  other arithmetic  6.91 us (1%)
    psum x1, waiting for transfers between devices, local(): gvec = lax.psum(jnp.concatenate([gv, gb], axis=0), ('fsdp', 'ctx'))  125 us
    psum x1, waiting for transfers between devices, local(): lax.psum(lax.psum_scatter(a, 'fsdp', scatter_dimension=0, tiled=True), 'c...  102 us
    pallas_call x1, Pallas kernels, run_mega(): pl.pallas_call(lambda *a: mega(n, *a), out_shape=outs, in_specs=[vm] * 9,...  101 us
    reduce_scatter x5, waiting for transfers between devices, local(): lax.psum_scatter(a, 'fsdp', scatter_dimension=0, tiled=True)  90.7 us
    all_gather x3, waiting for transfers between devices, local(): gather = lambda a, ax: lax.all_gather(a, 'fsdp', axis=ax, tiled=True)  53.7 us
    unnamed x12, waiting for transfers between devices  23.1 us
    all_gather x1, blocking collectives, local(): gather = lambda a, ax: lax.all_gather(a, 'fsdp', axis=ax, tiled=True)  20.5 us
  transfers between devices with their start and end apart: 11, of which 11 were waited for; matrix products, arithmetic and copies ran while one was open for 2% of the time, Pallas kernels for 0%

profile of v2, /device:TPU:0, one launch (start us, length us, event | category | flops | bytes accessed | tf_op | source)
XLA Modules:
  0.0 558.8 jit_solution(18204719416260854084)
XLA Ops:
  7.3 0.0 all-gather.10.cloned.1.call-start
  7.4 0.7 all-gather.10.cloned.1.call-update
  8.1 0.0 all-gather.6.cloned.1.call-start
  8.1 0.7 all-gather.6.cloned.1.call-update
  8.8 0.0 all-gather.8.cloned.1.call-start
  8.9 0.7 all-gather.8.cloned.1.call-update
  9.5 0.0 reduce-scatter.19.cloned.1.call-start
  9.8 0.1 concatenate.12
  9.8 5.3 all-gather.1
  15.2 0.6 copy.45
  15.8 0.6 concatenate.13.a_4_
  16.4 0.1 pad.5.clone
  16.5 0.0 copy-done.5
  16.5 0.1 pad_maximum_fusion
  16.5 20.5 %all_gather.18.a_3_ = bf16[3,192,768]{2,1,0:T(8,128)(2,1)} all-gather(bf16[3,96,768]{2,1,0:T(8,128)(2,1)S(1)} %pad_maximum_fusion), channel_id=1, replica_groups=mesh['fsdp'=2,'ctx'=16] {'fsdp'}, dimensions={1}, use_global_device_ids=true | all-gather | bytes 1327104 | tf_op jit(solution)/shard_map/all_gather | solution.py:442
  37.0 0.7 maximum_convert_fusion.a_8_
  37.7 3.4 all-gather.10.cloned.1.call-done.a_7_
  41.1 25.9 %all-gather.6.cloned.1.call-done.a_5_ = bf16[768,768]{1,0:T(8,128)(2,1)} async-done(((bf16[384,768]{1,0:T(8,128)(2,1)}), bf16[768,768]{1,0:T(8,128)(2,1)}) %all-gather.6.cloned.1.call-update) | async-done | bytes 1179664 | tf_op jit(solution)/shard_map/all_gather | solution.py:442
  67.0 24.4 %all-gather.8.cloned.1.call-done.a_6_ = bf16[192,3072]{1,0:T(8,128)(2,1)} async-done(((bf16[96,3072]{1,0:T(8,128)(2,1)}), bf16[192,3072]{1,0:T(8,128)(2,1)}) %all-gather.8.cloned.1.call-update) | async-done | bytes 1179664 | tf_op jit(solution)/shard_map/all_gather | solution.py:442
  91.4 100.7 %shard_map.305 = (bf16[384,768]{1,0:T(8,128)(2,1)}, bf16[384,768]{1,0:T(8,128)(2,1)}, bf16[3,192,768]{2,1,0:T(8,128)(2,1)}, f32[8,768]{1,0:T(8,128)}, bf16[768,7...) custom-call(bf16[384,768]{1,0:T(8,128)(2,1)} %bitcast.29, ...), custom_call_target="tpu_custom_call" | custom-call | tf_op jit(solution)/shard_map/pallas_call | solution.py:430
  192.1 2.4 copy.41
  194.4 0.0 reduce-scatter.19.cloned.1.call-update
  194.5 0.0 reduce-scatter.11.cloned.1.call-start
  194.5 1.1 copy-done
  195.6 0.9 slice_bitcast_fusion
  196.5 0.0 reduce-scatter.11.cloned.1.call-update
  196.6 0.0 reduce-scatter.13.cloned.1.call-start
  196.6 0.5 reduce-scatter.13.cloned.1.call-update
  197.1 0.0 reduce-scatter.9.cloned.1.call-start
  197.2 0.7 reduce-scatter.9.cloned.1.call-update
  197.9 0.0 reduce-scatter.15.cloned.1.call-start
  197.9 0.7 reduce-scatter.15.cloned.1.call-update
  198.6 0.0 reduce-scatter.17.cloned.1.call-start
  198.7 0.7 reduce-scatter.17.cloned.1.call-update
  199.4 0.0 all-reduce.5.cloned.1.call-start
  199.4 0.6 pad_maximum_fusion.1
  200.1 0.0 all-reduce.5.cloned.1.call-update
  200.1 0.0 all-reduce.7.cloned.1.call-start
  200.1 18.4 %reduce-scatter.19.cloned.1.call-done = bf16[384,768]{1,0:T(8,128)(2,1)} async-done(((bf16[768,768]{1,0:T(8,128)(2,1)}), bf16[384,768]{1,0:T(8,128)(2,1)}) %reduce-scatter.19.cloned.1.call-update) | async-done | bytes 589840
  218.5 2.1 copy.42
  220.6 12.7 %reduce-scatter.11.cloned.1.call-done = bf16[96,768]{1,0:T(8,128)(2,1)} async-done(((bf16[192,768]{1,0:T(8,128)(2,1)}), bf16[96,768]{1,0:T(8,128)(2,1)}) %reduce-scatter.11.cloned.1.call-update) | async-done | bytes 147472 | tf_op jit(solution)/shard_map/reduce_scatter | solution.py:455
  233.3 14.8 %reduce-scatter.13.cloned.1.call-done = bf16[96,768]{1,0:T(8,128)(2,1)} async-done(((bf16[192,768]{1,0:T(8,128)(2,1)}), bf16[96,768]{1,0:T(8,128)(2,1)}) %reduce-scatter.13.cloned.1.call-update) | async-done | bytes 147472 | tf_op jit(solution)/shard_map/reduce_scatter | solution.py:455
  248.2 15.0 %reduce-scatter.9.cloned.1.call-done = bf16[96,768]{1,0:T(8,128)(2,1)} async-done(((bf16[192,768]{1,0:T(8,128)(2,1)}), bf16[96,768]{1,0:T(8,128)(2,1)}) %reduce-scatter.9.cloned.1.call-update) | async-done | bytes 147472 | tf_op jit(solution)/shard_map/reduce_scatter | solution.py:455
  263.1 24.1 %reduce-scatter.15.cloned.1.call-done = bf16[384,768]{1,0:T(8,128)(2,1)} async-done(((bf16[768,768]{1,0:T(8,128)(2,1)}), bf16[384,768]{1,0:T(8,128)(2,1)}) %reduce-scatter.15.cloned.1.call-update) | async-done | bytes 589840 | tf_op jit(solution)/shard_map/reduce_scatter | solution.py:455
  287.3 24.0 %reduce-scatter.17.cloned.1.call-done = bf16[96,3072]{1,0:T(8,128)(2,1)} async-done(((bf16[192,3072]{1,0:T(8,128)(2,1)}), bf16[96,3072]{1,0:T(8,128)(2,1)}) %reduce-scatter.17.cloned.1.call-update) | async-done | bytes 589840 | tf_op jit(solution)/shard_map/reduce_scatter | solution.py:455
  311.3 0.0 all-reduce.7.cloned.1.call-update
  311.3 125.2 %all-reduce.5.cloned.1.call-done = f32[24,768]{1,0:T(8,128)} async-done(((f32[24,768]{1,0:T(8,128)}), f32[24,768]{1,0:T(8,128)}) %all-reduce.5.cloned.1.call-update) | async-done | bytes 73744 | tf_op jit(solution)/shard_map/psum | solution.py:456
  436.6 0.7 slice.72
  437.3 0.7 dynamic_slice.53
  438.0 1.0 fusion.8
  439.0 0.6 fusion.6
  439.6 0.6 fusion.4
  440.2 0.6 fusion.2
  440.8 0.6 fusion
  441.4 102.3 %all-reduce.7.cloned.1.call-done = (bf16[384,768]{0,1:T(8,128)(2,1)}, bf16[96,768]{1,0:T(8,128)(2,1)}, bf16[96,768]{1,0:T(8,128)(2,1)}, bf16[96,768]{1,0:T(8,128...) async-done(((bf16[384,768]{0,1:T(8,128)(2,1)}, bf16[96,768]{1,0:T(8,128)(2,1)}, bf16[96,768]{1,0:T(8,128)(2,1)}, bf16[96,768]{1,0:T(8,128)(2,1)}, ...) | async-done | bytes 2211856 | tf_op jit(solution)/shard_map/psum | solution.py:455
  543.7 2.2 convert_element_type.25
  545.9 1.1 convert_element_type.26
  547.0 0.1 copy-done.1
  547.1 1.3 copy.40
  548.4 0.7 convert_element_type.22
  549.1 0.7 convert_element_type.23
  549.9 0.7 convert_element_type.24
  550.6 0.8 copy.55
  551.4 0.8 copy.56
  (58 shorter events, 0.2 us)
Async XLA Ops:
  7.2 2.4 copy-start.13
  7.2 2.4 copy-start.15
  7.2 2.4 copy-start.16
  7.2 2.4 copy-start.17
  7.2 2.4 copy-start.18
  7.2 2.5 copy-start.19
  7.3 2.5 copy-start.20
  7.3 2.5 copy-start.21
  7.3 2.5 copy-start.22
  7.3 7.9 %copy-start.14 = (s32[3,1,128]{2,1,0:T(1,128)S(1)}, s32[3,1,128]{2,1,0:T(1,128)}, u32[]{:S(2)}) copy-start(s32[3,1,128]{2,1,0:T(1,128)} %param.20) | copy-start | bytes 4612
  7.3 9.2 %copy-start.7 = (bf16[96,768]{1,0:T(8,128)(2,1)S(1)}, bf16[96,768]{1,0:T(8,128)(2,1)}, u32[]{:S(2)}) copy-start(bf16[96,768]{1,0:T(8,128)(2,1)} %param.21) | copy-start | bytes 442372
  7.3 9.2 %copy-start.6 = (bf16[96,768]{1,0:T(8,128)(2,1)S(1)}, bf16[96,768]{1,0:T(8,128)(2,1)}, u32[]{:S(2)}) copy-start(bf16[96,768]{1,0:T(8,128)(2,1)} %param.22) | copy-start | bytes 442372
  7.3 9.2 %copy-start.5 = (bf16[96,768]{1,0:T(8,128)(2,1)S(1)}, bf16[96,768]{1,0:T(8,128)(2,1)}, u32[]{:S(2)}) copy-start(bf16[96,768]{1,0:T(8,128)(2,1)} %param.23) | copy-start | bytes 442372
  7.3 33.8 %all-gather.10.cloned.1.call-start = ((), (), s32[]{:S(2)}) async-start(), calls=%async_computation.8 | async-start | bytes 1769472 | tf_op jit(solution)/shard_map/all_gather | solution.py:442
  8.1 58.9 %all-gather.6.cloned.1.call-start = ((), (), s32[]{:S(2)}) async-start(), calls=%async_computation.6 | async-start | bytes 1769472 | tf_op jit(solution)/shard_map/all_gather | solution.py:442
  8.8 82.6 %all-gather.8.cloned.1.call-start = ((), (), s32[]{:S(2)}) async-start(), calls=%async_computation.7 | async-start | bytes 1769472 | tf_op jit(solution)/shard_map/all_gather | solution.py:442
  9.5 209.0 %reduce-scatter.19.cloned.1.call-start = ((), (), s32[]{:S(2)}) async-start(), calls=%async_computation.15 | async-start | bytes 1769472
  194.4 1.2 copy-start
  194.5 38.9 %reduce-scatter.11.cloned.1.call-start = ((), (), s32[]{:S(2)}) async-start(), calls=%async_computation.10 | async-start | bytes 442368 | tf_op jit(solution)/shard_map/reduce_scatter | solution.py:455
  196.6 51.6 %reduce-scatter.13.cloned.1.call-start = ((), (), s32[]{:S(2)}) async-start(), calls=%async_computation.11 | async-start | bytes 442368 | tf_op jit(solution)/shard_map/reduce_scatter | solution.py:455
  197.1 66.0 %reduce-scatter.9.cloned.1.call-start = ((), (), s32[]{:S(2)}) async-start(), calls=%async_computation.9 | async-start | bytes 442368 | tf_op jit(solution)/shard_map/reduce_scatter | solution.py:455
  197.9 89.4 %reduce-scatter.15.cloned.1.call-start = ((), (), s32[]{:S(2)}) async-start(), calls=%async_computation.13 | async-start | bytes 1769472 | tf_op jit(solution)/shard_map/reduce_scatter | solution.py:455
  197.9 1.5 copy-start.11
  197.9 1.5 copy-start.12
  198.6 112.7 %reduce-scatter.17.cloned.1.call-start = ((), (), s32[]{:S(2)}) async-start(), calls=%async_computation.14 | async-start | bytes 1769472 | tf_op jit(solution)/shard_map/reduce_scatter | solution.py:455
  199.4 237.2 %all-reduce.5.cloned.1.call-start = ((), (), s32[]{:S(2)}) async-start(), calls=%async_computation.12 | async-start | bytes 147456 | tf_op jit(solution)/shard_map/psum | solution.py:456
  200.1 343.6 %all-reduce.7.cloned.1.call-start = ((), (), s32[]{:S(2)}) async-start(), calls=%async_computation.16 | async-start | bytes 4423680 | tf_op jit(solution)/shard_map/psum | solution.py:455
  543.7 2.2 copy-start.2
  545.9 1.2 copy-start.1
  547.0 1.4 copy-start.10
  547.0 2.1 copy-start.9
  547.1 2.8 copy-start.8
  547.1 3.5 copy-start.4
  548.4 3.0 copy-start.3
Sparse Core Ops, SparseCore 0:
  9.7 31.4 all-gather.9
  42.7 24.2 all-gather.5
  68.5 22.7 all-gather.7
  194.6 23.8 reduce-scatter.18
  221.3 12.0 reduce-scatter.10
  236.1 12.0 reduce-scatter.12
  251.1 12.0 reduce-scatter.8
  265.5 21.7 reduce-scatter.14
  289.5 21.7 reduce-scatter.16
  318.2 118.3 all-reduce.4
  442.1 101.5 all-reduce.6

commit v3 on v2

v3 whole, which is shorter than its diff:
```python
import math

import jax
import jax.numpy as jnp
from jax import lax
from jax.experimental import pallas as pl
from jax.experimental.pallas import tpu as pltpu
from jax.sharding import PartitionSpec as P

MESH = pl.DeviceIdType.MESH
MICRO = 3


def place(n, g, m):
    return g * (n // 4) + m + (g % 2)


def owners(n):
    return [place(n, g, m) for m in range(MICRO) for g in range(4)]


def unit_of(c, n):
    g = c // (n // 4)
    m = c - g * (n // 4) - lax.rem(g, 2)
    return g, m, (m >= 0) & (m < MICRO)


BF, F32 = jnp.bfloat16, jnp.float32
HEAD, GW = 64, 192
CH = 208
XA = 240
BIG = 1e9
NN = (((1,), (0,)), ((), ()))
NT = (((1,), (1,)), ((), ()))
TN = (((0,), (0,)), ((), ()))

def mm(a, b, dims=NN):
    return lax.dot_general(a, b, dims, preferred_element_type=F32)

def iota(shape, axis):
    return lax.broadcasted_iota(jnp.int32, shape, axis)

def build_weights(w_ref, b_ref, wa_ref, wat_ref):
    for s in range(3):
        for h in range(3):
            w = w_ref[s, :, h * 64:h * 64 + 64].astype(F32)
            top = jnp.concatenate([w * (0.125 if s == 0 else 1.0), jnp.zeros((GW, 64), F32)], axis=1)
            r, c = iota((48, 128), 0), iota((48, 128), 1)
            same = (c - 64 == r)
            lanes = (c >= 64) & (c < 96) & (r < 32)
            one = (r == 32)
            zero = jnp.zeros((48, 128), F32)
            if s == 0:
                bias = jnp.concatenate([b_ref[0:1, h * 64:h * 64 + 64].astype(F32) * 0.125, jnp.zeros((1, 64), F32)], axis=1)
                low = jnp.where(lanes & same, 1.0, zero) + jnp.where(one, bias, zero)
            elif s == 1:
                low = jnp.where(lanes & ~same, -BIG, zero) + jnp.where(one & (c == 96), 1.0, zero)
            else:
                bias = jnp.concatenate([b_ref[1:2, h * 64:h * 64 + 64].astype(F32), jnp.zeros((1, 64), F32)], axis=1)
                low = jnp.where(one, bias, zero) + jnp.where(one & (c == 64), 1.0, zero)
            full = jnp.concatenate([top, low], axis=0)
            wa_ref[s, :, h * 128:h * 128 + 128] = full.astype(BF)
            wat_ref[s, h * 128:h * 128 + 128, :] = jnp.transpose(full).astype(BF)

D, FF = 768, 3072
EPS = 1e-12
WIN = (0, 128, 384, 512)
OFF = (0, 64, 0, 64)
RS2 = math.sqrt(0.5)
IPI = 1.0 / math.sqrt(2.0 * math.pi)
CK = 32

def rowmean(x):
    return jnp.sum(x, axis=-1, keepdims=True) * (1.0 / D)

def tall(ref, m):
    return jnp.concatenate([ref[m * 4 + g] for g in range(4)], axis=0)


def pad_weights(wint, wffo, wip, wfp):
    for j in range(4):
        o = OFF[j]
        wip[j] = jnp.zeros((256, D), BF)
        wip[j, o:o + 192, :] = wint[:, j * D:(j + 1) * D]
        lane = iota((D, 256), 1)
        w = wffo[:, WIN[j]:WIN[j] + 256]
        wfp[j] = jnp.where((lane >= o) & (lane < o + 192), w.astype(F32), 0.0).astype(BF)


def dense_body(rows, x, send, chains):
    tok, cot, ctxt, wout, out, d1, dct, gv = x.tok, x.cot, x.crecv, x.wout, x.out, x.d1, x.dsend, x.gv
    ctx, attn, n1b, wip, wfp, dpre, hid, br, dn, db, st = x.ctx, x.xh, x.n1b, x.wip, x.wfp, x.dpre, x.hid, x.br, x.dn, x.db, x.st
    da = ctx
    nm = rows // 128
    v = lambda i: x.vec[i:i + 1, :]
    for m in range(nm):
        ctx[m * 128:(m + 1) * 128, :] = jnp.transpose(tall(ctxt, m))
    attn[...] = mm(ctx[...], wout[...])
    def ln1(t, c):
        s = pl.ds(pl.multiple_of(t * CK, CK), CK)
        r = attn[s, :] + v(0) + tok[s, :].astype(F32)
        cen = r - rowmean(r)
        rstd = lax.rsqrt(rowmean(cen * cen) + EPS)
        xh = cen * rstd
        attn[s, :] = xh
        st[s, :] = jnp.broadcast_to(rstd, (CK, 128))
        n = xh * v(1) + v(2)
        n1b[s, :] = n.astype(BF)
        br[s, :] = n + v(3)
        return c
    lax.fori_loop(0, rows // CK, ln1, 0)
    for j in range(4):
        for m in range(nm):
            s = slice(m * 128, (m + 1) * 128)
            u = mm(n1b[s, WIN[j]:WIN[j] + 256], wip[j]) + v(8 + j)
            half = 0.5 + 0.5 * lax.erf(u * RS2)
            hid[j, s, :] = (u * half).astype(BF)
            dpre[j, s, :] = (half + u * (jnp.exp(u * u * -0.5) * IPI)).astype(BF)
        br[:, WIN[j]:WIN[j] + 256] += mm(hid[j], wfp[j])
    gv[...] = jnp.zeros_like(gv)
    def ln2(t, c):
        s = pl.ds(pl.multiple_of(t * CK, CK), CK)
        r = br[s, :]
        cen = r - rowmean(r)
        rstd = lax.rsqrt(rowmean(cen * cen) + EPS)
        xh = cen * rstd
        out[s, :] = (xh * v(4) + v(5)).astype(BF)
        ct = cot[s, :].astype(F32)
        u = ct * v(4)
        dd = rstd * (u - rowmean(u) - xh * rowmean(u * xh))
        dn[s, :] = dd
        ddb = dd.astype(BF)
        db[s, :] = ddb
        gv[4:5, :] += jnp.sum(ct * xh, axis=0, keepdims=True)
        gv[5:6, :] += jnp.sum(ct, axis=0, keepdims=True)
        gv[3:4, :] += jnp.sum(ddb.astype(F32), axis=0, keepdims=True)
        return c
    lax.fori_loop(0, rows // CK, ln2, 0)
    for j in range(4):
        for m in range(nm):
            s = slice(m * 128, (m + 1) * 128)
            dh = mm(db[s, WIN[j]:WIN[j] + 256], wfp[j], NT)
            dp = (dh * dpre[j, s, :].astype(F32)).astype(BF)
            dpre[j, s, :] = dp
            gv[8 + j:9 + j, :] += jnp.sum(dp.astype(F32), axis=0, keepdims=True)
        dn[:, WIN[j]:WIN[j] + 256] += mm(dpre[j], wip[j], NT)
    def lnb(t, c):
        s = pl.ds(pl.multiple_of(t * CK, CK), CK)
        g = dn[s, :]
        xh = attn[s, :]
        u = g * v(1)
        dd = st[s, 0:1] * (u - rowmean(u) - xh * rowmean(u * xh))
        d1[s, :] = dd
        ddb = dd.astype(BF)
        da[s, :] = ddb
        gv[1:2, :] += jnp.sum(g * xh, axis=0, keepdims=True)
        gv[2:3, :] += jnp.sum(g, axis=0, keepdims=True)
        gv[0:1, :] += jnp.sum(ddb.astype(F32), axis=0, keepdims=True)
        return c
    lax.fori_loop(0, rows // CK, lnb, 0)
    dc = mm(wout[...], da[...], NT).astype(BF)
    for m in range(nm):
        for g in range(4):
            dct[m * 4 + g] = dc[g * GW:g * GW + GW, m * 128:(m + 1) * 128]
    send()
    ct = jnp.concatenate([tall(ctxt, m) for m in range(nm)], axis=1)
    nt = jnp.transpose(n1b[...])
    dbt = jnp.transpose(db[...])
    if chains is None:
        x.ga[...] = mm(ct, da[...]).astype(BF)
        for j in range(4):
            o = WIN[j] + OFF[j]
            x.gi[:, j * D:(j + 1) * D] = mm(nt[o:o + 192, :], dpre[j]).astype(BF)
            x.gf[j * 192:(j + 1) * 192, :] = mm(dbt[o:o + 192, :], hid[j]).astype(BF)
        return
    for s in range(3):
        val = mm(ct, da[:, s * 256:s * 256 + 256])
        for f in range(2):
            for k in range(2):
                put(x.Ab, f, (2 * s + k) * 384, val[f * 384:f * 384 + 384, k * 128:k * 128 + 128])
    low = iota((16, 128), 0)
    for f in range(2):
        for b in range(16):
            two = []
            for k in (2 * b, 2 * b + 1):
                if k < 18:
                    at = f * 384 + (k % 3) * 128
                    two.append(gv[k // 3:k // 3 + 1, at:at + 128])
                elif k < 30:
                    row, at = 8 + 2 * f + (k - 18) // 6, (k - 18) % 6 * 128
                    two.append(gv[row:row + 1, at:at + 128])
                else:
                    two.append(jnp.zeros((1, 128), F32))
            x.Ab[b // 8, f, (b // 4) % 2, b % 4, 144:160, :] = jnp.where(low == 0, two[0], jnp.where(low == 1, two[1], 0.0)).astype(BF)
    chains["A"].step(0)
    for j in range(4):
        o = WIN[j] + OFF[j]
        val = mm(nt[o:o + 192, :], dpre[j])
        for f in range(2):
            for s in range(6):
                put(x.Bb, f, (j * 6 + s) * 96, val[f * 96:f * 96 + 96, s * 128:s * 128 + 128])
    chains["B"].step(0)
    for j in range(4):
        o = WIN[j] + OFF[j]
        val = mm(dbt[o:o + 192, :], hid[j])
        for f in range(2):
            for s in range(3):
                at = f * 384 + s * 128
                put(x.Cb, f, s * 768 + j * 192, val[:, at:at + 128])
    chains["C"].step(0)


def remote_copy(src, dst, ssem, rsem, f, c):
    return pltpu.make_async_remote_copy(src_ref=src, dst_ref=dst, send_sem=ssem, recv_sem=rsem, device_id=(f, c), device_id_type=MESH)


VECTORS = ("out_bias", "norm1_gain", "norm1_bias", "ffo_bias", "norm2_gain", "norm2_bias", "q_bias", "value_bias")
LEN = {"A": 160, "B": 144, "C": 144}


def pieces(base, rows):
    out, at = [], 0
    while at < rows:
        b, w = divmod(base + at, 144)
        size = min(144 - w, rows - at)
        out.append((b, w, at, size))
        at += size
    return out


def put(ref, f, base, val):
    for b, w, at, size in pieces(base, val.shape[0]):
        ref[b // 8, f, (b // 4) % 2, b % 4, w:w + size, :] = val[at:at + size].astype(BF)


class Chain:
    def __init__(self, order, f, c, refs):
        self.order, self.f, self.c = order, f, c
        self.b, self.c1, self.c2, self.c3, self.c4, self.out, self.ss, self.rs = refs
        self.r, self.x, self.z = lax.rem(c, 2), lax.rem(lax.div(c, 2), 2), lax.div(c, 4)
        self.started = []

    def core(self):
        return self.f, self.c + 1 - 2 * self.r

    def along_x(self):
        return self.f, self.c + 2 - 4 * self.x

    def along_z(self, d):
        return self.f, lax.rem(self.c + 4 * d, 16)

    def copy(self, k, src, dst, to):
        return remote_copy(src, dst, self.ss.at[k], self.rs.at[k], *to)

    def moves(self, k):
        b, r, f, x, z, o = self.b, self.r, self.f, self.x, self.z, self.out
        zs = [(d, lax.rem(z + d, 4)) for d in (1, 2, 3)]
        y = (1 - f, self.c)
        if k == 0:
            return [(0, b.at[1 - r], self.c1, self.core())]
        if k == 6:
            return [(4, o.at[r], o.at[r], self.core())]
        if self.order == "yxz":
            return {1: [(1, b.at[r, 1 - f], self.c2, y)],
                    2: [(2, b.at[r, f, 1 - x], self.c3, self.along_x())],
                    3: [(4 + d, b.at[r, f, x, t], self.c4.at[z], self.along_z(d)) for d, t in zs],
                    4: [(7 + d, o.at[r, x, z], o.at[r, x, z], self.along_z(d)) for d, t in zs],
                    5: [(3, o.at[r, x], o.at[r, x], self.along_x())]}[k]
        return {1: [(4 + d, b.at[r, :, :, t], self.c4.at[z], self.along_z(d)) for d, t in zs],
                2: [(1, b.at[r, 1 - f, :, z], self.c2, y)],
                3: [(2, b.at[r, f, 1 - x, z], self.c3, self.along_x())],
                4: [(3, o.at[r, x, z], o.at[r, x, z], self.along_x())],
                5: [(7 + d, o.at[r, :, z], o.at[r, :, z], self.along_z(d)) for d, t in zs]}[k]

    def start(self, k):
        for mv in self.moves(k):
            self.copy(*mv).start()

    def received(self, k):
        for mv in self.moves(k):
            self.copy(*mv).wait_recv()

    def sent(self):
        for k in range(7):
            for mv in self.moves(k):
                self.copy(*mv).wait_send()

    def add(self, k):
        b, r, f, x, z, o = self.b, self.r, self.f, self.x, self.z, self.out
        up = lambda v: v.astype(F32)
        others = [lax.rem(z + 4 - d, 4) for d in (1, 2, 3)]
        if k == 0:
            def one(t, carry):
                i, j, l = t // 8, lax.rem(t // 4, 2), lax.rem(t, 4)
                b[r, i, j, l] = (up(b[r, i, j, l]) + up(self.c1[i, j, l])).astype(BF)
                return carry
            lax.fori_loop(0, 16, one, 0)
        elif self.order == "yxz" and k == 1:
            def one(t, carry):
                j, l = t // 4, lax.rem(t, 4)
                b[r, f, j, l] = (up(b[r, f, j, l]) + up(self.c2[j, l])).astype(BF)
                return carry
            lax.fori_loop(0, 8, one, 0)
        elif self.order == "yxz" and k == 2:
            for l in range(4):
                b[r, f, x, l] = (up(b[r, f, x, l]) + up(self.c3[l])).astype(BF)
        elif self.order == "yxz" and k == 3:
            o[r, x, z] = (up(b[r, f, x, z]) + sum(up(self.c4[t]) for t in others)).astype(BF)
        elif self.order == "zyx" and k == 1:
            for i in range(2):
                for j in range(2):
                    b[r, i, j, z] = (up(b[r, i, j, z]) + sum(up(self.c4[t, i, j]) for t in others)).astype(BF)
        elif self.order == "zyx" and k == 2:
            for j in range(2):
                b[r, f, j, z] = (up(b[r, f, j, z]) + up(self.c2[j])).astype(BF)
        elif self.order == "zyx" and k == 3:
            o[r, x, z] = (up(b[r, f, x, z]) + up(self.c3[...])).astype(BF)

    def step(self, k):
        if k > 0:
            self.received(k - 1)
            self.add(k - 1)
        if k < 7:
            self.start(k)


def tile_at(q, t, half):
    p, mir = lax.rem(q, half // 2), lax.div(q, half // 2)
    b = lax.div(t + half - 1 - p, 2 * half)
    i = p + b * (half - 1 - 2 * p)
    j = t - b * (half + 1 + p)
    last = 2 * half - 1
    return b, i + mir * (last - 2 * i), j + mir * (last - 2 * j)


def rows_at(q, half):
    p, mir = lax.rem(q, half // 2), lax.div(q, half // 2)
    last = 2 * half - 1
    return [i + mir * (last - 2 * i) for i in (p, half - 1 - p)]


def in_parts(half, part):
    count = 3 * half + 1
    if count <= 13:
        part(0, count)
    else:
        size = max(d for d in range(1, 9) if count % d == 0)
        lax.fori_loop(0, count // size, lambda t, carry: (part(t * size, size), carry)[1], 0)


def forward_tiles(q, half, qt, ka, vt, acc):
    acc[...] = jnp.zeros_like(acc)
    def part(first, count):
        items = [(h,) + tile_at(q, first + t, half) for t in range(count) for h in range(3)]
        def front(it):
            h, _, i, j = it
            return mm(ka[h, j], qt[h, i])
        ready = [front(it) for it in items[:3]]
        for t, (h, b, i, j) in enumerate(items):
            if t + 3 < len(items):
                ready.append(front(items[t + 3]))
            e = jnp.exp(ready[t]).astype(BF)
            ready[t] = None
            acc[h, b] += mm(vt[h, j], e)
    in_parts(half, part)


def backward_tiles(q, half, qt, ka, kt, va, dnt, dq, dk, dv):
    dq[...] = jnp.zeros_like(dq)
    def part(first, count):
        items = [(h,) + tile_at(q, first + t, half) for t in range(count) for h in range(3)]
        def front(it):
            h, _, i, j = it
            return mm(ka[h, j], qt[h, i]), mm(va[h, j, :, 0:80], dnt[h, i])
        ready = [front(it) for it in items[:2]]
        for t, (h, b, i, j) in enumerate(items):
            if t + 2 < len(items):
                ready.append(front(items[t + 2]))
            s, dp = ready[t]
            ready[t] = None
            e = jnp.exp(s)
            eb = e.astype(BF)
            ds = (e * dp).astype(BF)
            dq[h, b] += mm(kt[h, j], ds)
            dk[h, j] += mm(qt[h, i, 0:64], ds, NT)
            dv[h, j] += mm(dnt[h, i, 0:64], eb, NT)
    in_parts(half, part)


def prep_block(i, xt, wa, wat, qt, ka, vt, kt, va):
    x = jnp.concatenate([xt[2 * i], xt[2 * i + 1]], axis=1)
    seg = x[GW:GW + 16].astype(F32)[0:1].astype(jnp.int32)
    r = iota((48, 256), 0)
    aug = jnp.where((r == seg) & (r < 32) | (r == 32), 1.0, 0.0).astype(BF)
    xa = jnp.concatenate([x[0:GW], aug], axis=0)
    xn = jnp.transpose(xa)
    q = mm(wat[0], xa).astype(BF)
    k = mm(wat[1], xa).astype(BF)
    v = mm(wat[2], xa).astype(BF)
    kn = mm(xn, wa[1]).astype(BF)
    vn = mm(xn, wa[2]).astype(BF)
    for h in range(3):
        o = h * 128
        qt[h, i] = q[o:o + 128]
        anchor = jnp.sum(q[o:o + 64].astype(F32) * k[o:o + 64].astype(F32), axis=0, keepdims=True)
        qt[h, i, 96:112] = jnp.where(iota((16, 256), 0) == 0, -anchor, 0.0).astype(BF)
        ka[h, i] = kn[:, o:o + 128]
        vt[h, i] = v[o:o + 80]
        kt[h, i] = k[o:o + 64]
        va[h, i] = vn[:, o:o + 128]


def mega(n, fast, x):
    f, c = lax.axis_index("fsdp"), lax.axis_index("ctx")
    g, m, mine = unit_of(c, n)
    u = m * 4 + g
    own = owners(n)
    sb, half = n // 2, n // 4
    r = lax.rem(c, 2)
    tok, dnt = x.tok, x.vt
    bar = pltpu.get_barrier_semaphore()
    for d in range(1, n):
        pl.semaphore_signal(bar, inc=1, device_id=(f, lax.rem(c + d, n)), device_id_type=MESH)
    greeted = n - 1
    if fast:
        for p in range(4):
            pl.semaphore_signal(bar, inc=1, device_id=(1 - f, g * 4 + p), device_id_type=MESH)
        greeted += 4
        fetch = [pltpu.make_async_copy(x.wo, x.wout.at[pl.ds(f * 384, 384)], x.lsem.at[0]),
                 pltpu.make_async_copy(x.wi, x.wint.at[pl.ds(f * 96, 96)], x.lsem.at[1]),
                 pltpu.make_async_copy(x.wf, x.wffo.at[pl.ds(f * 384, 384)], x.lsem.at[2]),
                 pltpu.make_async_copy(x.cot_in, x.cot, x.lsem.at[3])]
        for cp in fetch:
            cp.start()
    for k in range(MICRO):
        t = jnp.transpose(tok[k * 128:k * 128 + 128, :])
        sg = jnp.broadcast_to(x.seg[k:k + 1, :].astype(F32), (16, 128)).astype(BF)
        for j in range(4):
            x.tsend[k * 4 + j, 0:GW, :] = t[j * GW:j * GW + GW]
            x.tsend[k * 4 + j, GW:CH, :] = sg
    if fast:
        own_rows = [getattr(x, k)[...].astype(F32).reshape(1, 384) for k in VECTORS]
        inter = x.inter_bias[...].astype(F32).reshape(1, 1536)
        own_rows += [inter[:, k * 384:k * 384 + 384] for k in range(4)]
        x.vbuf[f] = jnp.concatenate(own_rows + [jnp.zeros((4, 384), F32)], axis=0).astype(BF)
    pl.semaphore_wait(bar, greeted)

    def spread(src, dst, ss, rs, start):
        for k in range(12):
            @pl.when(c != own[k])
            def _():
                cp = remote_copy(src.at[k], dst.at[c], ss.at[k], rs.at[c], f, own[k])
                cp.start() if start else cp.wait_send()
            if start:
                @pl.when(c == own[k])
                def _():
                    pltpu.make_async_copy(src.at[k], dst.at[c], rs.at[c]).start()
    def arrived(src, dst, rs, s):
        @pl.when(c != s)
        def _():
            remote_copy(src.at[0], dst.at[s], x.ls, rs.at[s], f, s).wait_recv()
        @pl.when(c == s)
        def _():
            pltpu.make_async_copy(src.at[0], dst.at[s], rs.at[s]).wait()
    def give(src, dst, ss, rs, t, start):
        @pl.when(c != t)
        def _():
            cp = remote_copy(src.at[t], dst.at[u], ss.at[t], rs.at[u], f, t)
            cp.start() if start else cp.wait_send()
        if start:
            @pl.when(c == t)
            def _():
                pltpu.make_async_copy(src.at[t], dst.at[u], rs.at[u]).start()
    def taken(src, dst, rs):
        for k in range(12):
            @pl.when(c != own[k])
            def _():
                remote_copy(src.at[0], dst.at[k], x.ls, rs.at[k], f, own[k]).wait_recv()
            @pl.when(c == own[k])
            def _():
                pltpu.make_async_copy(src.at[0], dst.at[k], rs.at[k]).wait()

    if fast:
        sib = c + 1 - 2 * r
        parts = ((x.wo, x.wout, 384), (x.wi, x.wint, 96), (x.wf, x.wffo, 384))
        def window(j, k):
            return remote_copy((x.wq, x.wk, x.wv)[j].at[:, WIN[k]:WIN[k] + 256], x.qrem.at[j], x.wss.at[6 + j], x.wrs.at[6 + j], 1 - f, c)
        def vectors():
            return remote_copy(x.vbuf.at[f], x.vbuf.at[f], x.wss.at[9], x.wrs.at[9], 1 - f, c)
        def half_over(j):
            src, dst, rows = parts[j]
            h = rows // 2
            return remote_copy(src.at[pl.ds(r * h, h)], dst.at[pl.ds(f * rows + r * h, h)], x.wss.at[j], x.wrs.at[j], 1 - f, c)
        def relay(j, back=False):
            _, dst, rows = parts[j]
            h = rows // 2
            at = pl.ds((1 - f) * rows + r * h, h)
            return remote_copy(dst.at[at], dst.at[at], x.wss.at[3 + j], x.wrs.at[3 + j], f, sib)
        @pl.when(mine)
        def _():
            for k in range(4):
                @pl.when(g == k)
                def _():
                    for j in range(3):
                        window(j, k).start()
        vectors().start()
    spread(x.tsend, x.xt, x.tss, x.trs, True)
    if fast:
        for j in range(3):
            half_over(j).start()
        def pass_on(j):
            half_over(j).wait_recv()
            relay(j).start()

    if fast:
        vectors().wait_recv()
        for k in range(2):
            for j in range(8):
                x.vec[j:j + 1, k * 384:k * 384 + 384] = x.vbuf[k, 0:16, :].astype(F32)[j:j + 1, :]
            for j in range(4):
                row, at = 8 + 2 * k + j // 2, (j % 2) * 384
                x.vec[row:row + 1, at:at + 384] = x.vbuf[k, 0:16, :].astype(F32)[8 + j:9 + j, :]

    @pl.when(mine)
    def _():
        for k in range(4):
            @pl.when(g == k)
            def _():
                lanes = slice(k * GW, k * GW + GW)
                if not fast:
                    x.w[...] = x.wqkv[:, :, lanes]
                else:
                    for j in range(3):
                        window(j, k).wait_recv()
                        for h in range(2):
                            @pl.when(f == h)
                            def _():
                                x.w[j, h * 96:h * 96 + 96, :] = (x.wq, x.wk, x.wv)[j][:, lanes]
                                x.w[j, 96 - h * 96:192 - h * 96, :] = x.qrem[j, :, OFF[k]:OFF[k] + GW]
                x.bias[0:2, :] = x.vec[6:8, lanes]
        build_weights(x.w, x.bias, x.wa, x.wat)
        def first(i, carry):
            arrived(x.tsend, x.xt, x.trs, 2 * i)
            arrived(x.tsend, x.xt, x.trs, 2 * i + 1)
            prep_block(i, x.xt, x.wa, x.wat, x.qt, x.ka, x.vt, x.kt, x.va)
            return carry
        lax.fori_loop(0, sb, first, 0)

    def forward_step(q, carry):
        @pl.when(mine)
        def _():
            forward_tiles(q, half, x.qt, x.ka, x.vt, x.acc)
            for b, i in enumerate(rows_at(q, half)):
                for h in range(3):
                    a = x.acc[h, b]
                    v = a[0:64] / a[64:65]
                    x.cf[i, h * 64:h * 64 + 64, :] = v
                    x.lsum[i, h:h + 1, :] = a[64:65]
                    vb = v.astype(BF)
                    x.csend[2 * i, h * 64:h * 64 + 64, :] = vb[:, 0:128]
                    x.csend[2 * i + 1, h * 64:h * 64 + 64, :] = vb[:, 128:256]
                give(x.csend, x.crecv, x.css, x.crs, 2 * i, True)
                give(x.csend, x.crecv, x.css, x.crs, 2 * i + 1, True)
        if fast:
            for j in range(3):
                @pl.when(q == j)
                def _():
                    pass_on(j)
        return carry
    lax.fori_loop(0, half, forward_step, 0)
    @pl.when(mine)
    def _():
        x.dk[...] = jnp.zeros_like(x.dk)
        x.dv[...] = jnp.zeros_like(x.dv)

    if fast:
        for cp in fetch:
            cp.wait()
        for j in range(3):
            relay(j).wait_recv()
        chains = {k: Chain(o, f, c, [getattr(x, k + s) for s in ("b", "1", "2", "3", "4", "o", "ss", "rs")])
                  for k, o in (("A", "yxz"), ("B", "zyx"), ("C", "yxz"))}
    pad_weights(x.wint, x.wffo, x.wip, x.wfp)
    taken(x.csend, x.crecv, x.crs)
    def send_dct():
        spread(x.dsend, x.dc, x.dss, x.drs, True)
    dense_body(MICRO * 128, x, send_dct, chains if fast else None)

    if fast:
        chains["A"].step(1)
        chains["B"].step(1)
    else:
        x.gw[...] = jnp.zeros_like(x.gw)
        x.gb[...] = jnp.zeros_like(x.gb)

    def backward_step(q, carry):
        @pl.when(mine)
        def _():
            for b, i in enumerate(rows_at(q, half)):
                arrived(x.dsend, x.dc, x.drs, 2 * i)
                arrived(x.dsend, x.dc, x.drs, 2 * i + 1)
                d = jnp.concatenate([x.dc[2 * i], x.dc[2 * i + 1]], axis=1).astype(F32)
                for h in range(3):
                    dh = d[h * 64:h * 64 + 64]
                    inv = 1.0 / x.lsum[i, h:h + 1, :]
                    delta = jnp.sum(dh * x.cf[i, h * 64:h * 64 + 64, :], axis=0, keepdims=True) * inv
                    dnt[h, i] = jnp.concatenate([dh * inv, jnp.where(iota((16, 256), 0) == 0, -delta, 0.0)], axis=0).astype(BF)
            backward_tiles(q, half, x.qt, x.ka, x.kt, x.va, dnt, x.dq, x.dk, x.dv)
            for b, i in enumerate(rows_at(q, half)):
                for h in range(3):
                    x.dqt[i, h * 64:h * 64 + 64, :] = (x.dq[h, b] * 0.125).astype(BF)
        if fast:
            for k in range(4):
                @pl.when(q == k)
                def _():
                    chains["A"].step(k + 2)
                    chains["B"].step(k + 2)
                    chains["C"].step(k + 1)
        return carry
    lax.fori_loop(0, half, backward_step, 0)

    xsend = x.csend
    @pl.when(mine)
    def _():
        for t in range(n):
            give(x.csend, x.crecv, x.css, x.crs, t, False)
        x.gacc[...] = jnp.zeros_like(x.gacc)
        x.gbacc[...] = jnp.zeros_like(x.gbacc)
        ones = jnp.ones((8, 256), BF)
        def post(i, carry):
            xb = jnp.concatenate([x.xt[2 * i, 0:GW, :], x.xt[2 * i + 1, 0:GW, :]], axis=1)
            q = x.dqt[i]
            k = jnp.concatenate([x.dk[h, i] for h in range(3)], axis=0).astype(BF)
            v = jnp.concatenate([x.dv[h, i] for h in range(3)], axis=0).astype(BF)
            x2 = (mm(x.w[0], q) + mm(x.w[1], k) + mm(x.w[2], v)).astype(BF)
            xsend[2 * i] = x2[:, 0:128]
            xsend[2 * i + 1] = x2[:, 128:256]
            give(xsend, x.xrecv, x.xss, x.xrs, 2 * i, True)
            give(xsend, x.xrecv, x.xss, x.xrs, 2 * i + 1, True)
            x.gacc[0] += mm(xb, q, NT)
            x.gacc[1] += mm(xb, k, NT)
            x.gacc[2] += mm(xb, v, NT)
            x.gbacc[0] += mm(ones, q, NT)
            x.gbacc[1] += mm(ones, v, NT)
            return carry
        lax.fori_loop(0, sb, post, 0)
        if fast:
            low = iota((96, 64), 0)
            bb = jnp.zeros((96, 64), F32)
            for k in range(2):
                for i in range(3):
                    bb = jnp.where(low == 3 * k + i, x.gbacc[k, 0:1, i * 64:i * 64 + 64], bb)
            for h in range(2):
                cat = jnp.concatenate([x.gacc[k, h * 96:h * 96 + 96, :] for k in range(3)] + [bb], axis=1).astype(BF)
                for s in range(5):
                    x.qs[h, s * 96:s * 96 + 96, :] = cat[:, s * 128:s * 128 + 128]
        else:
            for k in range(4):
                @pl.when(g == k)
                def _():
                    x.gw[:, :, k * GW:k * GW + GW] = x.gacc[...].astype(BF)
                    x.gb[0:1, k * GW:k * GW + GW] = x.gbacc[0, 0:1]
                    x.gb[1:2, k * GW:k * GW + GW] = x.gbacc[1, 0:1]

    if fast:
        def to_sum(h, t):
            return remote_copy(x.qs.at[h, pl.ds(t * 160, 160)], x.qr.at[f * 3 + m], x.qss.at[h * 3 + t], x.qrs.at[f * 3 + m], h, place_at(g, t))
        def stay():
            return pltpu.make_async_copy(x.qs.at[f, pl.ds(m * 160, 160)], x.qr.at[f * 3 + m], x.qrs.at[f * 3 + m])
        def place_at(g, t):
            return g * 4 + t + lax.rem(g, 2)
        def to_all(d):
            return remote_copy(x.qb.at[u], x.qb.at[u], x.qbs.at[d], x.qbr.at[u], f, lax.rem(c + d, n))
        def elsewhere(h, t):
            return (f != h) | (m != t)
        @pl.when(mine)
        def _():
            for h in range(2):
                for t in range(3):
                    @pl.when(elsewhere(h, t))
                    def _():
                        to_sum(h, t).start()
            stay().start()
        chains["A"].step(6)
        chains["B"].step(6)
        chains["C"].step(5)
        @pl.when(mine)
        def _():
            for h in range(2):
                for t in range(3):
                    @pl.when(elsewhere(h, t))
                    def _():
                        remote_copy(x.qs.at[0, pl.ds(0, 160)], x.qr.at[h * 3 + t], x.ls, x.qrs.at[h * 3 + t], h, place_at(g, t)).wait_recv()
            stay().wait()
            x.qb[u] = sum(x.qr[k].astype(F32) for k in range(6)).astype(BF)
            for d in range(1, n):
                to_all(d).start()
        chains["C"].step(6)
        for k in range(12):
            @pl.when(c != own[k])
            def _():
                remote_copy(x.qb.at[k], x.qb.at[k], x.ls, x.qbr.at[k], f, own[k]).wait_recv()

    taken(xsend, x.xrecv, x.xrs)
    if fast:
        for k in "ABC":
            chains[k].step(7)
            chains[k].sent()
        vectors().wait_send()
        for j in range(3):
            half_over(j).wait_send()
            relay(j).wait_send()
        @pl.when(mine)
        def _():
            for j in range(3):
                window(j, 0).wait_send()
            for h in range(2):
                for t in range(3):
                    @pl.when(elsewhere(h, t))
                    def _():
                        to_sum(h, t).wait_send()
            for d in range(1, n):
                to_all(d).wait_send()
    else:
        for k in range(MICRO):
            t = jnp.concatenate([x.xrecv[k * 4 + j] for j in range(4)], axis=0).astype(F32)
            s = slice(k * 128, k * 128 + 128)
            x.grad[s, :] = (jnp.transpose(t) + x.d1[s, :]).astype(BF)
    spread(x.tsend, x.xt, x.tss, x.trs, False)
    spread(x.dsend, x.dc, x.dss, x.drs, False)
    @pl.when(mine)
    def _():
        for t in range(n):
            give(xsend, x.xrecv, x.xss, x.xrs, t, False)


DMA = pltpu.SemaphoreType.DMA
S, V = jax.ShapeDtypeStruct, pltpu.VMEM


def common_scratch(n):
    rows, sb = MICRO * 128, n // 2
    return dict(
        tsend=V((12, CH, 128), BF), xt=V((n, CH, 128), BF), csend=V((n, GW, 128), BF), crecv=V((12, GW, 128), BF),
        dsend=V((12, GW, 128), BF), dc=V((n, GW, 128), BF),
        w=V((3, GW, GW), BF), bias=V((8, GW), F32), wa=V((3, XA, 384), BF), wat=V((3, 384, XA), BF),
        qt=V((3, sb, 128, 256), BF), ka=V((3, sb, 256, 128), BF), vt=V((3, sb, 80, 256), BF), kt=V((3, sb, 64, 256), BF), va=V((3, sb, 256, 128), BF),
        cf=V((sb, GW, 256), F32), lsum=V((sb, 8, 256), F32), acc=V((3, 2, 80, 256), F32), dq=V((3, 2, 64, 256), F32),
        dk=V((3, sb, 64, 256), F32), dv=V((3, sb, 64, 256), F32), dqt=V((sb, GW, 256), BF), gacc=V((3, GW, GW), F32), gbacc=V((2, 8, GW), F32),
        ctx=V((rows, D), BF), xh=V((rows, D), F32), n1b=V((rows, D), BF), wip=V((4, 256, D), BF), wfp=V((4, D, 256), BF), dpre=V((4, rows, D), BF),
        hid=V((4, rows, D), BF), br=V((rows, D), F32), dn=V((rows, D), F32), db=V((rows, D), BF), st=V((rows, 128), F32),
        tss=DMA((12,)), trs=DMA((n,)), css=DMA((n,)), crs=DMA((12,)), dss=DMA((12,)), drs=DMA((n,)), xss=DMA((n,)), xrs=DMA((12,)), ls=DMA)


class Refs:
    def __init__(self, **k):
        self.__dict__.update(k)


def call(n, fast, ins, outs, scratch, far):
    names, onames = list(ins), list(outs)
    def kernel(*a):
        refs = dict(zip(names, a[:len(names)]))
        refs.update(zip(onames, a[len(names):len(names) + len(onames)]))
        refs.update(a[-1])
        mega(n, fast, Refs(**refs))
    vm = pl.BlockSpec(memory_space=pltpu.VMEM)
    got = pl.pallas_call(
        kernel, out_shape=tuple(outs.values()),
        in_specs=[pl.BlockSpec(memory_space=pl.ANY) if k in far else vm for k in names], out_specs=(vm,) * len(onames),
        scratch_shapes=[scratch],
        compiler_params=pltpu.CompilerParams(collective_id=0, has_side_effects=True, vmem_limit_bytes=60 * 2**20))(*ins.values())
    return dict(zip(onames, got))


def run_whole(n, ins):
    rows = MICRO * 128
    outs = dict(out=S((rows, D), BF), grad=S((rows, D), BF), gw=S((3, GW, D), BF), gb=S((8, D), F32), ga=S((D, D), BF), gi=S((192, FF), BF),
                gf=S((D, D), BF), gv=S((16, D), F32))
    scratch = common_scratch(n)
    scratch.update(xrecv=V((12, GW, 128), BF), d1=V((rows, D), F32))
    return call(n, False, ins, outs, scratch, ())


def run_fast(n, ins):
    rows = MICRO * 128
    outs = dict(out=S((rows, D), BF), xrecv=S((12, GW, 128), BF), d1=S((rows, D), F32), qb=S((12, 160, 128), BF))
    for k in "ABC":
        outs[k + "o"] = S((2, 2, 4, LEN[k], 128), BF)
    scratch = common_scratch(n)
    scratch.update(cot=V((rows, D), BF), wout=V((D, D), BF), wint=V((192, FF), BF), wffo=V((D, D), BF), vec=V((16, D), F32), vbuf=V((2, 16, 384), BF),
                   qrem=V((3, 96, 256), BF), gv=V((16, D), F32), qs=V((2, 480, 128), BF), qr=V((6, 160, 128), BF),
                   lsem=DMA((4,)), wss=DMA((10,)), wrs=DMA((10,)), qss=DMA((6,)), qrs=DMA((6,)), qbs=DMA((n,)), qbr=DMA((12,)))
    for k in "ABC":
        l = LEN[k]
        scratch[k + "b"] = V((2, 2, 2, 4, l, 128), BF)
        scratch[k + "1"] = V((2, 2, 4, l, 128), BF)
        scratch[k + "2"] = V((2, l, 128) if k == "B" else (2, 4, l, 128), BF)
        scratch[k + "3"] = V((l, 128) if k == "B" else (4, l, 128), BF)
        scratch[k + "4"] = V((4, 2, 2, l, 128) if k == "B" else (4, l, 128), BF)
        scratch[k + "ss"] = DMA((11,))
        scratch[k + "rs"] = DMA((11,))
    return call(n, True, ins, outs, scratch, ("wo", "wi", "wf", "cot_in"))


def finish(out, xrecv, d1, qb, a, b, c, o_out, o_grad, o_q, o_k, o_v, o_qb, o_vb, o_w, o_b, o_g1, o_s1, o_i, o_ib, o_f, o_fb, o_g2, o_s2):
    f = lax.axis_index("fsdp")
    o_out[...] = out[...]
    for k in range(MICRO):
        t = jnp.concatenate([xrecv[k * 4 + j] for j in range(4)], axis=0).astype(F32)
        s = slice(k * 128, k * 128 + 128)
        o_grad[s, :] = (jnp.transpose(t) + d1[s, :]).astype(BF)
    def slab(ref, base, rows):
        got = [ref[b // 8, (b // 4) % 2, b % 4, w:w + size, :] for b, w, _, size in pieces(base, rows)]
        return jnp.concatenate(got, axis=0).astype(F32) if len(got) > 1 else got[0].astype(F32)
    for s in range(6):
        o_w[:, s * 128:s * 128 + 128] = slab(a, s * 384, 384)
    for s in range(24):
        o_i[:, s * 128:s * 128 + 128] = slab(b, s * 96, 96)
    for s in range(3):
        o_f[s * 128:s * 128 + 128, :] = jnp.transpose(slab(c, s * 768, 768))
    cats, qbs, vbs = [], [], []
    for g in range(4):
        rows = jnp.concatenate([qb[t * 4 + g] for t in range(3)], axis=0).astype(F32)
        cat = jnp.concatenate([rows[s * 96:s * 96 + 96] for s in range(5)], axis=1)
        cats.append(cat)
        qbs.append(jnp.concatenate([cat[i:i + 1, 576:640] for i in range(3)], axis=1))
        vbs.append(jnp.concatenate([cat[3 + i:4 + i, 576:640] for i in range(3)], axis=1))
    for k, o in enumerate((o_q, o_k, o_v)):
        o[...] = jnp.concatenate([cat[:, k * GW:k * GW + GW] for cat in cats], axis=1)
    pick = lambda v: jnp.where(f == 0, jnp.concatenate(v[0:2], axis=1), jnp.concatenate(v[2:4], axis=1))
    o_qb[...] = pick(qbs).reshape(384)
    o_vb[...] = pick(vbs).reshape(384)
    rows = []
    for k in range(30):
        b = k // 2
        rows.append(a[b // 8, (b // 4) % 2, b % 4, 144:160, :].astype(F32)[k % 2:k % 2 + 1, :])
    for i, o in enumerate((o_b, o_g1, o_s1, o_fb, o_g2, o_s2)):
        o[...] = jnp.concatenate(rows[3 * i:3 * i + 3], axis=1).reshape(384)
    o_ib[...] = jnp.concatenate(rows[18:30], axis=1).reshape(1536)


def local(tokens, cotangent, segment_ids, q_weight, key_weight, value_weight, q_bias, value_bias, out_weight, out_bias,
          norm1_gain, norm1_bias, inter_weight, inter_bias, ffo_weight, ffo_bias, norm2_gain, norm2_bias):
    n, nf = lax.axis_size("ctx"), lax.axis_size("fsdp")
    rows = MICRO * 128
    tok, cot, seg = tokens.reshape(rows, D), cotangent.reshape(rows, D), segment_ids.reshape(MICRO, 128)
    dl = q_bias.shape[0]
    if n == 16 and nf == 2:
        x = run_fast(n, dict(tok=tok, seg=seg, cot_in=cot, wq=q_weight, wk=key_weight, wv=value_weight, wo=out_weight, wi=inter_weight, wf=ffo_weight,
                             out_bias=out_bias, norm1_gain=norm1_gain, norm1_bias=norm1_bias, ffo_bias=ffo_bias, norm2_gain=norm2_gain,
                             norm2_bias=norm2_bias, q_bias=q_bias, value_bias=value_bias, inter_bias=inter_bias))
        vm = pl.BlockSpec(memory_space=pltpu.VMEM)
        row = S((dl,), F32)
        outs = (S((rows, D), BF), S((rows, D), BF)) + (S((96, D), F32),) * 3 + (row, row, S((384, D), F32), row, row, row, S((96, FF), F32), S((4 * dl,), F32),
                S((384, D), F32), row, row, row)
        got = pl.pallas_call(
            finish, out_shape=outs, in_specs=[vm] * 7, out_specs=(vm,) * 17,
            compiler_params=pltpu.CompilerParams(vmem_limit_bytes=60 * 2**20))(x["out"], x["xrecv"], x["d1"], x["qb"], x["Ao"], x["Bo"], x["Co"])
        return (got[0].reshape(tokens.shape), got[1].reshape(tokens.shape)) + tuple(got[2:])
    gather = lambda a, ax: lax.all_gather(a, "fsdp", axis=ax, tiled=True)
    pack = jnp.concatenate([out_bias, norm1_gain, norm1_bias, ffo_bias, norm2_gain, norm2_bias, q_bias, value_bias, inter_bias]).reshape(12, dl)
    wqkv = gather(jnp.stack([q_weight, key_weight, value_weight]), 1)
    allv = lax.all_gather(pack, "fsdp", axis=0)
    vec = jnp.concatenate([jnp.swapaxes(allv[:, 0:8], 0, 1).reshape(8, D), allv[:, 8:12].reshape(4, D), jnp.zeros((4, D), BF)], axis=0).astype(F32)
    x = run_whole(n, dict(tok=tok, seg=seg, cot=cot, wqkv=wqkv, wout=gather(out_weight, 0), wint=gather(inter_weight, 0), wffo=gather(ffo_weight, 0), vec=vec))
    gw, gv = x["gw"], x["gv"]
    scatter = lambda a: lax.psum(lax.psum_scatter(a, "fsdp", scatter_dimension=0, tiled=True), "ctx").astype(F32)
    gvec = lax.psum(jnp.concatenate([gv, x["gb"]], axis=0), ("fsdp", "ctx"))
    me = lax.axis_index("fsdp")
    part = lambda i: lax.dynamic_slice(gvec[i], (me * dl,), (dl,))
    gib = lax.dynamic_slice(gvec[8:12].reshape(4 * D), (me * 4 * dl,), (4 * dl,))
    return (x["out"].reshape(tokens.shape), x["grad"].reshape(tokens.shape), scatter(gw[0]), scatter(gw[1]), scatter(gw[2]), part(16), part(17),
            scatter(x["ga"]), part(0), part(1), part(2), scatter(x["gi"]), gib, scatter(x["gf"].T), part(3), part(4), part(5))


def solution(mesh):
    act, seg, mat, vec = P(None, "fsdp", "ctx", None), P(None, "fsdp", "ctx"), P("fsdp", None), P("fsdp")
    return jax.shard_map(
        local, mesh=mesh,
        in_specs=(act, act, seg, mat, mat, mat, vec, vec, mat, vec, vec, vec, mat, vec, mat, vec, vec, vec),
        out_specs=(act, act, mat, mat, mat, vec, vec, mat, vec, vec, vec, mat, vec, mat, vec, vec, vec),
        check_vma=False)
```

time: 559 us -> 147 us (0.26)
  waiting for transfers between devices: 395 us -> 0 us
  Pallas kernels: 101 us -> 143 us
  blocking collectives: 25.8 us -> 0 us
  local copies, waits for them, and re-layouts: 15.8 us -> 1.26 us
  between operations: 14.2 us -> 0.82 us
  other arithmetic: 6.91 us -> 0 us
    psum x2 -> x0, waiting for transfers between devices: 228 us -> none  [the longest x1 125 us: local(): gvec = lax.psum(jnp.concatenate([gv, gb], axis=0), ('fsdp', 'ctx'))]
    reduce_scatter x5 -> x0, waiting for transfers between devices: 90.7 us -> none  [local(): lax.psum_scatter(a, 'fsdp', scatter_dimension=0, tiled=True)]
    all_gather x3 -> x0, waiting for transfers between devices: 53.7 us -> none  [local(): gather = lambda a, ax: lax.all_gather(a, 'fsdp', axis=ax, tiled=True)]
    pallas_call x1 -> x2, Pallas kernels: 101 us -> 143 us  [the longest x1 138 us: call(): pl.pallas_call(kernel, out_shape=tuple(outs.values()), in_specs=[pl.Block...]
    all_gather x2 -> x0, blocking collectives: 25.8 us -> none  [the longest x1 20.5 us: local(): gather = lambda a, ax: lax.all_gather(a, 'fsdp', axis=ax, tiled=True)]
    unnamed x12 -> x0, waiting for transfers between devices: 23.1 us -> none
    unnamed x52 -> x1, local copies, waits for them, and re-layouts: 9.24 us -> 1.26 us
    convert_element_type x6 -> x0, other arithmetic: 6.22 us -> none  [the longest x5 5.53 us: local(): lax.psum(lax.psum_scatter(a, 'fsdp', scatter_dimension=0, tiled=True), 'c...]
  transfers between devices with their start and end apart: 11 -> 0, of which waited for: 11 -> 0; matrix products, arithmetic and copies ran while one was open for 2% -> 0% of each run, Pallas kernels for 0% -> 0%
where the time goes in v3:
time: 147 us; the launch traced here: 145 us
  Pallas kernels  143 us (97%)
    pallas_call x1, Pallas kernels, call(): pl.pallas_call(kernel, out_shape=tuple(outs.values()), in_specs=[pl.Block...  138 us
    pallas_call x1, Pallas kernels, local(): pl.pallas_call(finish, out_shape=outs, in_specs=[vm] * 7, out_specs=(vm,)...  5.21 us

profile of v3, /device:TPU:0, one launch (start us, length us, event | category | flops | bytes accessed | tf_op | source)
XLA Modules:
  0.0 145.4 jit_solution(3796311878735424770)
XLA Ops:
  0.7 1.3 copy.39
  1.9 138.1 %shard_map.305 = (bf16[384,768]{1,0:T(8,128)(2,1)}, bf16[12,192,128]{2,1,0:T(8,128)(2,1)}, f32[384,768]{1,0:T(8,128)}, bf16[12,160,128]{2,1,0:T(8,128)(2,1)}, bf...) custom-call(bf16[384,768]{1,0:T(8,128)(2,1)} %bitcast.11, ...), custom_call_target="tpu_custom_call" | custom-call | tf_op jit(solution)/shard_map/pallas_call | solution.py:768
  140.0 5.2 %shard_map.306 = (bf16[384,768]{1,0:T(8,128)(2,1)}, bf16[384,768]{1,0:T(8,128)(2,1)}, f32[96,768]{1,0:T(8,128)}, f32[96,768]{1,0:T(8,128)}, f32[96,768]{1,0:T(8,...) custom-call(bf16[384,768]{1,0:T(8,128)(2,1)} %get-tuple-element.41.o, ...), custom_call_target="tpu_custom_call" | custom-call | tf_op jit(solution)/shard_map/pallas_call | solution.py:857

commit v4 on v3

--- a/solution.py
+++ b/solution.py
@@ -87,7 +87,7 @@
         wfp[j] = jnp.where((lane >= o) & (lane < o + 192), w.astype(F32), 0.0).astype(BF)
 
 
-def dense_body(rows, x, send, chains):
+def dense_body(rows, x, send, chains, slot):
     tok, cot, ctxt, wout, out, d1, dct, gv = x.tok, x.cot, x.crecv, x.wout, x.out, x.d1, x.dsend, x.gv
     ctx, attn, n1b, wip, wfp, dpre, hid, br, dn, db, st = x.ctx, x.xh, x.n1b, x.wip, x.wfp, x.dpre, x.hid, x.br, x.dn, x.db, x.st
     da = ctx
@@ -136,6 +136,19 @@
         gv[3:4, :] += jnp.sum(ddb.astype(F32), axis=0, keepdims=True)
         return c
     lax.fori_loop(0, rows // CK, ln2, 0)
+    dbt = jnp.transpose(db[...])
+    for j in range(4):
+        o = WIN[j] + OFF[j]
+        val = mm(dbt[o:o + 192, :], hid[j])
+        if chains is None:
+            x.gf[j * 192:(j + 1) * 192, :] = val.astype(BF)
+            continue
+        for f in range(2):
+            for s in range(3):
+                at = f * 384 + s * 128
+                put(x.Cb, f, s * 768 + j * 192, val[:, at:at + 128])
+    if chains is not None:
+        chains["C"].step(0)
     for j in range(4):
         for m in range(nm):
             s = slice(m * 128, (m + 1) * 128)
@@ -144,6 +157,19 @@
             dpre[j, s, :] = dp
             gv[8 + j:9 + j, :] += jnp.sum(dp.astype(F32), axis=0, keepdims=True)
         dn[:, WIN[j]:WIN[j] + 256] += mm(dpre[j], wip[j], NT)
+    nt = jnp.transpose(n1b[...])
+    for j in range(4):
+        o = WIN[j] + OFF[j]
+        val = mm(nt[o:o + 192, :], dpre[j])
+        if chains is None:
+            x.gi[:, j * D:(j + 1) * D] = val.astype(BF)
+            continue
+        for f in range(2):
+            for s in range(6):
+                put(x.Bb, f, (j * 6 + s) * 96, val[f * 96:f * 96 + 96, s * 128:s * 128 + 128])
+    if chains is not None:
+        chains["B"].step(0)
+    slot(0)
     def lnb(t, c):
         s = pl.ds(pl.multiple_of(t * CK, CK), CK)
         g = dn[s, :]
@@ -164,14 +190,8 @@
             dct[m * 4 + g] = dc[g * GW:g * GW + GW, m * 128:(m + 1) * 128]
     send()
     ct = jnp.concatenate([tall(ctxt, m) for m in range(nm)], axis=1)
-    nt = jnp.transpose(n1b[...])
-    dbt = jnp.transpose(db[...])
     if chains is None:
         x.ga[...] = mm(ct, da[...]).astype(BF)
-        for j in range(4):
-            o = WIN[j] + OFF[j]
-            x.gi[:, j * D:(j + 1) * D] = mm(nt[o:o + 192, :], dpre[j]).astype(BF)
-            x.gf[j * 192:(j + 1) * 192, :] = mm(dbt[o:o + 192, :], hid[j]).astype(BF)
         return
     for s in range(3):
         val = mm(ct, da[:, s * 256:s * 256 + 256])
@@ -193,21 +213,6 @@
                     two.append(jnp.zeros((1, 128), F32))
             x.Ab[b // 8, f, (b // 4) % 2, b % 4, 144:160, :] = jnp.where(low == 0, two[0], jnp.where(low == 1, two[1], 0.0)).astype(BF)
     chains["A"].step(0)
-    for j in range(4):
-        o = WIN[j] + OFF[j]
-        val = mm(nt[o:o + 192, :], dpre[j])
-        for f in range(2):
-            for s in range(6):
-                put(x.Bb, f, (j * 6 + s) * 96, val[f * 96:f * 96 + 96, s * 128:s * 128 + 128])
-    chains["B"].step(0)
-    for j in range(4):
-        o = WIN[j] + OFF[j]
-        val = mm(dbt[o:o + 192, :], hid[j])
-        for f in range(2):
-            for s in range(3):
-                at = f * 384 + s * 128
-                put(x.Cb, f, s * 768 + j * 192, val[:, at:at + 128])
-    chains["C"].step(0)
 
 
 def remote_copy(src, dst, ssem, rsem, f, c):
@@ -215,6 +220,8 @@
 
 
 VECTORS = ("out_bias", "norm1_gain", "norm1_bias", "ffo_bias", "norm2_gain", "norm2_bias", "q_bias", "value_bias")
+ORDER = {"A": "yxz", "B": "yxz", "C": "yxz"}
+SCHEDULE = {"C": (0, 1, 3, 5, 7, 9, 10), "B": (1, 3, 5, 7, 9, 10, 11), "A": (1, 5, 7, 9, 10, 11, 12)}
 LEN = {"A": 160, "B": 144, "C": 144}
 
 
@@ -434,7 +441,7 @@
             cp.start()
     for k in range(MICRO):
         t = jnp.transpose(tok[k * 128:k * 128 + 128, :])
-        sg = jnp.broadcast_to(x.seg[k:k + 1, :].astype(F32), (16, 128)).astype(BF)
+        sg = jnp.broadcast_to(x.seg[k].astype(F32), (16, 128)).astype(BF)
         for j in range(4):
             x.tsend[k * 4 + j, 0:GW, :] = t[j * GW:j * GW + GW]
             x.tsend[k * 4 + j, GW:CH, :] = sg
@@ -578,17 +585,20 @@
             cp.wait()
         for j in range(3):
             relay(j).wait_recv()
-        chains = {k: Chain(o, f, c, [getattr(x, k + s) for s in ("b", "1", "2", "3", "4", "o", "ss", "rs")])
-                  for k, o in (("A", "yxz"), ("B", "zyx"), ("C", "yxz"))}
+        chains = {k: Chain(o, f, c, [getattr(x, k + s) for s in ("b", "1", "2", "3", "4", "o", "ss", "rs")]) for k, o in ORDER.items()}
+    def slot(s):
+        for k, at in SCHEDULE.items():
+            for i in range(7):
+                if fast and at[i] == s:
+                    chains[k].step(i + 1)
     pad_weights(x.wint, x.wffo, x.wip, x.wfp)
     taken(x.csend, x.crecv, x.crs)
     def send_dct():
         spread(x.dsend, x.dc, x.dss, x.drs, True)
-    dense_body(MICRO * 128, x, send_dct, chains if fast else None)
+    dense_body(MICRO * 128, x, send_dct, chains if fast else None, slot)
 
     if fast:
-        chains["A"].step(1)
-        chains["B"].step(1)
+        slot(1)
     else:
         x.gw[...] = jnp.zeros_like(x.gw)
         x.gb[...] = jnp.zeros_like(x.gb)
@@ -613,13 +623,15 @@
             for k in range(4):
                 @pl.when(q == k)
                 def _():
-                    chains["A"].step(k + 2)
-                    chains["B"].step(k + 2)
-                    chains["C"].step(k + 1)
+                    slot(2 * k + 3)
         return carry
     lax.fori_loop(0, half, backward_step, 0)
 
     xsend = x.csend
+    def grads_at(i):
+        k = jnp.concatenate([x.dk[h, i] for h in range(3)], axis=0).astype(BF)
+        v = jnp.concatenate([x.dv[h, i] for h in range(3)], axis=0).astype(BF)
+        return x.dqt[i], k, v
     @pl.when(mine)
     def _():
         for t in range(n):
@@ -627,23 +639,16 @@
         x.gacc[...] = jnp.zeros_like(x.gacc)
         x.gbacc[...] = jnp.zeros_like(x.gbacc)
         ones = jnp.ones((8, 256), BF)
-        def post(i, carry):
+        def weigh(i, carry):
             xb = jnp.concatenate([x.xt[2 * i, 0:GW, :], x.xt[2 * i + 1, 0:GW, :]], axis=1)
-            q = x.dqt[i]
-            k = jnp.concatenate([x.dk[h, i] for h in range(3)], axis=0).astype(BF)
-            v = jnp.concatenate([x.dv[h, i] for h in range(3)], axis=0).astype(BF)
-            x2 = (mm(x.w[0], q) + mm(x.w[1], k) + mm(x.w[2], v)).astype(BF)
-            xsend[2 * i] = x2[:, 0:128]
-            xsend[2 * i + 1] = x2[:, 128:256]
-            give(xsend, x.xrecv, x.xss, x.xrs, 2 * i, True)
-            give(xsend, x.xrecv, x.xss, x.xrs, 2 * i + 1, True)
+            q, k, v = grads_at(i)
             x.gacc[0] += mm(xb, q, NT)
             x.gacc[1] += mm(xb, k, NT)
             x.gacc[2] += mm(xb, v, NT)
             x.gbacc[0] += mm(ones, q, NT)
             x.gbacc[1] += mm(ones, v, NT)
             return carry
-        lax.fori_loop(0, sb, post, 0)
+        lax.fori_loop(0, sb, weigh, 0)
         if fast:
             low = iota((96, 64), 0)
             bb = jnp.zeros((96, 64), F32)
@@ -670,7 +675,9 @@
         def place_at(g, t):
             return g * 4 + t + lax.rem(g, 2)
         def to_all(d):
-            return remote_copy(x.qb.at[u], x.qb.at[u], x.qbs.at[d], x.qbr.at[u], f, lax.rem(c + d, n))
+            return remote_copy(x.qb.at[u], x.qb.at[u], x.qbs.at[d], x.qbr.at[u], f, lax.rem(c + 2 * d, n))
+        def hand_over(k):
+            return remote_copy(x.qb.at[k], x.qb.at[k], x.qbx.at[k], x.qbr.at[k], f, sib)
         def elsewhere(h, t):
             return (f != h) | (m != t)
         @pl.when(mine)
@@ -681,9 +688,19 @@
                     def _():
                         to_sum(h, t).start()
             stay().start()
-        chains["A"].step(6)
-        chains["B"].step(6)
-        chains["C"].step(5)
+    @pl.when(mine)
+    def _():
+        def post(i, carry):
+            q, k, v = grads_at(i)
+            x2 = (mm(x.w[0], q) + mm(x.w[1], k) + mm(x.w[2], v)).astype(BF)
+            xsend[2 * i] = x2[:, 0:128]
+            xsend[2 * i + 1] = x2[:, 128:256]
+            give(xsend, x.xrecv, x.xss, x.xrs, 2 * i, True)
+            give(xsend, x.xrecv, x.xss, x.xrs, 2 * i + 1, True)
+            return carry
+        lax.fori_loop(0, sb, post, 0)
+    if fast:
+        slot(10)
         @pl.when(mine)
         def _():
             for h in range(2):
@@ -693,18 +710,26 @@
                         remote_copy(x.qs.at[0, pl.ds(0, 160)], x.qr.at[h * 3 + t], x.ls, x.qrs.at[h * 3 + t], h, place_at(g, t)).wait_recv()
             stay().wait()
             x.qb[u] = sum(x.qr[k].astype(F32) for k in range(6)).astype(BF)
-            for d in range(1, n):
+            for d in range(1, n // 2):
                 to_all(d).start()
-        chains["C"].step(6)
+        slot(11)
         for k in range(12):
-            @pl.when(c != own[k])
+            @pl.when((r == own[k] % 2) & (c != own[k]))
             def _():
                 remote_copy(x.qb.at[k], x.qb.at[k], x.ls, x.qbr.at[k], f, own[k]).wait_recv()
+            @pl.when(r == own[k] % 2)
+            def _():
+                hand_over(k).start()
 
     taken(xsend, x.xrecv, x.xrs)
     if fast:
+        for k in range(12):
+            @pl.when(r != own[k] % 2)
+            def _():
+                hand_over(k).wait_recv()
+        for s in range(12, 16):
+            slot(s)
         for k in "ABC":
-            chains[k].step(7)
             chains[k].sent()
         vectors().wait_send()
         for j in range(3):
@@ -719,8 +744,12 @@
                     @pl.when(elsewhere(h, t))
                     def _():
                         to_sum(h, t).wait_send()
-            for d in range(1, n):
+            for d in range(1, n // 2):
                 to_all(d).wait_send()
+        for k in range(12):
+            @pl.when(r == own[k] % 2)
+            def _():
+                hand_over(k).wait_send()
     else:
         for k in range(MICRO):
             t = jnp.concatenate([x.xrecv[k * 4 + j] for j in range(4)], axis=0).astype(F32)
@@ -790,14 +819,14 @@
     scratch = common_scratch(n)
     scratch.update(cot=V((rows, D), BF), wout=V((D, D), BF), wint=V((192, FF), BF), wffo=V((D, D), BF), vec=V((16, D), F32), vbuf=V((2, 16, 384), BF),
                    qrem=V((3, 96, 256), BF), gv=V((16, D), F32), qs=V((2, 480, 128), BF), qr=V((6, 160, 128), BF),
-                   lsem=DMA((4,)), wss=DMA((10,)), wrs=DMA((10,)), qss=DMA((6,)), qrs=DMA((6,)), qbs=DMA((n,)), qbr=DMA((12,)))
+                   lsem=DMA((4,)), wss=DMA((10,)), wrs=DMA((10,)), qss=DMA((6,)), qrs=DMA((6,)), qbs=DMA((n,)), qbr=DMA((12,)), qbx=DMA((12,)))
     for k in "ABC":
         l = LEN[k]
         scratch[k + "b"] = V((2, 2, 2, 4, l, 128), BF)
         scratch[k + "1"] = V((2, 2, 4, l, 128), BF)
-        scratch[k + "2"] = V((2, l, 128) if k == "B" else (2, 4, l, 128), BF)
-        scratch[k + "3"] = V((l, 128) if k == "B" else (4, l, 128), BF)
-        scratch[k + "4"] = V((4, 2, 2, l, 128) if k == "B" else (4, l, 128), BF)
+        scratch[k + "2"] = V((2, l, 128) if ORDER[k] == "zyx" else (2, 4, l, 128), BF)
+        scratch[k + "3"] = V((l, 128) if ORDER[k] == "zyx" else (4, l, 128), BF)
+        scratch[k + "4"] = V((4, 2, 2, l, 128) if ORDER[k] == "zyx" else (4, l, 128), BF)
         scratch[k + "ss"] = DMA((11,))
         scratch[k + "rs"] = DMA((11,))
     return call(n, True, ins, outs, scratch, ("wo", "wi", "wf", "cot_in"))
@@ -844,7 +873,7 @@
           norm1_gain, norm1_bias, inter_weight, inter_bias, ffo_weight, ffo_bias, norm2_gain, norm2_bias):
     n, nf = lax.axis_size("ctx"), lax.axis_size("fsdp")
     rows = MICRO * 128
-    tok, cot, seg = tokens.reshape(rows, D), cotangent.reshape(rows, D), segment_ids.reshape(MICRO, 128)
+    tok, cot, seg = tokens.reshape(rows, D), cotangent.reshape(rows, D), segment_ids
     dl = q_bias.shape[0]
     if n == 16 and nf == 2:
         x = run_fast(n, dict(tok=tok, seg=seg, cot_in=cot, wq=q_weight, wk=key_weight, wv=value_weight, wo=out_weight, wi=inter_weight, wf=ffo_weight,

time: 147 us -> 130 us (0.88)
  Pallas kernels: 143 us -> 128 us
    pallas_call x1, Pallas kernels: 138 us -> 123 us  [call(): pl.pallas_call(kernel, out_shape=tuple(outs.values()), in_specs=[pl.Block...]
where the time goes in v4:
time: 130 us; the launch traced here: 129 us
  Pallas kernels  128 us (98%)
    pallas_call x1, Pallas kernels, call(): pl.pallas_call(kernel, out_shape=tuple(outs.values()), in_specs=[pl.Block...  123 us
    pallas_call x1, Pallas kernels, local(): pl.pallas_call(finish, out_shape=outs, in_specs=[vm] * 7, out_specs=(vm,)...  5.21 us

profile of v4, /device:TPU:0, one launch (start us, length us, event | category | flops | bytes accessed | tf_op | source)
XLA Modules:
  0.0 128.7 jit_solution(4069805898683438096)
XLA Ops:
  0.7 122.7 %shard_map.305 = (bf16[384,768]{1,0:T(8,128)(2,1)}, bf16[12,192,128]{2,1,0:T(8,128)(2,1)}, f32[384,768]{1,0:T(8,128)}, bf16[12,160,128]{2,1,0:T(8,128)(2,1)}, bf...) custom-call(bf16[384,768]{1,0:T(8,128)(2,1)} %bitcast.8, ...), custom_call_target="tpu_custom_call" | custom-call | tf_op jit(solution)/shard_map/pallas_call | solution.py:797
  123.3 5.2 %shard_map.306 = (bf16[384,768]{1,0:T(8,128)(2,1)}, bf16[384,768]{1,0:T(8,128)(2,1)}, f32[96,768]{1,0:T(8,128)}, f32[96,768]{1,0:T(8,128)}, f32[96,768]{1,0:T(8,...) custom-call(bf16[384,768]{1,0:T(8,128)(2,1)} %get-tuple-element.41.o, ...), custom_call_target="tpu_custom_call" | custom-call | tf_op jit(solution)/shard_map/pallas_call | solution.py:886

commit v5 on v4

--- a/solution.py
+++ b/solution.py
@@ -68,7 +68,7 @@
 OFF = (0, 64, 0, 64)
 RS2 = math.sqrt(0.5)
 IPI = 1.0 / math.sqrt(2.0 * math.pi)
-CK = 32
+CK = 128
 
 def rowmean(x):
     return jnp.sum(x, axis=-1, keepdims=True) * (1.0 / D)
@@ -636,6 +636,17 @@
     def _():
         for t in range(n):
             give(x.csend, x.crecv, x.css, x.crs, t, False)
+        def post(i, carry):
+            q, k, v = grads_at(i)
+            x2 = (mm(x.w[0], q) + mm(x.w[1], k) + mm(x.w[2], v)).astype(BF)
+            xsend[2 * i] = x2[:, 0:128]
+            xsend[2 * i + 1] = x2[:, 128:256]
+            give(xsend, x.xrecv, x.xss, x.xrs, 2 * i, True)
+            give(xsend, x.xrecv, x.xss, x.xrs, 2 * i + 1, True)
+            return carry
+        lax.fori_loop(0, sb, post, 0)
+    @pl.when(mine)
+    def _():
         x.gacc[...] = jnp.zeros_like(x.gacc)
         x.gbacc[...] = jnp.zeros_like(x.gbacc)
         ones = jnp.ones((8, 256), BF)
@@ -688,17 +699,6 @@
                     def _():
                         to_sum(h, t).start()
             stay().start()
-    @pl.when(mine)
-    def _():
-        def post(i, carry):
-            q, k, v = grads_at(i)
-            x2 = (mm(x.w[0], q) + mm(x.w[1], k) + mm(x.w[2], v)).astype(BF)
-            xsend[2 * i] = x2[:, 0:128]
-            xsend[2 * i + 1] = x2[:, 128:256]
-            give(xsend, x.xrecv, x.xss, x.xrs, 2 * i, True)
-            give(xsend, x.xrecv, x.xss, x.xrs, 2 * i + 1, True)
-            return carry
-        lax.fori_loop(0, sb, post, 0)
     if fast:
         slot(10)
         @pl.when(mine)

time: 130 us -> 124 us (0.954); the launches traced: 129 us -> 124 us
  Pallas kernels: 128 us -> 123 us
    pallas_call x1, Pallas kernels: 123 us -> 118 us  [call(): pl.pallas_call(kernel, out_shape=tuple(outs.values()), in_specs=[pl.Block...]
where the time goes in v5:
time: 124 us
  Pallas kernels  123 us (99%)
    pallas_call x1, Pallas kernels, call(): pl.pallas_call(kernel, out_shape=tuple(outs.values()), in_specs=[pl.Block...  118 us
    pallas_call x1, Pallas kernels, local(): pl.pallas_call(finish, out_shape=outs, in_specs=[vm] * 7, out_specs=(vm,)...  5.21 us

profile of v5, /device:TPU:0, one launch (start us, length us, event | category | flops | bytes accessed | tf_op | source)
XLA Modules:
  0.0 124.1 jit_solution(6541726749702355560)
XLA Ops:
  0.7 118.0 %shard_map.305 = (bf16[384,768]{1,0:T(8,128)(2,1)}, bf16[12,192,128]{2,1,0:T(8,128)(2,1)}, f32[384,768]{1,0:T(8,128)}, bf16[12,160,128]{2,1,0:T(8,128)(2,1)}, bf...) custom-call(bf16[384,768]{1,0:T(8,128)(2,1)} %bitcast.8, ...), custom_call_target="tpu_custom_call" | custom-call | tf_op jit(solution)/shard_map/pallas_call | solution.py:797
  118.7 5.2 %shard_map.306 = (bf16[384,768]{1,0:T(8,128)(2,1)}, bf16[384,768]{1,0:T(8,128)(2,1)}, f32[96,768]{1,0:T(8,128)}, f32[96,768]{1,0:T(8,128)}, f32[96,768]{1,0:T(8,...) custom-call(bf16[384,768]{1,0:T(8,128)(2,1)} %get-tuple-element.41.o, ...), custom_call_target="tpu_custom_call" | custom-call | tf_op jit(solution)/shard_map/pallas_call | solution.py:886

commit v6 on v5

--- a/solution.py
+++ b/solution.py
@@ -110,8 +110,7 @@
         return c
     lax.fori_loop(0, rows // CK, ln1, 0)
     for j in range(4):
-        for m in range(nm):
-            s = slice(m * 128, (m + 1) * 128)
+        for s in (slice(0, rows),):
             u = mm(n1b[s, WIN[j]:WIN[j] + 256], wip[j]) + v(8 + j)
             half = 0.5 + 0.5 * lax.erf(u * RS2)
             hid[j, s, :] = (u * half).astype(BF)
@@ -150,8 +149,7 @@
     if chains is not None:
         chains["C"].step(0)
     for j in range(4):
-        for m in range(nm):
-            s = slice(m * 128, (m + 1) * 128)
+        for s in (slice(0, rows),):
             dh = mm(db[s, WIN[j]:WIN[j] + 256], wfp[j], NT)
             dp = (dh * dpre[j, s, :].astype(F32)).astype(BF)
             dpre[j, s, :] = dp

time: 124 us -> 123 us (level)
  no operation moved by 1% of the time
where the time goes in v6:
time: 123 us
  Pallas kernels  122 us (99%)
    pallas_call x1, Pallas kernels, call(): pl.pallas_call(kernel, out_shape=tuple(outs.values()), in_specs=[pl.Block...  117 us
    pallas_call x1, Pallas kernels, local(): pl.pallas_call(finish, out_shape=outs, in_specs=[vm] * 7, out_specs=(vm,)...  5.21 us

profile of v6, /device:TPU:0, one launch (start us, length us, event | category | flops | bytes accessed | tf_op | source)
XLA Modules:
  0.0 122.9 jit_solution(2826792596391327518)
XLA Ops:
  0.7 116.9 %shard_map.305 = (bf16[384,768]{1,0:T(8,128)(2,1)}, bf16[12,192,128]{2,1,0:T(8,128)(2,1)}, f32[384,768]{1,0:T(8,128)}, bf16[12,160,128]{2,1,0:T(8,128)(2,1)}, bf...) custom-call(bf16[384,768]{1,0:T(8,128)(2,1)} %bitcast.8, ...), custom_call_target="tpu_custom_call" | custom-call | tf_op jit(solution)/shard_map/pallas_call | solution.py:795
  117.5 5.2 %shard_map.306 = (bf16[384,768]{1,0:T(8,128)(2,1)}, bf16[384,768]{1,0:T(8,128)(2,1)}, f32[96,768]{1,0:T(8,128)}, f32[96,768]{1,0:T(8,128)}, f32[96,768]{1,0:T(8,...) custom-call(bf16[384,768]{1,0:T(8,128)(2,1)} %get-tuple-element.41.o, ...), custom_call_target="tpu_custom_call" | custom-call | tf_op jit(solution)/shard_map/pallas_call | solution.py:884
